TPU v7x, 32 devices: a whole 2x2x4 slice. The times are simulated.
32 devices in a mesh: dp: 8 (over z, core), seq: 4 (over y, x).
Axes of the slice: x: 2, y: 2, z: 4, core: 2. Of those that a mesh axis runs over, the one named last changes fastest.
Arguments:
- tokens: bfloat16 [8, 2048, 1024], P('dp', 'seq'), may hold values from -6 to 6
- cotangent: bfloat16 [8, 2048, 1024], P('dp', 'seq'), may hold values from -6 to 6
- gain_mixer: bfloat16 [1024], P(('dp', 'seq')), may hold values from 0.25 to 1.75
- proj_input: bfloat16 [1024, 4096], P(('dp', 'seq')), may hold values from -0.1875 to 0.1875
- conv_filter: bfloat16 [4096, 4], P(('dp', 'seq')), may hold values from -3 to 3
- proj_gates: bfloat16 [1024, 16], P(('dp', 'seq')), may hold values from -0.1875 to 0.1875
- proj_outgate: bfloat16 [1024, 2048], P(('dp', 'seq')), may hold values from -0.1875 to 0.1875
- gain_heads: bfloat16 [256], P(('dp', 'seq')), may hold values from 0.25 to 1.75
- proj_output: bfloat16 [2048, 1024], P(('dp', 'seq')), may hold values from -0.1875 to 0.1875
- gain_feed: bfloat16 [1024], P(('dp', 'seq')), may hold values from 0.25 to 1.75
- feed_gate: bfloat16 [1024, 2816], P(('dp', 'seq')), may hold values from -0.1875 to 0.1875
- feed_up: bfloat16 [1024, 2816], P(('dp', 'seq')), may hold values from -0.1875 to 0.1875
- feed_down: bfloat16 [2816, 1024], P(('dp', 'seq')), may hold values from -0.109375 to 0.109375
- decay_log: float32 [8], replicated, may hold values from -7.8 to -3.2
- decay_bias: float32 [8], replicated, may hold values from -1 to 1
Outputs:
- layer_out: bfloat16 [8, 2048, 1024], P('dp', 'seq')
- tokens_grad: float32 [8, 2048, 1024], P('dp', 'seq')
- grad_gain_mixer: float32 [1024], P(('dp', 'seq'))
- grad_proj_input: float32 [1024, 4096], P(('dp', 'seq'))
- grad_conv_filter: float32 [4096, 4], P(('dp', 'seq'))
- grad_proj_gates: float32 [1024, 16], P(('dp', 'seq'))
- grad_proj_outgate: float32 [1024, 2048], P(('dp', 'seq'))
- grad_gain_heads: float32 [256], P(('dp', 'seq'))
- grad_proj_output: float32 [2048, 1024], P(('dp', 'seq'))
- grad_gain_feed: float32 [1024], P(('dp', 'seq'))
- grad_feed_gate: float32 [1024, 2816], P(('dp', 'seq'))
- grad_feed_up: float32 [1024, 2816], P(('dp', 'seq'))
- grad_feed_down: float32 [2816, 1024], P(('dp', 'seq'))
- grad_decay_log: float32 [8], replicated
- grad_decay_bias: float32 [8], replicated
All inputs are finite; a program needn't handle non-finite values.
Results may differ from a plain program's by a relative error of at most 0.017.
Values may be sent and summed in bfloat16 or wider, within the bound.
No kernel may reach another device: no remote copies, remote signals or barrier semaphores. Data moves between devices by JAX's collectives and lax.ppermute only.
A program may use at most 320 MiB of HBM per device.

v0:
```python
import jax
import jax.numpy as jnp
from jax import lax
from jax.sharding import PartitionSpec as P

D = 1024
HEADS = 8
DK = 128
DV = 256
CONV = 4
SPAN = 64


HIGH = lax.Precision.HIGHEST
EPS = 1e-06


def from_behind(block, axis, distance):
    devices = range(lax.axis_size(axis))
    route = [(i - distance, i) for i in devices if i - distance in devices]
    return lax.ppermute(block, axis, route)


def silu(value):
    return value * jax.nn.sigmoid(value)


def product(left, right):
    return jnp.dot(left, right, preferred_element_type=jnp.float32)


def product_left(left, right):
    return lax.dot_general(
        left, right, (((0,), (0,)), ((), ())), preferred_element_type=jnp.float32
    )


def product_right(left, right):
    return lax.dot_general(
        left, right, (((1,), (1,)), ((), ())), preferred_element_type=jnp.float32
    )


def inverse_root(value):
    return lax.rsqrt(jnp.mean(value * value, axis=-1, keepdims=True) + EPS)


def norm_back(grad, normed, inverse, gain):
    scaled = grad * gain
    return (
        jnp.sum(grad * normed, axis=0),
        inverse * (scaled - normed * jnp.mean(scaled * normed, axis=-1, keepdims=True)),
    )


def unit_rows(value):
    return value * lax.rsqrt(jnp.sum(value * value, axis=-1, keepdims=True) + EPS)


def prepare(padded, filters, gate_pre, decay_log, decay_bias):
    seqs = padded.shape[0]
    piece = padded.shape[1] - (CONV - 1)
    width = HEADS * DK
    convolved = filters[:, 0] * padded[:, 0:piece]
    for offset in range(1, CONV):
        convolved = convolved + filters[:, offset] * padded[:, offset : offset + piece]
    activated = silu(convolved)
    queries = unit_rows(activated[..., :width].reshape(seqs, piece, HEADS, DK)) * DK ** (-0.5)
    keys = unit_rows(activated[..., width : 2 * width].reshape(seqs, piece, HEADS, DK))
    values = activated[..., 2 * width :].reshape(seqs, piece, HEADS, DV)
    betas = jax.nn.sigmoid(gate_pre[..., :HEADS])
    decays = -jnp.exp(decay_log) * jax.nn.softplus(gate_pre[..., HEADS:] + decay_bias)
    order = (0, 2, 1, 3)
    return (
        jnp.transpose(queries, order),
        jnp.transpose(keys, order),
        jnp.transpose(values, order),
        jnp.transpose(betas, (0, 2, 1)),
        jnp.transpose(decays, (0, 2, 1)),
    )


def span_rule(queries, keys, values, betas, decays, state):
    seqs, heads, piece = (keys.shape[0], keys.shape[1], keys.shape[2])
    blocks = piece // SPAN

    def split(value):
        return value.reshape(seqs, heads, blocks, SPAN, *value.shape[3:])

    queries, keys, values, betas, decays = (
        split(queries),
        split(keys),
        split(values),
        split(betas),
        split(decays),
    )
    cumul = jnp.cumsum(decays, axis=-1)
    spread = cumul[..., :, None] - cumul[..., None, :]
    row_ids = lax.broadcasted_iota(jnp.int32, (SPAN, SPAN), 0)
    col_ids = lax.broadcasted_iota(jnp.int32, (SPAN, SPAN), 1)
    fading = jnp.exp(jnp.minimum(spread, 0.0))
    strict = jnp.where(row_ids > col_ids, fading, 0.0)
    causal = jnp.where(row_ids >= col_ids, fading, 0.0)
    intersections = jnp.einsum("...id,...jd->...ij", keys, keys, precision=HIGH)
    system = jnp.eye(SPAN, dtype=jnp.float32) + betas[..., :, None] * intersections * strict
    growth = jnp.exp(cumul)[..., None]
    right = jnp.concatenate([betas[..., None] * growth * keys, betas[..., None] * values], axis=-1)
    solved = jax.scipy.linalg.solve_triangular(system, right, lower=True, unit_diagonal=True)
    erasers = solved[..., :DK]
    targets = solved[..., DK:]
    scores = jnp.einsum("...id,...jd->...ij", queries, keys, precision=HIGH) * causal
    lifted = queries * growth
    tails = keys * jnp.exp(cumul[..., -1:] - cumul)[..., None]
    closing = jnp.exp(cumul[..., -1])[..., None, None]

    def advance(carry, block):
        erase_b, target_b, lifted_b, tail_b, score_b, closing_b = block
        fresh = target_b - jnp.einsum("...cd,...de->...ce", erase_b, carry, precision=HIGH)
        result = jnp.einsum("...cd,...de->...ce", lifted_b, carry, precision=HIGH) + jnp.einsum(
            "...ij,...je->...ie", score_b, fresh, precision=HIGH
        )
        carry = closing_b * carry + jnp.einsum("...cd,...ce->...de", tail_b, fresh, precision=HIGH)
        return (carry, result)

    stacked = tuple(
        (jnp.moveaxis(value, 2, 0) for value in (erasers, targets, lifted, tails, scores, closing))
    )
    final, results = lax.scan(advance, state, stacked)
    return (jnp.moveaxis(results, 0, 2).reshape(seqs, heads, piece, values.shape[-1]), final)


def finish(mixed, outgate, gain):
    seqs, heads, piece = (mixed.shape[0], mixed.shape[1], mixed.shape[2])
    tokens_first = jnp.transpose(mixed, (0, 2, 1, 3))
    normed = tokens_first * inverse_root(tokens_first) * gain
    return (normed * silu(outgate.reshape(seqs, piece, heads, DV))).reshape(seqs, piece, heads * DV)


def shards(
    tokens,
    cotangent,
    gain_mixer,
    proj_input,
    conv_filter,
    proj_gates,
    proj_outgate,
    gain_heads,
    proj_output,
    gain_feed,
    feed_gate,
    feed_up,
    feed_down,
    decay_log,
    decay_bias,
):
    seqs, piece = (tokens.shape[0], tokens.shape[1])
    rows = seqs * piece
    width = HEADS * DK
    channels = 2 * width + HEADS * DV
    edge_rows = CONV - 1
    (
        gain_first,
        input_matrix,
        filter_bank,
        gates_matrix,
        outgate_matrix,
        heads_gain,
        output_matrix,
    ) = (
        lax.all_gather(gain_mixer, ("dp", "seq"), axis=0, tiled=True),
        lax.all_gather(proj_input, ("dp", "seq"), axis=0, tiled=True),
        lax.all_gather(conv_filter, ("dp", "seq"), axis=0, tiled=True),
        lax.all_gather(proj_gates, ("dp", "seq"), axis=0, tiled=True),
        lax.all_gather(proj_outgate, ("dp", "seq"), axis=0, tiled=True),
        lax.all_gather(gain_heads, ("dp", "seq"), axis=0, tiled=True),
        lax.all_gather(proj_output, ("dp", "seq"), axis=0, tiled=True),
    )
    gain_second, gate_matrix, upward_matrix, down_matrix = (
        lax.all_gather(gain_feed, ("dp", "seq"), axis=0, tiled=True),
        lax.all_gather(feed_gate, ("dp", "seq"), axis=0, tiled=True),
        lax.all_gather(feed_up, ("dp", "seq"), axis=0, tiled=True),
        lax.all_gather(feed_down, ("dp", "seq"), axis=0, tiled=True),
    )
    residual = tokens.astype(jnp.float32).reshape(rows, D)
    inverse_one = inverse_root(residual)
    normed_one = residual * inverse_one
    first = (normed_one * gain_first.astype(jnp.float32)).astype(jnp.bfloat16)
    projected = product(first, input_matrix).astype(jnp.bfloat16).reshape(seqs, piece, channels)
    gate_pre = product(first, gates_matrix).reshape(seqs, piece, 2 * HEADS)
    outgate = product(first, outgate_matrix).reshape(seqs, piece, HEADS * DV)
    bank = filter_bank.astype(jnp.float32)
    edge = from_behind(projected[:, piece - edge_rows :], "seq", 1)
    padded = jnp.concatenate([edge, projected], axis=1).astype(jnp.float32)
    queries, keys, values, betas, decays = prepare(padded, bank, gate_pre, decay_log, decay_bias)
    identity = jnp.broadcast_to(jnp.eye(DK, dtype=jnp.float32), (seqs, HEADS, DK, DK))
    widened = jnp.concatenate([values, jnp.zeros((seqs, HEADS, piece, DK), jnp.float32)], axis=-1)
    opening = jnp.concatenate([jnp.zeros((seqs, HEADS, DK, DV), jnp.float32), identity], axis=-1)
    local_out, local_end = span_rule(queries, keys, widened, betas, decays, opening)
    carried = local_end[..., :DV]
    transfer = local_end[..., DV:]

    def forward_relay(turn, pair):
        arriving = from_behind(pair[0].astype(jnp.bfloat16), "seq", 1).astype(jnp.float32)

        def forward_update(held):
            return (
                carried + jnp.einsum("...dk,...ke->...de", transfer, arriving, precision=HIGH),
                arriving,
            )

        def forward_remain(held):
            return held

        return lax.cond(lax.axis_index("seq") == turn, forward_update, forward_remain, pair)

    incoming = lax.fori_loop(
        0, lax.axis_size("seq"), forward_relay, (jnp.zeros_like(carried), jnp.zeros_like(carried))
    )[1]
    reading = local_out[..., DV:]
    mixed = local_out[..., :DV] + jnp.einsum(
        "...pd,...de->...pe", reading, incoming, precision=HIGH
    )
    gated = (
        finish(mixed, outgate, heads_gain.astype(jnp.float32))
        .reshape(rows, HEADS * DV)
        .astype(jnp.bfloat16)
    )
    middle = residual + product(gated, output_matrix)
    inverse_two = inverse_root(middle)
    normed_two = middle * inverse_two
    second = (normed_two * gain_second.astype(jnp.float32)).astype(jnp.bfloat16)
    up_gate = product(second, gate_matrix)
    up_linear = product(second, upward_matrix)
    sigmoid_gate = jax.nn.sigmoid(up_gate)
    silu_gate = up_gate * sigmoid_gate
    hidden = (silu_gate * up_linear).astype(jnp.bfloat16)
    layer_out = (middle + product(hidden, down_matrix)).astype(jnp.bfloat16)
    grad_out = cotangent.astype(jnp.float32).reshape(rows, D)
    grad_branch = cotangent.reshape(rows, D)
    grad_feed_down = product_left(hidden, grad_branch)
    grad_hidden = product_right(grad_branch, down_matrix)
    grad_gate = (
        grad_hidden * up_linear * (sigmoid_gate + silu_gate * (1.0 - sigmoid_gate))
    ).astype(jnp.bfloat16)
    grad_up = (grad_hidden * silu_gate).astype(jnp.bfloat16)
    grad_feed_gate = product_left(second, grad_gate)
    grad_feed_up = product_left(second, grad_up)
    grad_second = product_right(grad_gate, gate_matrix) + product_right(grad_up, upward_matrix)
    grad_gain_feed, grad_norm_two = norm_back(
        grad_second, normed_two, inverse_two, gain_second.astype(jnp.float32)
    )
    grad_middle = grad_out + grad_norm_two
    grad_mixer_out = grad_middle.astype(jnp.bfloat16)
    grad_proj_output = product_left(gated, grad_mixer_out)
    grad_gated = product_right(grad_mixer_out, output_matrix).reshape(seqs, piece, HEADS * DV)
    _, pull_finish = jax.vjp(finish, mixed, outgate, heads_gain.astype(jnp.float32))
    grad_mixed, grad_outgate, grad_gain_heads = pull_finish(grad_gated)
    flow = jnp.einsum("...pd,...pe->...de", reading, grad_mixed, precision=HIGH)
    transposed = jnp.swapaxes(transfer, -1, -2)

    def backward_relay(turn, pair):
        arriving = from_behind(pair[0].astype(jnp.bfloat16), "seq", -1).astype(jnp.float32)

        def backward_update(held):
            return (
                flow + jnp.einsum("...ij,...je->...ie", transposed, arriving, precision=HIGH),
                arriving,
            )

        def backward_remain(held):
            return held

        return lax.cond(
            lax.axis_index("seq") == lax.axis_size("seq") - 1 - turn,
            backward_update,
            backward_remain,
            pair,
        )

    leaving = lax.fori_loop(
        0, lax.axis_size("seq"), backward_relay, (jnp.zeros_like(flow), jnp.zeros_like(flow))
    )[1]

    def rule_part(padded_in, filters_in, gates_in, log_in, bias_in):
        parts = prepare(padded_in, filters_in, gates_in, log_in, bias_in)
        return span_rule(parts[0], parts[1], parts[2], parts[3], parts[4], incoming)

    _, pull_rule = jax.vjp(rule_part, padded, bank, gate_pre, decay_log, decay_bias)
    grad_padded, grad_conv_filter, grad_gate_pre, grad_decay_log, grad_decay_bias = pull_rule(
        (grad_mixed, leaving)
    )
    returned = from_behind(grad_padded[:, :edge_rows].astype(jnp.bfloat16), "seq", -1).astype(
        jnp.float32
    )
    grad_local = grad_padded[:, edge_rows:]
    grad_projected = jnp.concatenate(
        [grad_local[:, : piece - edge_rows], grad_local[:, piece - edge_rows :] + returned], axis=1
    )
    grad_projected = grad_projected.astype(jnp.bfloat16).reshape(rows, channels)
    grad_gates_low = grad_gate_pre.reshape(rows, 2 * HEADS).astype(jnp.bfloat16)
    grad_outgate_low = grad_outgate.reshape(rows, HEADS * DV).astype(jnp.bfloat16)
    grad_proj_input = product_left(first, grad_projected)
    grad_proj_gates = product_left(first, grad_gates_low)
    grad_proj_outgate = product_left(first, grad_outgate_low)
    grad_first = (
        product_right(grad_projected, input_matrix)
        + product_right(grad_gates_low, gates_matrix)
        + product_right(grad_outgate_low, outgate_matrix)
    )
    grad_gain_mixer, grad_norm_one = norm_back(
        grad_first, normed_one, inverse_one, gain_first.astype(jnp.float32)
    )
    tokens_grad = (grad_middle + grad_norm_one).reshape(seqs, piece, D)
    summed = (
        lax.psum_scatter(grad_gain_mixer, ("dp", "seq"), scatter_dimension=0, tiled=True),
        lax.psum_scatter(grad_proj_input, ("dp", "seq"), scatter_dimension=0, tiled=True),
        lax.psum_scatter(grad_conv_filter, ("dp", "seq"), scatter_dimension=0, tiled=True),
        lax.psum_scatter(grad_proj_gates, ("dp", "seq"), scatter_dimension=0, tiled=True),
        lax.psum_scatter(grad_proj_outgate, ("dp", "seq"), scatter_dimension=0, tiled=True),
        lax.psum_scatter(grad_gain_heads, ("dp", "seq"), scatter_dimension=0, tiled=True),
        lax.psum_scatter(grad_proj_output, ("dp", "seq"), scatter_dimension=0, tiled=True),
        lax.psum_scatter(grad_gain_feed, ("dp", "seq"), scatter_dimension=0, tiled=True),
        lax.psum_scatter(grad_feed_gate, ("dp", "seq"), scatter_dimension=0, tiled=True),
        lax.psum_scatter(grad_feed_up, ("dp", "seq"), scatter_dimension=0, tiled=True),
        lax.psum_scatter(grad_feed_down, ("dp", "seq"), scatter_dimension=0, tiled=True),
    )
    decay_grads = lax.psum((grad_decay_log, grad_decay_bias), ("dp", "seq"))
    return (
        layer_out.reshape(seqs, piece, D),
        tokens_grad,
        summed[0],
        summed[1],
        summed[2],
        summed[3],
        summed[4],
        summed[5],
        summed[6],
        summed[7],
        summed[8],
        summed[9],
        summed[10],
        decay_grads[0],
        decay_grads[1],
    )


def solution(mesh):
    in_specs = (
        P("dp", "seq", None),
        P("dp", "seq", None),
        P(("dp", "seq")),
        P(("dp", "seq"), None),
        P(("dp", "seq"), None),
        P(("dp", "seq"), None),
        P(("dp", "seq"), None),
        P(("dp", "seq")),
        P(("dp", "seq"), None),
        P(("dp", "seq")),
        P(("dp", "seq"), None),
        P(("dp", "seq"), None),
        P(("dp", "seq"), None),
        P(),
        P(),
    )
    out_specs = (
        P("dp", "seq", None),
        P("dp", "seq", None),
        P(("dp", "seq")),
        P(("dp", "seq"), None),
        P(("dp", "seq"), None),
        P(("dp", "seq"), None),
        P(("dp", "seq"), None),
        P(("dp", "seq")),
        P(("dp", "seq"), None),
        P(("dp", "seq")),
        P(("dp", "seq"), None),
        P(("dp", "seq"), None),
        P(("dp", "seq"), None),
        P(),
        P(),
    )
    return jax.shard_map(shards, mesh=mesh, in_specs=in_specs, out_specs=out_specs, check_vma=False)
```

profile of v0, /device:TPU:0, one launch (start us, length us, event | category | flops | bytes accessed | tf_op | source)
XLA Modules:
  0.0 3102.4 jit_solution(1273707540434595056)
XLA Ops:
  11.4 72.2 %all-gather = bf16[32,32,16]{1,2,0:T(8,128)(2,1)S(1)} all-gather(bf16[1,32,16]{1,2,0:T(8,128)(2,1)} %bitcast.760), channel_id=1, replica_groups=mesh['dp'=8,'seq'=4] {'dp','seq'}, dimensions={0}, use_global_device_ids=true | all-gather | bytes 33792 | tf_op jit(solution)/shard_map/all_gather | solution.py:173
  84.6 37.3 %all-reduce.26 = (bf16[1024]{0:T(1024)(128)(2,1)S(1)}, bf16[256]{0:T(256)(128)(2,1)S(1)}, bf16[1024]{0:T(1024)(128)(2,1)S(1)}) all-reduce(bf16[1024]{0:T(1024)(128)(2,1)S(1)} %dynamic-update-slice, bf16[256]{0:T(256)(128)(2,1)S(1)} %dynamic-update-slice.1, ...), channel_id=1, replica_groups=mesh['dp'=8,'seq'=4] {'dp','seq'}, use_global_device_ids=true, to_apply=%add.19 | all-reduce | flops 2304 | bytes 9216
  126.4 65.8 %all_gather.35 = bf16[4096,4]{0,1:T(4,128)(2,1)S(1)} all-gather(bf16[128,4]{0,1:T(4,128)(2,1)S(1)} %copy-done.105), channel_id=1, replica_groups=mesh['dp'=8,'seq'=4] {'dp','seq'}, dimensions={0}, use_global_device_ids=true | all-gather | bytes 33792 | tf_op jit(solution)/shard_map/all_gather | solution.py:172
  192.7 8.3 fusion.102
  205.0 6.8 fusion.244
  211.8 5.8 copy.328
  217.6 7.0 maximum_convert_fusion
  224.6 18.6 fusion.94
  287.0 316.0 %custom-call.13 = f32[8,8,1,64,64]{3,4,2,1,0:T(8,128)} custom-call(f32[8,8,1,64,64]{4,3,2,1,0:T(8,128)} %get-tuple-element.996), custom_call_target="InvertDiagBlocksLowerTriangular" | custom-call | tf_op jit(solution)/shard_map/jit(_solve_triangular)/vmap(vmap())/triangular_solve | solution.py:108
  607.1 10.3 fusion.111
  625.5 79.9 %while.82 = (s32[]{:T(128)}, f32[1,8,128,384]{3,2,1,0:T(8,128)S(1)}, f32[8,1,8,64,384]{4,3,2,1,0:T(8,128)}, f32[8,1,8,1,1]{2,4,3,1,0:T(1,128)S(1)}, f32[8,1,8,64...) while((s32[]{:T(128)}, ...), condition=%wide.region_5.6_spmd, body=%wide.region_4.5_spmd.sunk | while | flops 1058144256 | bytes 12847321 | solution.py:128
  711.7 6.1 copy.321
  717.9 53.0 %while.83 = (s32[]{:T(128)}, bf16[1,8,128,256]{3,2,1,0:T(8,128)(2,1)}, f32[1,8,128,256]{3,2,1,0:T(8,128)S(1)}, f32[1,8,128,128]{3,2,1,0:T(8,128)S(1)}, f32[1,8,128,256]{3,2,1,0:T(8,128)S(1)}, /*index=5*/s32[]{:T(128)}, u32[]{:T(128)}) while((s32[]{:T(128)}, bf16[1,8,128,256]{3,2,1,0:T(8,128)(2,1)}, f32[1,8,128,256]{3,2,1,0:T(8,128)S(1)}, ...), condition=%wide.region_9.10_spmd, body=%wide.region_6.9_spmd.sunk | while | flops 403439616 | bytes 8913119 | solution.py:216
  721.3 6.4 collective-permute-done
  734.0 6.2 collective-permute-done
  741.4 7.1 collective-permute-start
  748.5 8.6 collective-permute-done
  758.3 5.2 collective-permute-start
  763.5 6.2 collective-permute-done
  770.9 6.8 multiply_reduce_fusion.7
  785.9 5.4 multiply_reduce_fusion.12
  795.2 6.9 fusion.95
  807.7 7.5 fusion.255
  815.2 8.0 fusion.256
  823.2 11.0 multiply_convert_fusion
  834.2 7.3 fusion.257
  852.2 5.3 copy.331
  857.6 6.5 multiply_reduce_fusion.4
  870.0 6.7 fusion.175
  877.7 68.7 %while.84 = (s32[]{:T(128)}, bf16[1,8,128,256]{3,2,1,0:T(8,128)(2,1)}, f32[1,8,128,256]{3,2,1,0:T(8,128)}, f32[1,8,128,128]{3,2,1,0:T(8,128)S(1)}, f32[1,8,128,2...) while((s32[]{:T(128)}, bf16[1,8,128,256]{3,2,1,0:T(8,128)(2,1)}, ...), condition=%wide.region_17.18_spmd, body=%wide.region_14.17_spmd.sunk | while | flops 403439616 | bytes 8913139 | solution.py:280
  879.0 15.2 collective-permute-done.1
  895.6 16.5 collective-permute-done.1
  913.6 14.4 collective-permute-done.1
  929.5 14.0 collective-permute-done.1
  956.8 48.1 %while.85 = (s32[]{:T(128)}, f32[1,8,128,256]{3,2,1,0:T(8,128)S(1)}, f32[8,1,8,128,256]{4,3,2,1,0:T(8,128)}, f32[8,1,8,64,256]{4,3,2,1,0:T(8,128)}, f32[8,1,8,1,...) while((s32[]{:T(128)}, ...), condition=%wide.region_19.20_spmd, body=%wide.region_18.19_spmd.sunk | while | flops 403308544 | bytes 7865553 | solution.py:128
  1013.9 194.9 %while.86 = (s32[]{:T(128)}, f32[1,8,128,256]{2,3,1,0:T(8,128)S(1)}, f32[8,1,8,64,128]{4,3,2,1,0:T(8,128)}, f32[8,1,8,64,256]{4,3,2,1,0:T(8,128)}, f32[8,1,8,64,...) while((s32[]{:T(128)}, ...), condition=%wide.region_22.23_spmd, body=%wide.region_20.22_spmd.sunk | while | flops 1410990080 | bytes 23078216 | solution.py:128
  1208.8 11.4 fusion.98
  1220.3 6.6 fusion.114
  1242.4 6.2 fusion.162
  1260.6 5.3 slice_multiply_fusion
  1269.5 5.4 add_add_fusion.1
  1277.6 8.7 bitcast_add_fusion.3
  1289.3 5.5 add_add_fusion.2
  1297.5 6.6 copy.491
  1304.1 5.0 reshape.1220
  1309.1 23.0 multiply_reduce_fusion.3
  1338.5 7.5 fusion.201
  1347.6 7.3 fusion.195
  1356.2 7.9 fusion.259
  1364.1 7.7 fusion.260
  1373.1 7.8 fusion.179
  1381.7 11.6 broadcast_multiply_fusion
  1393.3 14.3 fusion.252
  1415.5 8.5 fusion.112
  1430.4 6.9 fusion.174
  1437.3 9.8 fusion.130
  1447.1 42.1 %all-reduce.25 = (f32[1024]{0:T(1024)S(1)}, f32[256]{0:T(256)S(1)}, f32[1024]{0:T(1024)S(1)}, f32[8]{0:T(128)}, f32[8]{0:T(128)}) all-reduce(f32[1024]{0:T(1024)S(1)} %get-tuple-element.859, f32[256]{0:T(256)S(1)} %copy-done.100, f32[1024]{0:T(1024)S(1)} %copy-done.99, ...), channel_id=2, replica_groups=mesh['dp'=8,'seq'=4] {'dp','seq'}, use_global_device_ids=true, to_apply=%region_36.37.clone | all-reduce | flops 2320 | bytes 18560
  1495.9 110.2 %reduce-scatter.27.cloned.1.call-done = f32[32,16]{1,0:T(8,128)} async-done(((f32[1024,16]{1,0:T(8,128)}), f32[32,16]{1,0:T(8,128)}) %reduce-scatter.27.cloned.1.call-update) | async-done | bytes 2064
  1607.5 181.1 %reduce-scatter.15.cloned.1.call-done = f32[32,2048]{1,0:T(8,128)} async-done(((f32[1024,2048]{1,0:T(8,128)}), f32[32,2048]{1,0:T(8,128)}) %reduce-scatter.15.cloned.1.call-update) | async-done | bytes 262160 | tf_op jit(solution)/shard_map/reduce_scatter | solution.py:319
  1788.6 187.2 %reduce-scatter.17.cloned.1.call-done = f32[64,1024]{1,0:T(8,128)} async-done(((f32[2048,1024]{1,0:T(8,128)}), f32[64,1024]{1,0:T(8,128)}) %reduce-scatter.17.cloned.1.call-update) | async-done | bytes 262160 | tf_op jit(solution)/shard_map/reduce_scatter | solution.py:321
  1975.8 252.6 %reduce-scatter.19.cloned.1.call-done = f32[32,2816]{1,0:T(8,128)} async-done(((f32[1024,2816]{1,0:T(8,128)}), f32[32,2816]{1,0:T(8,128)}) %reduce-scatter.19.cloned.1.call-update) | async-done | bytes 360464 | tf_op jit(solution)/shard_map/reduce_scatter | solution.py:323
  2228.4 252.8 %reduce-scatter.21.cloned.1.call-done = f32[32,2816]{1,0:T(8,128)} async-done(((f32[1024,2816]{1,0:T(8,128)}), f32[32,2816]{1,0:T(8,128)}) %reduce-scatter.21.cloned.1.call-update) | async-done | bytes 360464 | tf_op jit(solution)/shard_map/reduce_scatter | solution.py:324
  2481.2 252.9 %reduce-scatter.23.cloned.1.call-done = f32[88,1024]{1,0:T(8,128)} async-done(((f32[2816,1024]{1,0:T(8,128)}), f32[88,1024]{1,0:T(8,128)}) %reduce-scatter.23.cloned.1.call-update) | async-done | bytes 360464 | tf_op jit(solution)/shard_map/reduce_scatter | solution.py:325
  2734.2 361.5 %reduce-scatter.13.cloned.1.call-done = f32[32,4096]{1,0:T(8,128)} async-done(((f32[1024,4096]{1,0:T(8,128)}), f32[32,4096]{1,0:T(8,128)}) %reduce-scatter.13.cloned.1.call-update) | async-done | bytes 524304 | tf_op jit(solution)/shard_map/reduce_scatter | solution.py:316
  (617 shorter events, 551.1 us)
Async XLA Ops:
  7.2 76.7 %copy-start.108 = (bf16[32]{0:T(256)(128)(2,1)S(1)}, bf16[32]{0:T(256)(128)(2,1)}, u32[]{:S(2)}) copy-start(bf16[32]{0:T(256)(128)(2,1)} %param.31) | copy-start | bytes 196
  7.2 76.9 %copy-start.109 = (bf16[32]{0:T(256)(128)(2,1)S(1)}, bf16[32]{0:T(256)(128)(2,1)}, u32[]{:S(2)}) copy-start(bf16[32]{0:T(256)(128)(2,1)} %param.38) | copy-start | bytes 196
  7.2 77.1 %copy-start.110 = (bf16[8]{0:T(256)(128)(2,1)S(1)}, bf16[8]{0:T(256)(128)(2,1)}, u32[]{:S(2)}) copy-start(bf16[8]{0:T(256)(128)(2,1)} %param.36) | copy-start | bytes 52
  7.2 114.6 %copy-start.45 = (bf16[1,512,1024]{2,1,0:T(8,128)(2,1)S(1)}, bf16[1,512,1024]{2,1,0:T(8,128)(2,1)}, u32[]{:S(2)}) copy-start(bf16[1,512,1024]{2,1,0:T(8,128)(2,1)} %param.29) | copy-start | bytes 3145732
  7.2 114.9 %copy-start.111 = (f32[8]{0:T(128)S(1)}, f32[8]{0:T(128)}, u32[]{:S(2)}) copy-start(f32[8]{0:T(128)} %param.42) | copy-start | bytes 100
  7.2 185.5 %all-gather.8.cloned.1.call-start = ((), (), s32[]{:S(2)}) async-start(), calls=%async_computation.8 | async-start | bytes 8650752 | tf_op jit(solution)/shard_map/all_gather | solution.py:171
  8.0 197.0 %all-gather.10.cloned.1.call-start = ((), (), s32[]{:S(2)}) async-start(), calls=%async_computation.9 | async-start | bytes 4325376 | tf_op jit(solution)/shard_map/all_gather | solution.py:174
  8.7 777.2 %all-gather.12.cloned.1.call-start = ((), (), s32[]{:S(2)}) async-start(), calls=%async_computation.10 | async-start | bytes 4325376 | tf_op jit(solution)/shard_map/all_gather | solution.py:176
  9.5 798.2 %all-gather.14.cloned.1.call-start = ((), (), s32[]{:S(2)}) async-start(), calls=%async_computation.11 | async-start | bytes 5947392 | tf_op jit(solution)/shard_map/all_gather | solution.py:180
  10.0 805.2 %all-gather.16.cloned.1.call-start = ((), (), s32[]{:S(2)}) async-start(), calls=%async_computation.12 | async-start | bytes 5947392 | tf_op jit(solution)/shard_map/all_gather | solution.py:181
  10.6 812.6 %all-gather.18.cloned.1.call-start = ((), (), s32[]{:S(2)}) async-start(), calls=%async_computation.13 | async-start | bytes 5947392 | tf_op jit(solution)/shard_map/all_gather | solution.py:182
  11.2 111.5 %copy-start.101 = (f32[8]{0:T(128)S(1)}, f32[8]{0:T(128)}, u32[]{:S(2)}) copy-start(f32[8]{0:T(128)} %param.43) | copy-start | bytes 100
  11.2 1483.2 %reduce-scatter.25.cloned.1.call-start = ((), (), s32[]{:S(2)}) async-start(), calls=%async_computation.20 | async-start | bytes 2162688
  11.3 113.0 %copy-start.59 = (bf16[1,8,128,256]{3,2,1,0:T(8,128)(2,1)}, bf16[1,8,128,256]{3,2,1,0:T(8,128)(2,1)S(1)}, u32[]{:S(2)}) copy-start(bf16[1,8,128,256]{3,2,1,0:T(8,128)(2,1)S(1)} %fusion.253) | copy-start | bytes 1572868
  11.4 272.9 %copy-start.72 = (pred[64,64]{1,0:T(8,128)(4,1)}, pred[64,64]{1,0:T(8,128)(4,1)S(1)}, u32[]{:S(2)}) copy-start(pred[64,64]{1,0:T(8,128)(4,1)S(1)} %get-tuple-element.1019) | copy-start | bytes 12292
  11.4 272.9 %copy-start.78 = (pred[64,64]{1,0:T(8,128)(4,1)}, pred[64,64]{1,0:T(8,128)(4,1)S(1)}, u32[]{:S(2)}) copy-start(pred[64,64]{1,0:T(8,128)(4,1)S(1)} %get-tuple-element.1018) | copy-start | bytes 12292
  83.8 38.4 %copy-start.92 = (bf16[1024,16]{0,1:T(8,128)(2,1)}, bf16[1024,16]{0,1:T(8,128)(2,1)S(1)}, u32[]{:S(2)}) copy-start(bf16[1024,16]{0,1:T(8,128)(2,1)S(1)} %reshape.1236) | copy-start | bytes 98308
  121.9 83.1 %copy-start.66 = (f32[1024]{0:T(1024)}, f32[1024]{0:T(1024)S(1)}, u32[]{:S(2)}) copy-start(f32[1024]{0:T(1024)S(1)} %convert_element_type.143) | copy-start | bytes 12292
  122.2 82.8 %copy-start.76 = (f32[512]{0:T(512)}, f32[512]{0:T(512)S(1)}, u32[]{:S(2)}) copy-start(f32[512]{0:T(512)S(1)} %add_rsqrt_fusion.3) | copy-start | bytes 6148
  126.2 158.1 %copy-start.43 = (f32[1,8,8,64]{3,2,1,0:T(8,128)}, f32[1,8,8,64]{3,2,1,0:T(8,128)S(1)}, u32[]{:S(2)}) copy-start(f32[1,8,8,64]{3,2,1,0:T(8,128)S(1)} %reduce_window_sum.24) | copy-start | bytes 49156
  126.3 74.7 %copy-start.97 = (f32[8,8]{1,0:T(8,128)}, f32[8,8]{1,0:T(8,128)S(1)}, u32[]{:S(2)}) copy-start(f32[8,8]{1,0:T(8,128)S(1)} %get-tuple-element.865) | copy-start | bytes 772
  192.3 32.3 %copy-start.80 = (f32[4096,1]{0,1:T(1,128)}, f32[4096,1]{0,1:T(1,128)S(1)}, u32[]{:S(2)}) copy-start(f32[4096,1]{0,1:T(1,128)S(1)} %get-tuple-element.1002) | copy-start | bytes 49156
  192.3 32.3 %copy-start.82 = (f32[4096,1]{0,1:T(1,128)}, f32[4096,1]{0,1:T(1,128)S(1)}, u32[]{:S(2)}) copy-start(f32[4096,1]{0,1:T(1,128)S(1)} %get-tuple-element.1003) | copy-start | bytes 49156
  192.3 32.3 %copy-start.84 = (f32[4096,1]{0,1:T(1,128)}, f32[4096,1]{0,1:T(1,128)S(1)}, u32[]{:S(2)}) copy-start(f32[4096,1]{0,1:T(1,128)S(1)} %get-tuple-element.1004) | copy-start | bytes 49156
  192.3 32.3 %copy-start.86 = (f32[4096,1]{0,1:T(1,128)}, f32[4096,1]{0,1:T(1,128)S(1)}, u32[]{:S(2)}) copy-start(f32[4096,1]{0,1:T(1,128)S(1)} %get-tuple-element.1005) | copy-start | bytes 49156
  192.4 91.9 %copy-start.74 = (pred[64,64]{1,0:T(8,128)(4,1)}, pred[64,64]{1,0:T(8,128)(4,1)S(1)}, u32[]{:S(2)}) copy-start(pred[64,64]{1,0:T(8,128)(4,1)S(1)} %get-tuple-element.1020) | copy-start | bytes 12292
  192.7 410.3 %copy-start.64 = (f32[8,8,64]{2,1,0:T(8,128)}, f32[8,8,64]{2,1,0:T(8,128)S(1)}, u32[]{:S(2)}) copy-start(f32[8,8,64]{2,1,0:T(8,128)S(1)} %get-tuple-element.998) | copy-start | bytes 49156
  192.7 410.3 %copy-start.68 = (f32[8,8,64]{2,1,0:T(8,128)}, f32[8,8,64]{2,1,0:T(8,128)S(1)}, u32[]{:S(2)}) copy-start(f32[8,8,64]{2,1,0:T(8,128)S(1)} %get-tuple-element.999) | copy-start | bytes 49156
  192.7 410.3 %copy-start.70 = (f32[8,8,64]{2,1,0:T(8,128)}, f32[8,8,64]{2,1,0:T(8,128)S(1)}, u32[]{:S(2)}) copy-start(f32[8,8,64]{2,1,0:T(8,128)S(1)} %get-tuple-element.997) | copy-start | bytes 49156
  203.0 14.6 collective-permute-start.2
  253.7 22.4 copy-start.56
  607.1 10.3 copy-start.27
  718.1 9.6 collective-permute-start
  730.7 9.5 collective-permute-start
  741.4 15.7 collective-permute-start
  758.3 11.4 collective-permute-start
  770.8 8.8 copy-start.8
  792.6 22.6 copy-start.60
  834.2 7.4 copy-start.114
  834.2 7.4 copy-start.113
  834.2 7.4 copy-start.53
  834.2 7.4 copy-start.106
  857.6 8.3 copy-start.16
  877.7 16.5 collective-permute-start.1
  894.3 17.8 collective-permute-start.1
  912.3 15.7 collective-permute-start.1
  928.2 15.3 collective-permute-start.1
  1208.8 11.4 copy-start.13
  1208.8 11.4 copy-start.22
  1208.8 11.4 copy-start.30
  1220.2 7.1 copy-start.34
  1226.9 26.6 copy-start.19
  1277.6 10.0 copy-start.4
  1334.2 271.9 %reduce-scatter.27.cloned.1.call-start = ((), (), s32[]{:S(2)}) async-start(), calls=%async_computation.21 | async-start | bytes 540672
  1338.5 450.1 %reduce-scatter.15.cloned.1.call-start = ((), (), s32[]{:S(2)}) async-start(), calls=%async_computation.15 | async-start | bytes 8650752 | tf_op jit(solution)/shard_map/reduce_scatter | solution.py:319
  1346.0 629.7 %reduce-scatter.17.cloned.1.call-start = ((), (), s32[]{:S(2)}) async-start(), calls=%async_computation.16 | async-start | bytes 8650752 | tf_op jit(solution)/shard_map/reduce_scatter | solution.py:321
  1355.0 873.5 %reduce-scatter.19.cloned.1.call-start = ((), (), s32[]{:S(2)}) async-start(), calls=%async_computation.17 | async-start | bytes 11894784 | tf_op jit(solution)/shard_map/reduce_scatter | solution.py:323
  1364.1 1117.2 %reduce-scatter.21.cloned.1.call-start = ((), (), s32[]{:S(2)}) async-start(), calls=%async_computation.18 | async-start | bytes 11894784 | tf_op jit(solution)/shard_map/reduce_scatter | solution.py:324
  1371.9 1362.3 %reduce-scatter.23.cloned.1.call-start = ((), (), s32[]{:S(2)}) async-start(), calls=%async_computation.19 | async-start | bytes 11894784 | tf_op jit(solution)/shard_map/reduce_scatter | solution.py:325
  1380.9 1714.7 %reduce-scatter.13.cloned.1.call-start = ((), (), s32[]{:S(2)}) async-start(), calls=%async_computation.14 | async-start | bytes 17301504 | tf_op jit(solution)/shard_map/reduce_scatter | solution.py:316
  1408.4 6.2 collective-permute-start.3
  1437.3 9.8 copy-start.99
  1437.3 9.8 copy-start.100
  1437.3 53.6 %copy-start.40 = (f32[512,1024]{1,0:T(8,128)S(1)}, f32[512,1024]{1,0:T(8,128)}, u32[]{:S(2)}) copy-start(f32[512,1024]{1,0:T(8,128)} %copy-done.38) | copy-start | bytes 6291460
  (76 other events, 246.9 us)
Sparse Core Ops, SparseCore 0:
  10.9 80.4 all-gather.7
  94.3 61.3 all-gather.9
  158.6 60.3 all-gather.11
  221.7 66.4 all-gather.13
  290.9 67.5 all-gather.15
  361.3 68.8 all-gather.17
  1334.3 138.9 reduce-scatter.24
  1475.7 130.3 reduce-scatter.26
  1608.9 179.5 reduce-scatter.14
  1791.3 184.4 reduce-scatter.16
  1978.7 249.6 reduce-scatter.18
  2231.2 250.0 reduce-scatter.20
  2484.1 250.0 reduce-scatter.22
  2736.9 358.7 reduce-scatter.12
where the time goes:
time: 3110 us; the launch traced here: 3100 us
  waiting for transfers between devices  1690 us (54%)
  matrix products  520 us (17%)
  other arithmetic  463 us (15%)
  blocking collectives  217 us (7%)
  local copies, waits for them, and re-layouts  166 us (5%)
    reduce_scatter x1, waiting for transfers between devices, shards(): lax.psum_scatter(grad_proj_input, ('dp', 'seq'), scatter_dimension=0, til...  362 us
    another operation x4, other arithmetic, span_rule(): jax.scipy.linalg.solve_triangular(system, right, lower=True, unit_diagona...  316 us
    reduce_scatter x1, waiting for transfers between devices, shards(): lax.psum_scatter(grad_feed_down, ('dp', 'seq'), scatter_dimension=0, tile...  253 us
    reduce_scatter x1, waiting for transfers between devices, shards(): lax.psum_scatter(grad_feed_up, ('dp', 'seq'), scatter_dimension=0, tiled=...  253 us
    reduce_scatter x1, waiting for transfers between devices, shards(): lax.psum_scatter(grad_feed_gate, ('dp', 'seq'), scatter_dimension=0, tile...  253 us
    reduce_scatter x1, waiting for transfers between devices, shards(): lax.psum_scatter(grad_proj_output, ('dp', 'seq'), scatter_dimension=0, ti...  187 us
    reduce_scatter x1, waiting for transfers between devices, shards(): lax.psum_scatter(grad_proj_outgate, ('dp', 'seq'), scatter_dimension=0, t...  181 us
    unnamed x16, waiting for transfers between devices  114 us
  transfers between devices with their start and end apart: 24, of which 16 were waited for; matrix products, arithmetic and copies ran while one was open for 22% of the time, Pallas kernels for 0%

commit v1 on v0

v1 whole, which is shorter than its diff:
```python
import functools
import math
import jax
import jax.numpy as jnp
from jax import lax
from jax.experimental import pallas as pl
from jax.experimental.pallas import tpu as pltpu
from jax.sharding import PartitionSpec as P

D = 1024
HEADS = 8
DK = 128
DV = 256
CONV = 4
CHUNK = 128
PAIR = 2
EPS = 1e-06
WIDE = DV + DK
VMEM = 56 * 1024 * 1024
BF = jnp.bfloat16
F32 = jnp.float32


def mm(left, right, over=(1, 0)):
    return lax.dot_general(
        left.astype(BF), right.astype(BF), (((over[0],), (over[1],)), ((), ())), preferred_element_type=F32
    )


def mm_nt(left, right):
    return mm(left, right, (1, 1))


def mm_tn(left, right):
    return mm(left, right, (0, 0))


def grids():
    rows = lax.broadcasted_iota(jnp.int32, (CHUNK, CHUNK), 0)
    cols = lax.broadcasted_iota(jnp.int32, (CHUNK, CHUNK), 1)
    return rows, cols


def to_column(row, rows, cols):
    return jnp.sum(jnp.where(rows == cols, row, 0.0), axis=1, keepdims=True)


def to_row(column, rows, cols):
    return jnp.sum(jnp.where(rows == cols, column, 0.0), axis=0, keepdims=True)


def fades(decay_row, beta_row, rows, cols):
    cumul = jnp.sum(jnp.where(cols <= rows, decay_row, 0.0), axis=1, keepdims=True)
    cumul_row = to_row(cumul, rows, cols)
    beta = to_column(beta_row, rows, cols)
    fading = jnp.exp(jnp.minimum(cumul - cumul_row, 0.0))
    strict = jnp.where(rows > cols, fading, 0.0)
    causal = jnp.where(rows >= cols, fading, 0.0)
    last = cumul[CHUNK - 1 : CHUNK]
    return beta, strict, causal, jnp.exp(cumul), jnp.exp(last - cumul), jnp.exp(last)


def unit_lower_inverse(lower, rows, cols):
    def level(width):
        shift = width.bit_length() - 1
        row_block, col_block = lax.shift_right_logical(rows, shift), lax.shift_right_logical(cols, shift)
        return jnp.where((row_block == col_block + 1) & ((col_block & 1) == 0), lower, 0.0)

    inverse = jnp.where(rows == cols, 1.0, 0.0) - level(1)
    width = 2
    while width < CHUNK:
        inverse = inverse - mm(mm(inverse, level(width)), inverse)
        width *= 2
    return inverse


def convolve(x, edge, taps, held, piece):
    held[0:8] = edge
    held[8 : 8 + piece] = x.astype(F32)
    total = taps[0:1] * held[5 : 5 + piece]
    for j in range(1, CONV):
        total = total + taps[j : j + 1] * held[5 + j : 5 + j + piece]
    return total


def units(active):
    inverse = lax.rsqrt(jnp.sum(active * active, axis=-1, keepdims=True) + EPS)
    return active * inverse, inverse


def opening_kernel(
    piece, q_ref, k_ref, v_ref, qe_ref, ke_ref, ve_ref, qf_ref, kf_ref, vf_ref, beta_ref, decay_ref,
    local_ref, reading_ref, states_ref, inverse_ref, held_q, held_k, held_v,
):
    rows, cols = grids()
    q_conv = convolve(q_ref[...], qe_ref[...], qf_ref[...], held_q, piece)
    k_conv = convolve(k_ref[...], ke_ref[...], kf_ref[...], held_k, piece)
    v_conv = convolve(v_ref[...], ve_ref[...], vf_ref[...], held_v, piece)
    q_act = q_conv * jax.nn.sigmoid(q_conv)
    k_act = k_conv * jax.nn.sigmoid(k_conv)
    v_act = v_conv * jax.nn.sigmoid(v_conv)
    for head in range(PAIR):
        queries = units(q_act[:, head * DK : (head + 1) * DK])[0] * DK**-0.5
        keys = units(k_act[:, head * DK : (head + 1) * DK])[0]
        values = v_act[:, head * DV : (head + 1) * DV]
        state = jnp.concatenate(
            [jnp.zeros((DK, DV), F32), jnp.where(rows == cols, 1.0, 0.0)], axis=1
        )
        for chunk in range(piece // CHUNK):
            part = slice(chunk * CHUNK, (chunk + 1) * CHUNK)
            query, key, value = queries[part], keys[part], values[part]
            beta, strict, causal, grow, fade, closing = fades(
                decay_ref[head, :, part], beta_ref[head, :, part], rows, cols
            )
            both = mm_nt(jnp.concatenate([key, query], axis=0), key)
            inverse = unit_lower_inverse(beta * both[:CHUNK] * strict, rows, cols)
            scores = both[CHUNK:] * causal
            inverse_ref[part, head * CHUNK : (head + 1) * CHUNK] = inverse.astype(BF)
            seen = mm(jnp.concatenate([key * grow, query * grow], axis=0), state)
            wide = jnp.concatenate([value, jnp.zeros((CHUNK, DK), F32)], axis=1)
            fresh = mm(inverse, beta * (wide - seen[:CHUNK]))
            result = seen[CHUNK:] + mm(scores, fresh)
            state = closing * state + mm_tn(key * fade, fresh)
            local_ref[part, head * DV : (head + 1) * DV] = result[:, :DV]
            reading_ref[part, head * DK : (head + 1) * DK] = result[:, DV:].astype(BF)
            states_ref[0, head, chunk] = state.astype(BF)


def finish_kernel(local_ref, reading_ref, incoming_ref, outgate_ref, gain_ref, mixed_ref, gated_ref):
    for head in range(PAIR):
        wide = slice(head * DV, (head + 1) * DV)
        mixed = local_ref[:, wide] + mm(reading_ref[:, head * DK : (head + 1) * DK], incoming_ref[0, head])
        mixed_ref[:, wide] = mixed
        inverse = lax.rsqrt(jnp.mean(mixed * mixed, axis=-1, keepdims=True) + EPS)
        outgate = outgate_ref[:, wide]
        gated = mixed * inverse * gain_ref[0:1] * (outgate * jax.nn.sigmoid(outgate))
        gated_ref[:, wide] = gated.astype(BF)


def unfinish_kernel(
    grad_ref, mixed_ref, outgate_ref, gain_ref, reading_ref, grad_mixed_ref, grad_outgate_ref, gain_grad_ref, flow_ref
):
    gain = gain_ref[0:1]
    for head in range(PAIR):
        wide = slice(head * DV, (head + 1) * DV)
        mixed, outgate, grad = mixed_ref[:, wide], outgate_ref[:, wide], grad_ref[:, wide]
        inverse = lax.rsqrt(jnp.mean(mixed * mixed, axis=-1, keepdims=True) + EPS)
        normed = mixed * inverse
        sigmoid = jax.nn.sigmoid(outgate)
        gate = outgate * sigmoid
        along = grad * normed
        gain_grad = jnp.sum(along * gate, axis=0, keepdims=True)
        gain_grad_ref[0, head] = jnp.broadcast_to(gain_grad, (8, DV))
        grad_outgate_ref[:, wide] = (along * gain * (sigmoid + gate * (1.0 - sigmoid))).astype(BF)
        scaled = grad * gain * gate
        grad_mixed = inverse * (scaled - normed * jnp.mean(scaled * normed, axis=-1, keepdims=True))
        grad_mixed_ref[:, wide] = grad_mixed.astype(BF)
        flow_ref[0, head] = mm_tn(reading_ref[:, head * DK : (head + 1) * DK], grad_mixed)


def unconvolve(grad, taps, held_in, held_out, piece, grad_ref, edge_ref, taps_ref):
    width = grad.shape[1]
    held_out[0:8] = jnp.zeros((8, width), F32)
    held_out[8 : 8 + piece] = grad
    held_out[8 + piece : 16 + piece] = jnp.zeros((8, width), F32)
    total = taps[0:1] * held_out[11 : 11 + piece]
    edge = taps[0:1] * held_out[3:11]
    for j in range(1, CONV):
        total = total + taps[j : j + 1] * held_out[11 - j : 11 - j + piece]
        edge = edge + taps[j : j + 1] * held_out[3 - j : 11 - j]
    grad_ref[...] = total.astype(BF)
    edge_ref[...] = edge
    sums = [jnp.sum(grad * held_in[5 + j : 5 + j + piece], axis=0, keepdims=True) for j in range(CONV)]
    taps_ref[0] = jnp.concatenate(sums + [jnp.zeros((8 - CONV, width), F32)], axis=0)


def silu_slope(value, sigmoid):
    return sigmoid * (1.0 + value * (1.0 - sigmoid))


def closing_kernel(
    piece, q_ref, k_ref, v_ref, qe_ref, ke_ref, ve_ref, qf_ref, kf_ref, vf_ref, beta_ref, decay_ref,
    inverse_ref, states_ref, incoming_ref, grad_ref, leaving_ref,
    dq_ref, dk_ref, dv_ref, dqe_ref, dke_ref, dve_ref, dqf_ref, dkf_ref, dvf_ref, dbeta_ref, ddecay_ref,
    held_q, held_k, held_v, back_q, back_k, back_v,
):
    rows, cols = grids()
    q_conv = convolve(q_ref[...], qe_ref[...], qf_ref[...], held_q, piece)
    k_conv = convolve(k_ref[...], ke_ref[...], kf_ref[...], held_k, piece)
    v_conv = convolve(v_ref[...], ve_ref[...], vf_ref[...], held_v, piece)
    q_sig, k_sig, v_sig = jax.nn.sigmoid(q_conv), jax.nn.sigmoid(k_conv), jax.nn.sigmoid(v_conv)
    q_act, k_act, v_act = q_conv * q_sig, k_conv * k_sig, v_conv * v_sig
    dq_all, dk_all, dv_all = [], [], []
    chunks = piece // CHUNK
    for head in range(PAIR):
        narrow, wide = slice(head * DK, (head + 1) * DK), slice(head * DV, (head + 1) * DV)
        query_unit, query_scale = units(q_act[:, narrow])
        queries = query_unit * DK**-0.5
        keys, key_scale = units(k_act[:, narrow])
        values = v_act[:, wide]
        incoming = incoming_ref[0, head]
        grad_state = leaving_ref[0, head].astype(F32)
        grad_queries, grad_keys, grad_values = [None] * chunks, [None] * chunks, [None] * chunks
        for chunk in reversed(range(chunks)):
            part = slice(chunk * CHUNK, (chunk + 1) * CHUNK)
            query, key, value = queries[part], keys[part], values[part]
            beta, strict, causal, grow, fade, closing = fades(
                decay_ref[head, :, part], beta_ref[head, :, part], rows, cols
            )
            both = mm_nt(jnp.concatenate([key, query], axis=0), key)
            cross = both[:CHUNK] * strict
            lower = beta * cross
            scores = both[CHUNK:] * causal
            inverse = inverse_ref[part, head * CHUNK : (head + 1) * CHUNK]
            if chunk == 0:
                state = incoming.astype(F32)
            else:
                before = states_ref[0, head, chunk - 1]
                state = before[:, :DV].astype(F32) + mm(before[:, DV:], incoming)
            grad = grad_ref[part, wide]
            seen = mm(key, state)
            plain = value - grow * seen
            fresh = mm(inverse, beta * plain)
            tail = key * fade
            lifted = query * grow
            grad_fresh = mm_tn(scores, grad) + mm(tail, grad_state)
            grad_right = mm_tn(inverse, grad_fresh)
            grad_seen = -(beta * grow) * grad_right
            pair = mm_nt(jnp.concatenate([grad.astype(F32), grad_right], axis=0), fresh)
            grad_scores = jnp.where(rows >= cols, pair[:CHUNK], 0.0)
            grad_lower = jnp.where(rows > cols, -pair[CHUNK:], 0.0)
            pair = mm_nt(jnp.concatenate([grad.astype(F32), grad_seen], axis=0), state)
            grad_lifted, grad_key = pair[:CHUNK], pair[CHUNK:]
            grad_tail = mm_nt(fresh, grad_state)
            grad_cross = grad_lower * strict * beta
            grad_both = grad_scores * causal
            grad_query = mm(grad_both, key) + grad_lifted * grow
            grad_key = (
                grad_key
                + mm(grad_cross, key)
                + mm_tn(jnp.concatenate([grad_cross, grad_both], axis=0), jnp.concatenate([key, query], axis=0))
                + grad_tail * fade
            )
            spread = grad_lower * lower + grad_scores * scores
            tail_sum = jnp.sum(grad_tail * tail, axis=1, keepdims=True)
            grad_cumul = (
                jnp.sum(spread, axis=1, keepdims=True)
                - to_column(jnp.sum(spread, axis=0, keepdims=True), rows, cols)
                + jnp.sum(grad_lifted * lifted, axis=1, keepdims=True)
                - tail_sum
                + jnp.sum(grad_seen * seen, axis=1, keepdims=True)
            )
            grad_last = jnp.sum(tail_sum, axis=0, keepdims=True) + closing * jnp.sum(
                jnp.sum(state * grad_state, axis=1, keepdims=True), axis=0, keepdims=True
            )
            ddecay_ref[head, :, part] = (
                jnp.sum(jnp.where(rows >= cols, grad_cumul, 0.0), axis=0, keepdims=True) + grad_last
            )
            grad_beta = jnp.sum(grad_right * plain, axis=1, keepdims=True) + jnp.sum(
                grad_lower * cross, axis=1, keepdims=True
            )
            dbeta_ref[head, :, part] = to_row(grad_beta, rows, cols)
            grad_state = (
                closing * grad_state
                + mm_tn(jnp.concatenate([lifted, key], axis=0), jnp.concatenate([grad.astype(F32), grad_seen], axis=0))
            )
            grad_queries[chunk], grad_keys[chunk], grad_values[chunk] = grad_query, grad_key, beta * grad_right
        dq, dk, dv = (
            jnp.concatenate(grad_queries, axis=0) * DK**-0.5,
            jnp.concatenate(grad_keys, axis=0),
            jnp.concatenate(grad_values, axis=0),
        )
        dq_all.append(query_scale * (dq - query_unit * jnp.sum(dq * query_unit, axis=-1, keepdims=True)))
        dk_all.append(key_scale * (dk - keys * jnp.sum(dk * keys, axis=-1, keepdims=True)))
        dv_all.append(dv)
    dq = jnp.concatenate(dq_all, axis=1) * silu_slope(q_conv, q_sig)
    dk = jnp.concatenate(dk_all, axis=1) * silu_slope(k_conv, k_sig)
    dv = jnp.concatenate(dv_all, axis=1) * silu_slope(v_conv, v_sig)
    unconvolve(dq, qf_ref[...], held_q, back_q, piece, dq_ref, dqe_ref, dqf_ref)
    unconvolve(dk, kf_ref[...], held_k, back_k, piece, dk_ref, dke_ref, dkf_ref)
    unconvolve(dv, vf_ref[...], held_v, back_v, piece, dv_ref, dve_ref, dvf_ref)


def column_specs(rows, first_axis):
    steps = HEADS // PAIR
    return [
        pl.BlockSpec((rows, PAIR * DK), lambda h, s: (s if first_axis else 0, h)),
        pl.BlockSpec((rows, PAIR * DK), lambda h, s: (s if first_axis else 0, steps + h)),
        pl.BlockSpec((rows, PAIR * DV), lambda h, s: (s if first_axis else 0, steps + h)),
    ]


def gate_spec(piece):
    return pl.BlockSpec((PAIR, 1, piece), lambda h, s: (h, 0, s))


def rows_spec(piece, width):
    return pl.BlockSpec((piece, PAIR * width), lambda h, s: (s, h))


def head_spec(*shape):
    zeros = (0,) * len(shape)
    return pl.BlockSpec((1, PAIR) + shape, lambda h, s: (s, h) + zeros)


def params():
    return pltpu.CompilerParams(vmem_limit_bytes=VMEM, dimension_semantics=("arbitrary", "arbitrary"))


def shape_of(shape, dtype):
    return jax.ShapeDtypeStruct(shape, dtype)


def held(piece, extra):
    return [pltpu.VMEM((piece + extra, PAIR * width), F32) for width in (DK, DK, DV)]


def open_rule(projected, edges, taps, betas, decays, seqs, piece):
    rows, chunks = seqs * piece, piece // CHUNK
    return pl.pallas_call(
        functools.partial(opening_kernel, piece),
        grid=(HEADS // PAIR, seqs),
        in_specs=column_specs(piece, True) + column_specs(8, True) + column_specs(8, False)
        + [gate_spec(piece), gate_spec(piece)],
        out_specs=[rows_spec(piece, DV), rows_spec(piece, DK), head_spec(chunks, DK, WIDE), rows_spec(piece, CHUNK)],
        out_shape=[
            shape_of((rows, HEADS * DV), F32),
            shape_of((rows, HEADS * DK), BF),
            shape_of((seqs, HEADS, chunks, DK, WIDE), BF),
            shape_of((rows, HEADS * CHUNK), BF),
        ],
        scratch_shapes=held(piece, 8),
        compiler_params=params(),
        cost_estimate=pl.CostEstimate(flops=8 * 10**9, bytes_accessed=20 * 2**20, transcendentals=0),
        name="open_rule",
    )(projected, projected, projected, edges, edges, edges, taps, taps, taps, betas, decays)


def finish(local, reading, incoming, outgate, gain, seqs, piece):
    rows = seqs * piece
    return pl.pallas_call(
        finish_kernel,
        grid=(HEADS // PAIR, seqs),
        in_specs=[
            rows_spec(piece, DV), rows_spec(piece, DK), head_spec(DK, DV), rows_spec(piece, DV),
            pl.BlockSpec((8, DV), lambda h, s: (0, 0)),
        ],
        out_specs=[rows_spec(piece, DV), rows_spec(piece, DV)],
        out_shape=[shape_of((rows, HEADS * DV), F32), shape_of((rows, HEADS * DV), BF)],
        compiler_params=params(),
        name="finish_heads",
    )(local, reading, incoming, outgate, gain)


def unfinish(grad, mixed, outgate, gain, reading, seqs, piece):
    rows = seqs * piece
    return pl.pallas_call(
        unfinish_kernel,
        grid=(HEADS // PAIR, seqs),
        in_specs=[
            rows_spec(piece, DV), rows_spec(piece, DV), rows_spec(piece, DV),
            pl.BlockSpec((8, DV), lambda h, s: (0, 0)), rows_spec(piece, DK),
        ],
        out_specs=[rows_spec(piece, DV), rows_spec(piece, DV), head_spec(8, DV), head_spec(DK, DV)],
        out_shape=[
            shape_of((rows, HEADS * DV), BF), shape_of((rows, HEADS * DV), BF),
            shape_of((seqs, HEADS, 8, DV), F32), shape_of((seqs, HEADS, DK, DV), F32),
        ],
        compiler_params=params(),
        name="unfinish_heads",
    )(grad, mixed, outgate, gain, reading)


def close_rule(projected, edges, taps, betas, decays, inverse, states, incoming, grad, leaving, seqs, piece):
    rows, chunks = seqs * piece, piece // CHUNK
    sizes = (HEADS * DK, HEADS * DK, HEADS * DV)
    steps = HEADS // PAIR

    def blocks(height):
        return [pl.BlockSpec((height, PAIR * w), lambda h, s: (s, h)) for w in (DK, DK, DV)]

    return pl.pallas_call(
        functools.partial(closing_kernel, piece),
        grid=(steps, seqs),
        in_specs=column_specs(piece, True) + column_specs(8, True) + column_specs(8, False)
        + [gate_spec(piece), gate_spec(piece), rows_spec(piece, CHUNK), head_spec(chunks, DK, WIDE),
           head_spec(DK, DV), rows_spec(piece, DV), head_spec(DK, DV)],
        out_specs=blocks(piece) + blocks(8)
        + [pl.BlockSpec((1, 8, PAIR * w), lambda h, s: (s, 0, h)) for w in (DK, DK, DV)]
        + [gate_spec(piece), gate_spec(piece)],
        out_shape=[shape_of((rows, w), BF) for w in sizes]
        + [shape_of((seqs * 8, w), F32) for w in sizes]
        + [shape_of((seqs, 8, w), F32) for w in sizes]
        + [shape_of((HEADS, 1, rows), F32)] * 2,
        scratch_shapes=held(piece, 8) + held(piece, 16),
        compiler_params=params(),
        cost_estimate=pl.CostEstimate(flops=16 * 10**9, bytes_accessed=30 * 2**20, transcendentals=0),
        name="close_rule",
    )(projected, projected, projected, edges, edges, edges, taps, taps, taps, betas, decays,
      inverse, states, incoming, grad, leaving)


SEQ = ("y", "x")
ALL = ("z", "c", "y", "x")


def product(left, right):
    return jnp.dot(left, right, preferred_element_type=F32)


def product_left(left, right):
    return lax.dot_general(left, right, (((0,), (0,)), ((), ())), preferred_element_type=F32)


def product_right(left, right):
    return lax.dot_general(left, right, (((1,), (1,)), ((), ())), preferred_element_type=F32)


def inverse_root(value):
    return lax.rsqrt(jnp.mean(value * value, axis=-1, keepdims=True) + EPS)


def norm_back(grad, normed, inverse, gain):
    scaled = grad * gain
    return (
        jnp.sum(grad * normed, axis=0),
        inverse * (scaled - normed * jnp.mean(scaled * normed, axis=-1, keepdims=True)),
    )


def shift(block, distance):
    devices = range(lax.axis_size(SEQ))
    return lax.ppermute(block, SEQ, [(i - distance, i) for i in devices if i - distance in devices])


def take(block, dim, index):
    return lax.dynamic_index_in_dim(block, index, dim, keepdims=False)


def line_sum(parts, axis, dim):
    size, me = lax.axis_size(axis), lax.axis_index(axis)

    def share(index):
        index = jnp.clip(index, 0, size - 1)
        total = take(parts[0], dim, index).astype(F32)
        for part in parts[1:]:
            total = total + take(part, dim, index).astype(F32)
        return total

    from_left = from_right = None
    for step in range(1, size):
        right_going = share(me + size - step)
        left_going = share(me - size + step)
        if from_left is not None:
            right_going = right_going + from_left.astype(F32)
            left_going = left_going + from_right.astype(F32)
        from_left = lax.ppermute(right_going.astype(BF), axis, [(i, i + 1) for i in range(step) if i + 1 < size])
        from_right = lax.ppermute(
            left_going.astype(BF), axis, [(i, i - 1) for i in range(size - step, size) if i > 0]
        )
    return [share(me), from_left, from_right]


def scatter_sum(grad, order):
    sizes = [lax.axis_size(axis) for axis in ALL]
    rows = grad.shape[0] // (sizes[0] * sizes[1] * sizes[2] * sizes[3])
    parts = [grad.reshape(*sizes, rows, grad.shape[1])]
    left = list(ALL)
    for axis in order:
        dim = left.index(axis)
        me, size = lax.axis_index(axis), lax.axis_size(axis)
        if size == 2:
            total_other = sum_of([take(part, dim, 1 - me) for part in parts])
            total_mine = sum_of([take(part, dim, me) for part in parts])
            parts = [total_mine.astype(BF), lax.ppermute(total_other.astype(BF), axis, [(0, 1), (1, 0)])]
        else:
            parts = [part for part in line_sum(parts, axis, dim)]
        left.remove(axis)
    return sum_of(parts)


def sum_of(parts):
    total = parts[0].astype(F32)
    for part in parts[1:]:
        total = total + part.astype(F32)
    return total


def shards(
    tokens, cotangent, gain_mixer, proj_input, conv_filter, proj_gates, proj_outgate, gain_heads,
    proj_output, gain_feed, feed_gate, feed_up, feed_down, decay_log, decay_bias,
):
    seqs, piece = tokens.shape[0], tokens.shape[1]
    rows = seqs * piece
    width = HEADS * DK
    channels = 2 * width + HEADS * DV
    devices = lax.axis_size(ALL)
    own = proj_input.shape[0]

    extras = jnp.concatenate(
        [
            proj_gates,
            conv_filter.reshape(own, -1),
            gain_mixer[:, None],
            gain_feed[:, None],
            jnp.pad(gain_heads, (0, own - gain_heads.shape[0]))[:, None],
        ],
        axis=1,
    )
    extras = jnp.pad(extras, ((0, 0), (0, 128 - extras.shape[1])))
    group = lax.all_gather(jnp.concatenate([proj_input, proj_outgate, extras], axis=1), ALL, axis=0, tiled=True)
    output_matrix = lax.all_gather(proj_output, ALL, axis=0, tiled=True)
    feed_group = lax.all_gather(jnp.concatenate([feed_gate, feed_up], axis=1), ALL, axis=0, tiled=True)
    down_matrix = lax.all_gather(feed_down, ALL, axis=0, tiled=True)
    hidden_units = feed_gate.shape[1]

    input_matrix = group[:, :channels]
    outgate_matrix = group[:, channels : channels + HEADS * DV]
    small = group[:, channels + HEADS * DV :]
    gates_matrix = small[:, : 2 * HEADS]
    bank = small[:, 2 * HEADS : 2 * HEADS + 16].reshape(channels, CONV).astype(F32)
    gain_first = small[:, 2 * HEADS + 16].astype(F32)
    gain_second = small[:, 2 * HEADS + 17].astype(F32)
    heads_gain = small[:, 2 * HEADS + 18].reshape(devices, own)[:, : gain_heads.shape[0]].reshape(1, DV)
    heads_gain = jnp.broadcast_to(heads_gain.astype(F32), (8, DV))
    taps = jnp.pad(bank.T, ((0, 8 - CONV), (0, 0)))

    residual = tokens.astype(F32).reshape(rows, D)
    inverse_one = inverse_root(residual)
    normed_one = residual * inverse_one
    first = (normed_one * gain_first).astype(BF)
    projected = product(first, input_matrix).astype(BF)
    gate_pre = lax.dot_general(gates_matrix, first, (((0,), (1,)), ((), ())), preferred_element_type=F32)
    betas = jax.nn.sigmoid(gate_pre[:HEADS])
    decay_pre = gate_pre[HEADS:] + decay_bias[:, None]
    rates = jnp.exp(decay_log)[:, None]
    decays = -rates * jax.nn.softplus(decay_pre)
    beta_rows, decay_rows = betas.reshape(HEADS, 1, rows), decays.reshape(HEADS, 1, rows)
    edge = shift(projected.reshape(seqs, piece, channels)[:, piece - CONV + 1 :], 1)
    edges = jnp.pad(edge.astype(F32), ((0, 0), (9 - CONV, 0), (0, 0))).reshape(seqs * 8, channels)
    local, reading, states, inverse = open_rule(projected, edges, taps, beta_rows, decay_rows, seqs, piece)
    outgate = product(first, outgate_matrix)

    pieces = lax.axis_size(SEQ)
    carried, transfer = states[:, :, -1, :, :DV], states[:, :, -1, :, DV:]
    incoming = jnp.zeros(carried.shape, BF)
    for hop in range(1, pieces):
        ending = carried.astype(F32) + jnp.einsum(
            "...dk,...ke->...de", transfer, incoming, preferred_element_type=F32
        )
        incoming = incoming + lax.ppermute(ending.astype(BF), SEQ, [(hop - 1, hop)])

    mixed, gated = finish(local, reading, incoming, outgate, heads_gain, seqs, piece)
    middle = residual + product(gated, output_matrix)
    inverse_two = inverse_root(middle)
    normed_two = middle * inverse_two
    second = (normed_two * gain_second).astype(BF)
    gate_matrix, upward_matrix = feed_group[:, :hidden_units], feed_group[:, hidden_units:]
    up_gate = product(second, gate_matrix)
    up_linear = product(second, upward_matrix)
    sigmoid_gate = jax.nn.sigmoid(up_gate)
    silu_gate = up_gate * sigmoid_gate
    hidden = (silu_gate * up_linear).astype(BF)
    layer_out = (middle + product(hidden, down_matrix)).astype(BF)

    grad_branch = cotangent.reshape(rows, D)
    grad_feed_down = product_left(hidden, grad_branch).astype(BF)
    grad_hidden = product_right(grad_branch, down_matrix)
    grad_gate = (grad_hidden * up_linear * (sigmoid_gate + silu_gate * (1.0 - sigmoid_gate))).astype(BF)
    grad_up = (grad_hidden * silu_gate).astype(BF)
    grad_feed_gate = product_left(second, grad_gate).astype(BF)
    grad_feed_up = product_left(second, grad_up).astype(BF)
    sum_feed_down = scatter_sum(grad_feed_down, ("c", "z", "x", "y"))
    sum_feed_gate = scatter_sum(grad_feed_gate, ("c", "x", "y", "z"))
    sum_feed_up = scatter_sum(grad_feed_up, ("c", "y", "x", "z"))
    grad_second = product_right(grad_gate, gate_matrix) + product_right(grad_up, upward_matrix)
    grad_gain_feed, grad_norm_two = norm_back(grad_second, normed_two, inverse_two, gain_second)
    grad_middle = grad_branch.astype(F32) + grad_norm_two
    grad_mixer_out = grad_middle.astype(BF)
    grad_proj_output = product_left(gated, grad_mixer_out).astype(BF)
    sum_proj_output = scatter_sum(grad_proj_output, ("c", "x", "y", "z"))
    grad_gated = product_right(grad_mixer_out, output_matrix)
    grad_mixed, grad_outgate, gain_parts, flow = unfinish(
        grad_gated, mixed, outgate, heads_gain, reading, seqs, piece
    )
    grad_gain_heads = jnp.sum(gain_parts[:, :, 0], axis=(0, 1))
    grad_proj_outgate = product_left(first, grad_outgate).astype(BF)
    sum_proj_outgate = scatter_sum(grad_proj_outgate, ("c", "y", "x", "z"))

    leaving = jnp.zeros(carried.shape, BF)
    for hop in range(pieces - 1, 0, -1):
        starting = flow + jnp.einsum("...ki,...ke->...ie", transfer, leaving, preferred_element_type=F32)
        leaving = leaving + lax.ppermute(starting.astype(BF), SEQ, [(hop, hop - 1)])

    outs = close_rule(
        projected, edges, taps, beta_rows, decay_rows, inverse, states, incoming, grad_mixed, leaving, seqs, piece
    )
    grad_edges = jnp.concatenate(outs[3:6], axis=1).reshape(seqs, 8, channels)[:, 9 - CONV :]
    returned = shift(grad_edges.astype(BF), -1)
    starts = (0, width, 2 * width, channels)
    grad_parts = []
    for part, grad in enumerate(outs[:3]):
        back = returned[:, :, starts[part] : starts[part + 1]]
        grad = grad.reshape(seqs, piece, -1)
        tail = (grad[:, piece - 8 :].astype(F32) + jnp.pad(back.astype(F32), ((0, 0), (9 - CONV, 0), (0, 0)))).astype(BF)
        grad_parts.append(lax.dynamic_update_slice(grad, tail, (0, piece - 8, 0)).reshape(rows, -1))
    bank_grad = jnp.concatenate(outs[6:9], axis=2).sum(axis=0)[:CONV].T
    grad_betas, grad_decays = outs[9].reshape(HEADS, rows), outs[10].reshape(HEADS, rows)
    grad_beta_pre = grad_betas * betas * (1.0 - betas)
    grad_decay_pre = -rates * grad_decays * jax.nn.sigmoid(decay_pre)
    grad_decay_log = jnp.sum(grad_decays * decays, axis=1)
    grad_decay_bias = jnp.sum(grad_decay_pre, axis=1)
    grad_gates = jnp.concatenate([grad_beta_pre, grad_decay_pre], axis=0).astype(BF)

    orders = (("c", "z", "x", "y"), ("c", "x", "y", "z"), ("c", "y", "x", "z"))
    sums = [
        scatter_sum(product_left(first, grad).astype(BF), order) for grad, order in zip(grad_parts, orders)
    ]
    sum_proj_input = jnp.concatenate(sums, axis=1)
    grad_first = (
        product_right(grad_outgate, outgate_matrix)
        + lax.dot_general(grad_gates, gates_matrix, (((0,), (1,)), ((), ())), preferred_element_type=F32)
    )
    for part, grad in enumerate(grad_parts):
        grad_first = grad_first + product_right(grad, input_matrix[:, starts[part] : starts[part + 1]])
    grad_gain_mixer, grad_norm_one = norm_back(grad_first, normed_one, inverse_one, gain_first)
    tokens_grad = (grad_middle + grad_norm_one).reshape(seqs, piece, D)
    grad_proj_gates = lax.dot_general(first, grad_gates, (((0,), (1,)), ((), ())), preferred_element_type=F32)

    pieces_small = (
        grad_gain_mixer, grad_gain_feed, grad_gain_heads, grad_decay_log, grad_decay_bias,
        bank_grad.reshape(-1), grad_proj_gates.reshape(-1),
    )
    packed = jnp.concatenate(pieces_small)
    packed = lax.psum(jnp.pad(packed, (0, -packed.shape[0] % 1024)), ALL)
    me = lax.axis_index(ALL)
    found, place = [], 0
    for block in pieces_small:
        size = block.shape[0]
        if size == HEADS:
            found.append(packed[place : place + size])
        else:
            found.append(lax.dynamic_slice(packed, (place + me * (size // devices),), (size // devices,)))
        place += size
    return (
        layer_out.reshape(seqs, piece, D),
        tokens_grad,
        found[0],
        sum_proj_input,
        found[5].reshape(-1, CONV),
        found[6].reshape(-1, 2 * HEADS),
        sum_proj_outgate,
        found[2],
        sum_proj_output,
        found[1],
        sum_feed_gate,
        sum_feed_up,
        sum_feed_down,
        found[3],
        found[4],
    )


def solution(mesh):
    dp, seq = mesh.shape["dp"], mesh.shape["seq"]
    side = math.isqrt(seq)
    side = side if side * side == seq else 1
    fine = jax.sharding.Mesh(mesh.devices.reshape(dp // 2, 2, seq // side, side), ALL)
    row, vector, split = P(("z", "c"), SEQ, None), P(ALL), P(ALL, None)
    in_specs = (row, row, vector, split, split, split, split, vector, split, vector, split, split, split, P(), P())
    out_specs = (row, row, vector, split, split, split, split, vector, split, vector, split, split, split, P(), P())
    return jax.shard_map(shards, mesh=fine, in_specs=in_specs, out_specs=out_specs, check_vma=False)
```

time: 3110 us -> 962 us (0.31)
  waiting for transfers between devices: 1690 us -> 430 us
  other arithmetic: 463 us -> 52.5 us
  matrix products: 520 us -> 122 us
  blocking collectives: 217 us -> 0 us
  starting transfers between devices: 28.1 us -> 164 us
  Pallas kernels: 0 us -> 122 us
  local copies, waits for them, and re-layouts: 166 us -> 44.2 us
    reduce_scatter x6 -> x0, waiting for transfers between devices: 1490 us -> none  [the longest x1 362 us: shards(): lax.psum_scatter(grad_proj_input, ('dp', 'seq'), scatter_dimension=0, til...]
    dot_general x130 -> x15, matrix products: 401 us -> 52.8 us  [the longest x6 39.1 us: product(): return jnp.dot(left, right, preferred_element_type=F32)]
    another operation x7 -> x3, other arithmetic: 335 us -> 2.37 us  [the longest x4 316 us: span_rule(): jax.scipy.linalg.solve_triangular(system, right, lower=True, unit_diagona...]
    all_gather x6 -> x4, waiting for transfers between devices: 0.05 us -> 191 us  [the longest x1 96.7 us: shards(): lax.all_gather(jnp.concatenate([proj_input, proj_outgate, extras], axis=1...]
    all_gather x2 -> x0, blocking collectives: 138 us -> none  [the longest x1 72.2 us: shards(): lax.all_gather(proj_gates, ('dp', 'seq'), axis=0, tiled=True)]
    ppermute x10 -> x80, starting transfers between devices: 27.2 us -> 164 us  [the longest x24 111 us: line_sum(): lax.ppermute(right_going.astype(BF), axis, [(i, i + 1) for i in range(ste...]
    pallas_call x0 -> x4, Pallas kernels: none -> 122 us  [the longest x1 61.3 us: open_rule(): pl.pallas_call(functools.partial(opening_kernel, piece), grid=(HEADS // P...]
    unnamed x16 -> x5, waiting for transfers between devices: 114 us -> 1.27 us
  transfers between devices with their start and end apart: 24 -> 85, of which waited for: 16 -> 31; matrix products, arithmetic and copies ran while one was open for 22% -> 17% of each run, Pallas kernels for 0% -> 12%
where the time goes in v1:
time: 962 us; the launch traced here: 951 us
  waiting for transfers between devices  430 us (45%)
  starting transfers between devices  164 us (17%)
  matrix products  122 us (13%)
  Pallas kernels  122 us (13%)
  other arithmetic  52.5 us (5%)
  local copies, waits for them, and re-layouts  44.2 us (5%)
  between operations  16.1 us (2%)
    ppermute x24, starting transfers between devices, line_sum(): lax.ppermute(right_going.astype(BF), axis, [(i, i + 1) for i in range(ste...  111 us
    psum x1, waiting for transfers between devices, shards(): packed = lax.psum(jnp.pad(packed, (0, -packed.shape[0] % 1024)), ALL)  103 us
    all_gather x1, waiting for transfers between devices, shards(): lax.all_gather(jnp.concatenate([proj_input, proj_outgate, extras], axis=1...  96.7 us
    ppermute x24, waiting for transfers between devices, scatter_sum(): lax.ppermute(total_other.astype(BF), axis, [(0, 1), (1, 0)])  63.4 us
    all_gather x1, waiting for transfers between devices, shards(): down_matrix = lax.all_gather(feed_down, ALL, axis=0, tiled=True)  62.9 us
    pallas_call x1, Pallas kernels, open_rule(): pl.pallas_call(functools.partial(opening_kernel, piece), grid=(HEADS // P...  61.3 us
    pallas_call x1, Pallas kernels, close_rule(): pl.pallas_call(functools.partial(closing_kernel, piece), grid=(steps, seq...  44.6 us
    dot_general x8, matrix products, product_right(): lax.dot_general(left, right, (((1,), (1,)), ((), ())), preferred_element_...  41.3 us
  transfers between devices with their start and end apart: 85, of which 31 were waited for; matrix products, arithmetic and copies ran while one was open for 17% of the time, Pallas kernels for 12%

profile of v1, /device:TPU:0, one launch (start us, length us, event | category | flops | bytes accessed | tf_op | source)
XLA Modules:
  0.0 950.8 jit_solution(1440745638608087918)
XLA Ops:
  16.7 96.7 %all-gather.5.cloned.1.call-done = bf16[1024,6272]{1,0:T(8,128)(2,1)} async-done(((bf16[32,6272]{1,0:T(8,128)(2,1)}), bf16[1024,6272]{1,0:T(8,128)(2,1)}) %all-gather.5.cloned.1.call-update) | async-done | bytes 12845072 | tf_op jit(solution)/shard_map/all_gather | solution.py:511
  114.9 8.3 fusion.2.q_ref.k_ref.v_ref
  123.2 3.2 collective-permute-start
  132.4 61.3 %open_rule.1 = (f32[512,2048]{1,0:T(8,128)}, bf16[512,1024]{1,0:T(8,128)(2,1)}, bf16[1,8,4,128,384]{4,3,2,1,0:T(8,128)(2,1)}, bf16[512,1024]{1,0:T(8,128)(2,1)}) custom-call(bf16[512,4096]{1,0:T(8,128)(2,1)} %copy-done.30, bf16[512,4096]{1,0:T(8,128)(2,1)} %copy-done.30, bf16[512,4096]{1,0:T(8,128)(2,1)} %copy-done.30, ...), custom_call_target="tpu_custom_call" | custom-call | flops 8000000000 | bytes 20971520 | tf_op jit(solution)/shard_map/open_rule/pallas_call | solution.py:320
  195.0 3.6 collective-permute-start.1
  198.6 15.2 %collective-permute-done.1 = bf16[1,8,128,256]{3,2,1,0:T(8,128)(2,1)S(1)} collective-permute-done((bf16[1,8,128,256]{3,2,1,0:T(8,128)(2,1)S(1)}, bf16[1,8,128,256]{3,2,1,0:T(8,128)(2,1)S(1)}, u32[]{:S(2)}, u32[]{:S(2)}) %collective-permute-start.1) | collective-permute-done | bytes 524320 | tf_op jit(solution)/shard_map/ppermute | solution.py:551
  220.0 6.6 fusion.18.outgate_ref
  228.1 7.3 finish_heads.1
  235.4 6.4 multiply_reduce_fusion.2
  243.1 31.4 %all-gather.9.cloned.1.call-done = bf16[1024,5632]{1,0:T(8,128)(2,1)} async-done(((bf16[32,5632]{1,0:T(8,128)(2,1)}), bf16[1024,5632]{1,0:T(8,128)(2,1)}) %all-gather.9.cloned.1.call-update) | async-done | bytes 11534352 | tf_op jit(solution)/shard_map/all_gather | solution.py:513
  274.5 8.7 fusion.7
  283.2 5.0 fusion.11
  288.3 62.9 %all-gather.11.cloned.1.call-done = bf16[2816,1024]{1,0:T(8,128)(2,1)} async-done(((bf16[88,1024]{1,0:T(8,128)(2,1)}), bf16[2816,1024]{1,0:T(8,128)(2,1)}) %all-gather.11.cloned.1.call-update) | async-done | bytes 5767184 | tf_op jit(solution)/shard_map/all_gather | solution.py:514
  351.2 11.6 %multiply_convert_fusion.1 = (bf16[512,2816]{1,0:T(8,128)(2,1)S(1)}, bf16[512,2816]{1,0:T(8,128)(2,1)}, bf16[512,2816]{1,0:T(8,128)(2,1)}) fusion(f32[512,2816]{1,0:T(8,128)} %fusion.7, f32[512,2816]{1,0:T(8,128)} %fusion.11, bf16[2816,1024]{1,0:T(8,128)(2,1)} %all-gather.11.cloned.1.call-done, bf16[1,512,1024]{2,1,0:T(8,128)(2,1)} %param.16), kind=kOutput, calls=%fused_computation.4 | convolution fusion | flops 2972975104 | bytes 27000832 | tf_op jit(solution)/shard_map/dot_general | solution.py:416
  362.8 5.2 convolution_convert_fusion.2
  368.0 5.2 convolution_convert_fusion.1
  373.3 3.2 fusion.5
  376.5 3.5 multiply_reduce_fusion
  384.5 4.3 fusion.100.grad_ref
  388.8 8.9 unfinish_heads.1
  400.5 4.2 convolution_convert_fusion.4
  415.1 4.1 fusion.61
  421.4 3.5 convolution_convert_fusion
  431.1 5.9 fusion.16
  437.0 16.1 %collective-permute-done.6 = bf16[1,8,128,256]{3,2,1,0:T(8,128)(2,1)S(1)} collective-permute-done((bf16[1,8,128,256]{3,2,1,0:T(8,128)(2,1)S(1)}, bf16[1,8,128,256]{3,2,1,0:T(8,128)(2,1)S(1)}, u32[]{:S(2)}, u32[]{:S(2)}) %collective-permute-start.6) | collective-permute-done | bytes 524320 | tf_op jit(solution)/shard_map/ppermute | solution.py:593
  454.0 44.6 %close_rule.1 = (bf16[512,1024]{1,0:T(8,128)(2,1)}, bf16[512,1024]{1,0:T(8,128)(2,1)}, bf16[512,2048]{1,0:T(8,128)(2,1)}, f32[8,1024]{1,0:T(8,128)}, f32[8,1024]...) custom-call(bf16[512,4096]{1,0:T(8,128)(2,1)} %copy-done.30, ...), custom_call_target="tpu_custom_call" | custom-call | flops 16000000000 | bytes 31457280 | tf_op jit(solution)/shard_map/close_rule/pallas_call | solution.py:382
  517.2 3.3 fusion.36
  520.6 3.0 fusion.38
  524.4 6.5 fusion.34
  549.7 103.0 %all-reduce.10.cloned.1.call-done = f32[35840]{0:T(1024)} async-done(((f32[35840]{0:T(1024)}), f32[35840]{0:T(1024)}) %all-reduce.10.cloned.1.call-update) | async-done | bytes 143376 | tf_op jit(solution)/shard_map/psum | solution.py:635
  657.7 3.3 fusion.41
  669.7 3.6 fusion.27
  673.3 5.5 collective-permute-start.9
  686.8 4.4 collective-permute-start.10
  695.7 4.4 collective-permute-start.72
  702.3 5.3 collective-permute-done.45
  707.6 3.9 collective-permute-start.20
  715.7 4.4 collective-permute-start.21
  724.6 8.9 collective-permute-start.11
  733.6 14.8 %collective-permute-done.37 = bf16[4,32,2048]{2,1,0:T(8,128)(2,1)S(1)} collective-permute-done((bf16[4,32,2048]{2,1,0:T(8,128)(2,1)S(1)}, bf16[4,32,2048]{2,1,0:T(8,128)(2,1)S(1)}, u32[]{:S(2)}, u32[]{:S(2)}) %collective-permute-start.37) | collective-permute-done | bytes 524320 | tf_op jit(solution)/shard_map/ppermute | solution.py:475
  748.4 4.5 collective-permute-start.22
  755.5 3.7 collective-permute-done.25
  762.7 5.2 collective-permute-start.47
  770.4 4.3 collective-permute-start.39
  777.3 4.6 collective-permute-start.48
  784.9 5.0 collective-permute-start.73
  791.6 4.1 collective-permute-done.15
  795.8 5.1 collective-permute-start.40
  801.8 10.3 %collective-permute-done.16 = bf16[32,1024]{1,0:T(8,128)(2,1)S(1)} collective-permute-done((bf16[32,1024]{1,0:T(8,128)(2,1)S(1)}, bf16[32,1024]{1,0:T(8,128)(2,1)S(1)}, u32[]{:S(2)}, u32[]{:S(2)}) %collective-permute-start.16) | collective-permute-done | bytes 65568 | tf_op jit(solution)/shard_map/ppermute | solution.py:475
  813.5 4.6 collective-permute-start.49
  822.5 3.9 collective-permute-done.52
  832.0 3.0 collective-permute-start.74
  835.0 12.2 %collective-permute-done.27 = bf16[4,2,32,2048]{3,2,1,0:T(8,128)(2,1)S(1)} collective-permute-done((bf16[4,2,32,2048]{3,2,1,0:T(8,128)(2,1)S(1)}, bf16[4,2,32,2048]{3,2,1,0:T(8,128)(2,1)S(1)}, u32[]{:S(2)}, u32[]{:S(2)}) %collective-permute-start.27) | collective-permute-done | bytes 1048608 | tf_op jit(solution)/shard_map/ppermute | solution.py:475
  848.4 6.5 collective-permute-done.55
  854.9 4.3 collective-permute-start.56
  864.8 4.6 collective-permute-start.29
  871.9 4.3 collective-permute-start.57
  881.7 4.4 collective-permute-start.30
  890.4 5.7 collective-permute-start.67
  896.9 12.0 %collective-permute-start.31 = (bf16[32,2048]{1,0:T(8,128)(2,1)S(1)}, bf16[32,2048]{1,0:T(8,128)(2,1)S(1)}, u32[]{:S(2)}, u32[]{:S(2)}) collective-permute-start(bf16[32,2048]{1,0:T(8,128)(2,1)S(1)} %get-tuple-element.133), channel_id=1, source_target_pairs={{0,8},{8,16},{16,24},{1,9},{9,17},{17,25},{2,10},{10,18},{18,26},{... | collective-permute-start | bytes 393224 | tf_op jit(solution)/shard_map/ppermute | solution.py:457
  912.0 4.5 collective-permute-done.61
  920.7 8.9 collective-permute-done.77
  931.1 6.4 collective-permute-done.78
  939.2 3.8 collective-permute-done.79
  (388 shorter events, 187.4 us)
Async XLA Ops:
  7.2 106.2 %all-gather.5.cloned.1.call-start = ((), (), s32[]{:S(2)}) async-start(), calls=%async_computation | async-start | bytes 13246464 | tf_op jit(solution)/shard_map/all_gather | solution.py:511
  13.2 222.2 %all-gather.7.cloned.1.call-start = ((), (), s32[]{:S(2)}) async-start(), calls=%async_computation.1 | async-start | bytes 4325376 | tf_op jit(solution)/shard_map/all_gather | solution.py:512
  13.9 260.6 %all-gather.9.cloned.1.call-start = ((), (), s32[]{:S(2)}) async-start(), calls=%async_computation.2 | async-start | bytes 11894784 | tf_op jit(solution)/shard_map/all_gather | solution.py:513
  15.8 335.4 %all-gather.11.cloned.1.call-start = ((), (), s32[]{:S(2)}) async-start(), calls=%async_computation.3 | async-start | bytes 5947392 | tf_op jit(solution)/shard_map/all_gather | solution.py:514
  16.4 636.3 %all-reduce.10.cloned.1.call-start = ((), (), s32[]{:S(2)}) async-start(), calls=%async_computation.4 | async-start | bytes 286720 | tf_op jit(solution)/shard_map/psum | solution.py:635
  123.2 8.5 collective-permute-start
  195.0 18.8 %collective-permute-start.1 = (bf16[1,8,128,256]{3,2,1,0:T(8,128)(2,1)S(1)}, bf16[1,8,128,256]{3,2,1,0:T(8,128)(2,1)S(1)}, u32[]{:S(2)}, u32[]{:S(2)}) collective-permute-start(bf16[1,8,128,256]{3,2,1,0:T(8,128)(2,1)S(1)} %fusion.73), channel_id=1, source_target_pairs={{0,1},{4,5},{8,9},{12,13},{16,17},{20,21},{24,25},{28,29}} | collective-permute-start | bytes 1572872 | tf_op jit(solution)/shard_map/ppermute | solution.py:551
  399.5 19.7 %collective-permute-start.4 = (bf16[1,8,128,256]{3,2,1,0:T(8,128)(2,1)S(1)}, bf16[1,8,128,256]{3,2,1,0:T(8,128)(2,1)S(1)}, u32[]{:S(2)}, u32[]{:S(2)}) collective-permute-start(bf16[1,8,128,256]{3,2,1,0:T(8,128)(2,1)S(1)} %fusion.70), channel_id=1, source_target_pairs={{3,2},{7,6},{11,10},{15,14},{19,18},{23,22},{27,26},{31,30}} | collective-permute-start | bytes 1572872 | tf_op jit(solution)/shard_map/ppermute | solution.py:593
  407.8 138.3 %collective-permute-start.35 = (bf16[4,2,2,32,2048]{4,3,2,0,1:T(8,128)(2,1)}, bf16[4,2,2,32,2048]{4,3,2,0,1:T(8,128)(2,1)}, u32[]{:S(2)}, u32[]{:S(2)}) collective-permute-start(bf16[4,2,2,32,2048]{4,3,2,0,1:T(8,128)(2,1)} %copy_bitcast_fusion.3), channel_id=1, source_target_pairs={{0,4},{4,0},{1,5},{5,1},{2,6},{6,2},{3,7},{7,3},{8,12},{12,8},{9,1... | collective-permute-start | bytes 6291464 | tf_op jit(solution)/shard_map/ppermute | solution.py:475
  409.6 137.0 %collective-permute-start.44 = (bf16[4,2,2,64,1024]{4,3,1,0,2:T(8,128)(2,1)}, bf16[4,2,2,64,1024]{4,3,1,0,2:T(8,128)(2,1)}, u32[]{:S(2)}, u32[]{:S(2)}) collective-permute-start(bf16[4,2,2,64,1024]{4,3,1,0,2:T(8,128)(2,1)} %copy_bitcast_fusion.2), channel_id=1, source_target_pairs={{0,4},{4,0},{1,5},{5,1},{2,6},{6,2},{3,7},{7,3},{8,12},{12,8},{9,1... | collective-permute-start | bytes 6291464 | tf_op jit(solution)/shard_map/ppermute | solution.py:475
  411.7 257.3 %collective-permute-start.53 = (bf16[4,2,2,32,2816]{4,3,1,0,2:T(8,128)(2,1)}, bf16[4,2,2,32,2816]{4,3,1,0,2:T(8,128)(2,1)}, u32[]{:S(2)}, u32[]{:S(2)}) collective-permute-start(bf16[4,2,2,32,2816]{4,3,1,0,2:T(8,128)(2,1)} %copy_bitcast_fusion.1), channel_id=1, source_target_pairs={{0,4},{4,0},{1,5},{5,1},{2,6},{6,2},{3,7},{7,3},{8,12},{12,8},{9,1... | collective-permute-start | bytes 8650760 | tf_op jit(solution)/shard_map/ppermute | solution.py:475
  413.8 259.6 %collective-permute-start.62 = (bf16[4,2,2,32,2816]{4,3,2,0,1:T(8,128)(2,1)}, bf16[4,2,2,32,2816]{4,3,2,0,1:T(8,128)(2,1)}, u32[]{:S(2)}, u32[]{:S(2)}) collective-permute-start(bf16[4,2,2,32,2816]{4,3,2,0,1:T(8,128)(2,1)} %copy_bitcast_fusion), channel_id=1, source_target_pairs={{0,4},{4,0},{1,5},{5,1},{2,6},{6,2},{3,7},{7,3},{8,12},{12,8},{9,1... | collective-permute-start | bytes 8650760 | tf_op jit(solution)/shard_map/ppermute | solution.py:475
  420.7 7.5 collective-permute-start.5
  429.8 23.3 %collective-permute-start.6 = (bf16[1,8,128,256]{3,2,1,0:T(8,128)(2,1)S(1)}, bf16[1,8,128,256]{3,2,1,0:T(8,128)(2,1)S(1)}, u32[]{:S(2)}, u32[]{:S(2)}) collective-permute-start(bf16[1,8,128,256]{3,2,1,0:T(8,128)(2,1)S(1)} %fusion.68), channel_id=1, source_target_pairs={{1,0},{5,4},{9,8},{13,12},{17,16},{21,20},{25,24},{29,28}} | collective-permute-start | bytes 1572872 | tf_op jit(solution)/shard_map/ppermute | solution.py:593
  501.0 13.3 %collective-permute-start.7 = (bf16[1,3,4096]{2,1,0:T(4,128)(2,1)S(1)}, bf16[1,3,4096]{2,1,0:T(4,128)(2,1)S(1)}, u32[]{:S(2)}, u32[]{:S(2)}) collective-permute-start(bf16[1,3,4096]{2,1,0:T(4,128)(2,1)S(1)} %slice.145), channel_id=1, source_target_pairs={{1,0},{2,1},{3,2},{5,4},{6,5},{7,6},{9,8},{10,9},{11,10},{13,12},{... | collective-permute-start | bytes 73736 | tf_op jit(solution)/shard_map/ppermute | solution.py:433
  514.4 167.1 %collective-permute-start.71 = (bf16[4,2,2,88,1024]{4,3,2,1,0:T(8,128)(2,1)}, bf16[4,2,2,88,1024]{4,3,2,1,0:T(8,128)(2,1)S(1)}, u32[]{:S(2)}, u32[]{:S(2)}) collective-permute-start(bf16[4,2,2,88,1024]{4,3,2,1,0:T(8,128)(2,1)} %dynamic-slice_bitcast_fusion), channel_id=1, source_target_pairs={{0,4},{4,0},{1,5},{5,1},{2,6},{6,2},{3,7},{7,3},{8,12},{12,8},{9,1... | collective-permute-start | bytes 8650760 | tf_op jit(solution)/shard_map/ppermute | solution.py:475
  546.1 119.8 %collective-permute-start.17 = (bf16[4,2,2,32,1024]{4,3,1,0,2:T(8,128)(2,1)}, bf16[4,2,2,32,1024]{4,3,1,0,2:T(8,128)(2,1)}, u32[]{:S(2)}, u32[]{:S(2)}) collective-permute-start(bf16[4,2,2,32,1024]{4,3,1,0,2:T(8,128)(2,1)} %copy_bitcast_fusion.5), channel_id=1, source_target_pairs={{0,4},{4,0},{1,5},{5,1},{2,6},{6,2},{3,7},{7,3},{8,12},{12,8},{9,1... | collective-permute-start | bytes 3145736 | tf_op jit(solution)/shard_map/ppermute | solution.py:475
  546.7 116.9 %collective-permute-start.8 = (bf16[4,2,2,32,1024]{4,3,2,1,0:T(8,128)(2,1)}, bf16[4,2,2,32,1024]{4,3,2,1,0:T(8,128)(2,1)}, u32[]{:S(2)}, u32[]{:S(2)}) collective-permute-start(bf16[4,2,2,32,1024]{4,3,2,1,0:T(8,128)(2,1)} %dynamic-slice_bitcast_fusion.1), channel_id=1, source_target_pairs={{0,4},{4,0},{1,5},{5,1},{2,6},{6,2},{3,7},{7,3},{8,12},{12,8},{9,1... | collective-permute-start | bytes 3145736 | tf_op jit(solution)/shard_map/ppermute | solution.py:475
  663.6 97.6 %collective-permute-start.26 = (bf16[4,2,2,32,2048]{4,3,2,0,1:T(8,128)(2,1)}, bf16[4,2,2,32,2048]{4,3,2,0,1:T(8,128)(2,1)S(1)}, u32[]{:S(2)}, u32[]{:S(2)}) collective-permute-start(bf16[4,2,2,32,2048]{4,3,2,0,1:T(8,128)(2,1)} %copy_bitcast_fusion.4), channel_id=1, source_target_pairs={{0,4},{4,0},{1,5},{5,1},{2,6},{6,2},{3,7},{7,3},{8,12},{12,8},{9,1... | collective-permute-start | bytes 6291464 | tf_op jit(solution)/shard_map/ppermute | solution.py:475
  665.9 25.6 %collective-permute-start.36 = (bf16[4,2,32,2048]{3,2,1,0:T(8,128)(2,1)S(1)}, bf16[4,2,32,2048]{3,2,1,0:T(8,128)(2,1)S(1)}, u32[]{:S(2)}, u32[]{:S(2)}) collective-permute-start(bf16[4,2,32,2048]{3,2,1,0:T(8,128)(2,1)S(1)} %get-tuple-element.93), channel_id=1, source_target_pairs={{0,2},{2,0},{1,3},{3,1},{4,6},{6,4},{5,7},{7,5},{8,10},{10,8},{9,1... | collective-permute-start | bytes 3145736 | tf_op jit(solution)/shard_map/ppermute | solution.py:475
  669.0 17.8 %collective-permute-start.18 = (bf16[4,2,32,1024]{3,2,1,0:T(8,128)(2,1)S(1)}, bf16[4,2,32,1024]{3,2,1,0:T(8,128)(2,1)S(1)}, u32[]{:S(2)}, u32[]{:S(2)}) collective-permute-start(bf16[4,2,32,1024]{3,2,1,0:T(8,128)(2,1)S(1)} %get-tuple-element.100), channel_id=1, source_target_pairs={{0,1},{1,0},{2,3},{3,2},{4,5},{5,4},{6,7},{7,6},{8,9},{9,8},{10,11... | collective-permute-start | bytes 1572872 | tf_op jit(solution)/shard_map/ppermute | solution.py:475
  673.3 11.1 %collective-permute-start.9 = (bf16[2,2,32,1024]{3,2,1,0:T(8,128)(2,1)S(1)}, bf16[2,2,32,1024]{3,2,1,0:T(8,128)(2,1)S(1)}, u32[]{:S(2)}, u32[]{:S(2)}) collective-permute-start(bf16[2,2,32,1024]{3,2,1,0:T(8,128)(2,1)S(1)} %fusion.90), channel_id=1, source_target_pairs={{0,8},{1,9},{2,10},{3,11},{4,12},{5,13},{6,14},{7,15}} | collective-permute-start | bytes 786440 | tf_op jit(solution)/shard_map/ppermute | solution.py:457
  681.5 26.1 %collective-permute-start.45 = (bf16[4,2,64,1024]{3,2,1,0:T(8,128)(2,1)S(1)}, bf16[4,2,64,1024]{3,2,1,0:T(8,128)(2,1)S(1)}, u32[]{:S(2)}, u32[]{:S(2)}) collective-permute-start(bf16[4,2,64,1024]{3,2,1,0:T(8,128)(2,1)S(1)} %get-tuple-element.91), channel_id=1, source_target_pairs={{0,1},{1,0},{2,3},{3,2},{4,5},{5,4},{6,7},{7,6},{8,9},{9,8},{10,11... | collective-permute-start | bytes 3145736 | tf_op jit(solution)/shard_map/ppermute | solution.py:475
  684.5 142.7 %collective-permute-start.54 = (bf16[4,2,32,2816]{3,2,1,0:T(8,128)(2,1)S(1)}, bf16[4,2,32,2816]{3,2,1,0:T(8,128)(2,1)S(1)}, u32[]{:S(2)}, u32[]{:S(2)}) collective-permute-start(bf16[4,2,32,2816]{3,2,1,0:T(8,128)(2,1)S(1)} %get-tuple-element.89), channel_id=1, source_target_pairs={{0,1},{1,0},{2,3},{3,2},{4,5},{5,4},{6,7},{7,6},{8,9},{9,8},{10,11... | collective-permute-start | bytes 4325384 | tf_op jit(solution)/shard_map/ppermute | solution.py:475
  686.8 8.9 collective-permute-start.10
  691.5 10.1 %collective-permute-start.19 = (bf16[4,32,1024]{2,1,0:T(8,128)(2,1)S(1)}, bf16[4,32,1024]{2,1,0:T(8,128)(2,1)S(1)}, u32[]{:S(2)}, u32[]{:S(2)}) collective-permute-start(bf16[4,32,1024]{2,1,0:T(8,128)(2,1)S(1)} %get-tuple-element.132), channel_id=1, source_target_pairs={{0,2},{2,0},{1,3},{3,1},{4,6},{6,4},{5,7},{7,5},{8,10},{10,8},{9,1... | collective-permute-start | bytes 786440 | tf_op jit(solution)/shard_map/ppermute | solution.py:475
  695.7 27.6 %collective-permute-start.72 = (bf16[2,2,88,1024]{3,2,1,0:T(8,128)(2,1)S(1)}, bf16[2,2,88,1024]{3,2,1,0:T(8,128)(2,1)S(1)}, u32[]{:S(2)}, u32[]{:S(2)}) collective-permute-start(bf16[2,2,88,1024]{3,2,1,0:T(8,128)(2,1)S(1)} %fusion.56), channel_id=1, source_target_pairs={{0,8},{1,9},{2,10},{3,11},{4,12},{5,13},{6,14},{7,15}} | collective-permute-start | bytes 2162696 | tf_op jit(solution)/shard_map/ppermute | solution.py:457
  701.6 14.1 %collective-permute-start.12 = (bf16[2,2,32,1024]{3,2,1,0:T(8,128)(2,1)S(1)}, bf16[2,2,32,1024]{3,2,1,0:T(8,128)(2,1)S(1)}, u32[]{:S(2)}, u32[]{:S(2)}) collective-permute-start(bf16[2,2,32,1024]{3,2,1,0:T(8,128)(2,1)S(1)} %get-tuple-element.97), channel_id=1, source_target_pairs={{24,16},{25,17},{26,18},{27,19},{28,20},{29,21},{30,22},{31,23}} | collective-permute-start | bytes 786440 | tf_op jit(solution)/shard_map/ppermute | solution.py:458
  721.2 27.2 %collective-permute-start.37 = (bf16[4,32,2048]{2,1,0:T(8,128)(2,1)S(1)}, bf16[4,32,2048]{2,1,0:T(8,128)(2,1)S(1)}, u32[]{:S(2)}, u32[]{:S(2)}) collective-permute-start(bf16[4,32,2048]{2,1,0:T(8,128)(2,1)S(1)} %get-tuple-element.110), channel_id=1, source_target_pairs={{0,1},{1,0},{2,3},{3,2},{4,5},{5,4},{6,7},{7,6},{8,9},{9,8},{10,11... | collective-permute-start | bytes 1572872 | tf_op jit(solution)/shard_map/ppermute | solution.py:475
  722.0 31.1 %collective-permute-start.46 = (bf16[4,64,1024]{2,1,0:T(8,128)(2,1)S(1)}, bf16[4,64,1024]{2,1,0:T(8,128)(2,1)S(1)}, u32[]{:S(2)}, u32[]{:S(2)}) collective-permute-start(bf16[4,64,1024]{2,1,0:T(8,128)(2,1)S(1)} %get-tuple-element.108), channel_id=1, source_target_pairs={{0,2},{2,0},{1,3},{3,1},{4,6},{6,4},{5,7},{7,5},{8,10},{10,8},{9,1... | collective-permute-start | bytes 1572872 | tf_op jit(solution)/shard_map/ppermute | solution.py:475
  724.6 60.3 %collective-permute-start.11 = (bf16[2,2,32,1024]{3,2,1,0:T(8,128)(2,1)S(1)}, bf16[2,2,32,1024]{3,2,1,0:T(8,128)(2,1)S(1)}, u32[]{:S(2)}, u32[]{:S(2)}) collective-permute-start(bf16[2,2,32,1024]{3,2,1,0:T(8,128)(2,1)S(1)} %get-tuple-element.96), channel_id=1, source_target_pairs={{0,8},{8,16},{16,24},{1,9},{9,17},{17,25},{2,10},{10,18},{18,26},{... | collective-permute-start | bytes 786440 | tf_op jit(solution)/shard_map/ppermute | solution.py:457
  754.8 7.8 collective-permute-start.13
  759.2 9.8 %collective-permute-start.38 = (bf16[32,2048]{1,0:T(8,128)(2,1)S(1)}, bf16[32,2048]{1,0:T(8,128)(2,1)S(1)}, u32[]{:S(2)}, u32[]{:S(2)}) collective-permute-start(bf16[32,2048]{1,0:T(8,128)(2,1)S(1)} %get-tuple-element.127), channel_id=1, source_target_pairs={{0,8},{1,9},{2,10},{3,11},{4,12},{5,13},{6,14},{7,15}} | collective-permute-start | bytes 393224 | tf_op jit(solution)/shard_map/ppermute | solution.py:457
  761.2 13.6 %collective-permute-start.41 = (bf16[32,2048]{1,0:T(8,128)(2,1)S(1)}, bf16[32,2048]{1,0:T(8,128)(2,1)S(1)}, u32[]{:S(2)}, u32[]{:S(2)}) collective-permute-start(bf16[32,2048]{1,0:T(8,128)(2,1)S(1)} %get-tuple-element.128), channel_id=1, source_target_pairs={{24,16},{25,17},{26,18},{27,19},{28,20},{29,21},{30,22},{31,23}} | collective-permute-start | bytes 393224 | tf_op jit(solution)/shard_map/ppermute | solution.py:458
  762.7 7.7 collective-permute-start.47
  769.0 13.0 %collective-permute-start.50 = (bf16[64,1024]{1,0:T(8,128)(2,1)S(1)}, bf16[64,1024]{1,0:T(8,128)(2,1)S(1)}, u32[]{:S(2)}, u32[]{:S(2)}) collective-permute-start(bf16[64,1024]{1,0:T(8,128)(2,1)S(1)} %get-tuple-element.124), channel_id=1, source_target_pairs={{24,16},{25,17},{26,18},{27,19},{28,20},{29,21},{30,22},{31,23}} | collective-permute-start | bytes 393224 | tf_op jit(solution)/shard_map/ppermute | solution.py:458
  774.8 15.1 %collective-permute-start.14 = (bf16[2,2,32,1024]{3,2,1,0:T(8,128)(2,1)S(1)}, bf16[2,2,32,1024]{3,2,1,0:T(8,128)(2,1)S(1)}, u32[]{:S(2)}, u32[]{:S(2)}) collective-permute-start(bf16[2,2,32,1024]{3,2,1,0:T(8,128)(2,1)S(1)} %fusion.89), channel_id=1, source_target_pairs={{8,0},{16,8},{24,16},{9,1},{17,9},{25,17},{10,2},{18,10},{26,18},{... | collective-permute-start | bytes 786440 | tf_op jit(solution)/shard_map/ppermute | solution.py:458
  782.0 46.4 %collective-permute-start.63 = (bf16[4,2,32,2816]{3,2,1,0:T(8,128)(2,1)S(1)}, bf16[4,2,32,2816]{3,2,1,0:T(8,128)(2,1)S(1)}, u32[]{:S(2)}, u32[]{:S(2)}) collective-permute-start(bf16[4,2,32,2816]{3,2,1,0:T(8,128)(2,1)S(1)} %get-tuple-element.87), channel_id=1, source_target_pairs={{0,2},{2,0},{1,3},{3,1},{4,6},{6,4},{5,7},{7,5},{8,10},{10,8},{9,1... | collective-permute-start | bytes 4325384 | tf_op jit(solution)/shard_map/ppermute | solution.py:475
  784.9 45.2 %collective-permute-start.73 = (bf16[2,2,88,1024]{3,2,1,0:T(8,128)(2,1)S(1)}, bf16[2,2,88,1024]{3,2,1,0:T(8,128)(2,1)S(1)}, u32[]{:S(2)}, u32[]{:S(2)}) collective-permute-start(bf16[2,2,88,1024]{3,2,1,0:T(8,128)(2,1)S(1)} %fusion.58), channel_id=1, source_target_pairs={{0,8},{8,16},{1,9},{9,17},{2,10},{10,18},{3,11},{11,19},{4,12},{12... | collective-permute-start | bytes 2162696 | tf_op jit(solution)/shard_map/ppermute | solution.py:457
  789.9 11.0 %collective-permute-start.51 = (bf16[64,1024]{1,0:T(8,128)(2,1)S(1)}, bf16[64,1024]{1,0:T(8,128)(2,1)S(1)}, u32[]{:S(2)}, u32[]{:S(2)}) collective-permute-start(bf16[64,1024]{1,0:T(8,128)(2,1)S(1)} %get-tuple-element.122), channel_id=1, source_target_pairs={{16,8},{24,16},{17,9},{25,17},{18,10},{26,18},{19,11},{27,19},{20,... | collective-permute-start | bytes 393224 | tf_op jit(solution)/shard_map/ppermute | solution.py:458
  795.8 17.7 %collective-permute-start.40 = (bf16[32,2048]{1,0:T(8,128)(2,1)S(1)}, bf16[32,2048]{1,0:T(8,128)(2,1)S(1)}, u32[]{:S(2)}, u32[]{:S(2)}) collective-permute-start(bf16[32,2048]{1,0:T(8,128)(2,1)S(1)} %get-tuple-element.125), channel_id=1, source_target_pairs={{0,8},{8,16},{16,24},{1,9},{9,17},{17,25},{2,10},{10,18},{18,26},{... | collective-permute-start | bytes 393224 | tf_op jit(solution)/shard_map/ppermute | solution.py:457
  801.0 11.2 %collective-permute-start.16 = (bf16[32,1024]{1,0:T(8,128)(2,1)S(1)}, bf16[32,1024]{1,0:T(8,128)(2,1)S(1)}, u32[]{:S(2)}, u32[]{:S(2)}) collective-permute-start(bf16[32,1024]{1,0:T(8,128)(2,1)S(1)} %fusion.243), channel_id=1, source_target_pairs={{0,2},{2,0},{1,3},{3,1},{4,6},{6,4},{5,7},{7,5},{8,10},{10,8},{9,1... | collective-permute-start | bytes 196616 | tf_op jit(solution)/shard_map/ppermute | solution.py:475
  813.5 8.1 collective-permute-start.49
  821.6 25.5 %collective-permute-start.27 = (bf16[4,2,32,2048]{3,2,1,0:T(8,128)(2,1)S(1)}, bf16[4,2,32,2048]{3,2,1,0:T(8,128)(2,1)S(1)}, u32[]{:S(2)}, u32[]{:S(2)}) collective-permute-start(bf16[4,2,32,2048]{3,2,1,0:T(8,128)(2,1)S(1)} %get-tuple-element.95), channel_id=1, source_target_pairs={{0,2},{2,0},{1,3},{3,1},{4,6},{6,4},{5,7},{7,5},{8,10},{10,8},{9,1... | collective-permute-start | bytes 3145736 | tf_op jit(solution)/shard_map/ppermute | solution.py:475
  827.5 27.3 %collective-permute-start.55 = (bf16[4,32,2816]{2,1,0:T(8,128)(2,1)S(1)}, bf16[4,32,2816]{2,1,0:T(8,128)(2,1)S(1)}, u32[]{:S(2)}, u32[]{:S(2)}) collective-permute-start(bf16[4,32,2816]{2,1,0:T(8,128)(2,1)S(1)} %get-tuple-element.106), channel_id=1, source_target_pairs={{0,2},{2,0},{1,3},{3,1},{4,6},{6,4},{5,7},{7,5},{8,10},{10,8},{9,1... | collective-permute-start | bytes 2162696 | tf_op jit(solution)/shard_map/ppermute | solution.py:475
  828.8 30.4 %collective-permute-start.64 = (bf16[4,32,2816]{2,1,0:T(8,128)(2,1)S(1)}, bf16[4,32,2816]{2,1,0:T(8,128)(2,1)S(1)}, u32[]{:S(2)}, u32[]{:S(2)}) collective-permute-start(bf16[4,32,2816]{2,1,0:T(8,128)(2,1)S(1)} %get-tuple-element.104), channel_id=1, source_target_pairs={{0,1},{1,0},{2,3},{3,2},{4,5},{5,4},{6,7},{7,6},{8,9},{9,8},{10,11... | collective-permute-start | bytes 2162696 | tf_op jit(solution)/shard_map/ppermute | solution.py:475
  831.3 28.8 %collective-permute-start.75 = (bf16[2,2,88,1024]{3,2,1,0:T(8,128)(2,1)S(1)}, bf16[2,2,88,1024]{3,2,1,0:T(8,128)(2,1)S(1)}, u32[]{:S(2)}, u32[]{:S(2)}) collective-permute-start(bf16[2,2,88,1024]{3,2,1,0:T(8,128)(2,1)S(1)} %get-tuple-element.84), channel_id=1, source_target_pairs={{24,16},{25,17},{26,18},{27,19},{28,20},{29,21},{30,22},{31,23}} | collective-permute-start | bytes 2162696 | tf_op jit(solution)/shard_map/ppermute | solution.py:458
  832.0 88.7 %collective-permute-start.74 = (bf16[2,2,88,1024]{3,2,1,0:T(8,128)(2,1)S(1)}, bf16[2,2,88,1024]{3,2,1,0:T(8,128)(2,1)S(1)}, u32[]{:S(2)}, u32[]{:S(2)}) collective-permute-start(bf16[2,2,88,1024]{3,2,1,0:T(8,128)(2,1)S(1)} %get-tuple-element.83), channel_id=1, source_target_pairs={{0,8},{8,16},{16,24},{1,9},{9,17},{17,25},{2,10},{10,18},{18,26},{... | collective-permute-start | bytes 2162696 | tf_op jit(solution)/shard_map/ppermute | solution.py:457
  847.5 16.1 %collective-permute-start.28 = (bf16[4,32,2048]{2,1,0:T(8,128)(2,1)S(1)}, bf16[4,32,2048]{2,1,0:T(8,128)(2,1)S(1)}, u32[]{:S(2)}, u32[]{:S(2)}) collective-permute-start(bf16[4,32,2048]{2,1,0:T(8,128)(2,1)S(1)} %get-tuple-element.112), channel_id=1, source_target_pairs={{0,1},{1,0},{2,3},{3,2},{4,5},{5,4},{6,7},{7,6},{8,9},{9,8},{10,11... | collective-permute-start | bytes 1572872 | tf_op jit(solution)/shard_map/ppermute | solution.py:475
  854.9 7.9 collective-permute-start.56
  859.2 17.1 %collective-permute-start.59 = (bf16[32,2816]{1,0:T(8,128)(2,1)S(1)}, bf16[32,2816]{1,0:T(8,128)(2,1)S(1)}, u32[]{:S(2)}, u32[]{:S(2)}) collective-permute-start(bf16[32,2816]{1,0:T(8,128)(2,1)S(1)} %get-tuple-element.120), channel_id=1, source_target_pairs={{24,16},{25,17},{26,18},{27,19},{28,20},{29,21},{30,22},{31,23}} | collective-permute-start | bytes 540680 | tf_op jit(solution)/shard_map/ppermute | solution.py:458
  862.8 18.9 %collective-permute-start.68 = (bf16[32,2816]{1,0:T(8,128)(2,1)S(1)}, bf16[32,2816]{1,0:T(8,128)(2,1)S(1)}, u32[]{:S(2)}, u32[]{:S(2)}) collective-permute-start(bf16[32,2816]{1,0:T(8,128)(2,1)S(1)} %get-tuple-element.116), channel_id=1, source_target_pairs={{24,16},{25,17},{26,18},{27,19},{28,20},{29,21},{30,22},{31,23}} | collective-permute-start | bytes 540680 | tf_op jit(solution)/shard_map/ppermute | solution.py:458
  863.6 45.3 %collective-permute-start.76 = (bf16[2,2,88,1024]{3,2,1,0:T(8,128)(2,1)S(1)}, bf16[2,2,88,1024]{3,2,1,0:T(8,128)(2,1)S(1)}, u32[]{:S(2)}, u32[]{:S(2)}) collective-permute-start(bf16[2,2,88,1024]{3,2,1,0:T(8,128)(2,1)S(1)} %fusion.53), channel_id=1, source_target_pairs={{16,8},{24,16},{17,9},{25,17},{18,10},{26,18},{19,11},{27,19},{20,... | collective-permute-start | bytes 2162696 | tf_op jit(solution)/shard_map/ppermute | solution.py:458
  871.9 9.0 collective-permute-start.57
  876.3 9.8 %collective-permute-start.66 = (bf16[32,2816]{1,0:T(8,128)(2,1)S(1)}, bf16[32,2816]{1,0:T(8,128)(2,1)S(1)}, u32[]{:S(2)}, u32[]{:S(2)}) collective-permute-start(bf16[32,2816]{1,0:T(8,128)(2,1)S(1)} %fusion.116), channel_id=1, source_target_pairs={{0,8},{8,16},{1,9},{9,17},{2,10},{10,18},{3,11},{11,19},{4,12},{12... | collective-permute-start | bytes 540680 | tf_op jit(solution)/shard_map/ppermute | solution.py:457
  881.7 7.8 collective-permute-start.30
  887.0 23.7 %collective-permute-start.58 = (bf16[32,2816]{1,0:T(8,128)(2,1)S(1)}, bf16[32,2816]{1,0:T(8,128)(2,1)S(1)}, u32[]{:S(2)}, u32[]{:S(2)}) collective-permute-start(bf16[32,2816]{1,0:T(8,128)(2,1)S(1)} %get-tuple-element.117), channel_id=1, source_target_pairs={{0,8},{8,16},{16,24},{1,9},{9,17},{17,25},{2,10},{10,18},{18,26},{... | collective-permute-start | bytes 540680 | tf_op jit(solution)/shard_map/ppermute | solution.py:457
  890.4 28.2 %collective-permute-start.67 = (bf16[32,2816]{1,0:T(8,128)(2,1)S(1)}, bf16[32,2816]{1,0:T(8,128)(2,1)S(1)}, u32[]{:S(2)}, u32[]{:S(2)}) collective-permute-start(bf16[32,2816]{1,0:T(8,128)(2,1)S(1)} %get-tuple-element.113), channel_id=1, source_target_pairs={{0,8},{8,16},{16,24},{1,9},{9,17},{17,25},{2,10},{10,18},{18,26},{... | collective-permute-start | bytes 540680 | tf_op jit(solution)/shard_map/ppermute | solution.py:457
  896.9 33.9 %collective-permute-start.31 = (bf16[32,2048]{1,0:T(8,128)(2,1)S(1)}, bf16[32,2048]{1,0:T(8,128)(2,1)S(1)}, u32[]{:S(2)}, u32[]{:S(2)}) collective-permute-start(bf16[32,2048]{1,0:T(8,128)(2,1)S(1)} %get-tuple-element.133), channel_id=1, source_target_pairs={{0,8},{8,16},{16,24},{1,9},{9,17},{17,25},{2,10},{10,18},{18,26},{... | collective-permute-start | bytes 393224 | tf_op jit(solution)/shard_map/ppermute | solution.py:457
  909.0 7.5 collective-permute-start.61
  910.7 9.2 collective-permute-start.70
  916.4 13.2 %collective-permute-start.77 = (bf16[2,2,88,1024]{3,2,1,0:T(8,128)(2,1)S(1)}, bf16[2,2,88,1024]{3,2,1,0:T(8,128)(2,1)S(1)}, u32[]{:S(2)}, u32[]{:S(2)}) collective-permute-start(bf16[2,2,88,1024]{3,2,1,0:T(8,128)(2,1)S(1)} %fusion.55), channel_id=1, source_target_pairs={{8,0},{16,8},{24,16},{9,1},{17,9},{25,17},{10,2},{18,10},{26,18},{... | collective-permute-start | bytes 2162696 | tf_op jit(solution)/shard_map/ppermute | solution.py:458
  918.5 12.5 %collective-permute-start.34 = (bf16[32,2048]{1,0:T(8,128)(2,1)S(1)}, bf16[32,2048]{1,0:T(8,128)(2,1)S(1)}, u32[]{:S(2)}, u32[]{:S(2)}) collective-permute-start(bf16[32,2048]{1,0:T(8,128)(2,1)S(1)} %fusion.181), channel_id=1, source_target_pairs={{8,0},{16,8},{24,16},{9,1},{17,9},{25,17},{10,2},{18,10},{26,18},{... | collective-permute-start | bytes 393224 | tf_op jit(solution)/shard_map/ppermute | solution.py:458
  929.9 7.5 collective-permute-start.78
  (73 other events, 450.7 us)
Sparse Core Ops, SparseCore 0:
  13.3 100.0 all-gather.4
  116.3 60.9 all-gather.6
  180.7 93.7 all-gather.8
  277.3 73.8 all-gather.10
  531.8 120.8 all-reduce.9

commit v2 on v1

--- a/solution.py
+++ b/solution.py
@@ -21,10 +21,25 @@
 F32 = jnp.float32
 
 
+def dot(left, right, over):
+    return lax.dot_general(left, right, (((over[0],), (over[1],)), ((), ())), preferred_element_type=F32)
+
+
+def split(value):
+    if value.dtype == BF:
+        return value, None
+    high = value.astype(BF)
+    return high, (value - high.astype(F32)).astype(BF)
+
+
 def mm(left, right, over=(1, 0)):
-    return lax.dot_general(
-        left.astype(BF), right.astype(BF), (((over[0],), (over[1],)), ((), ())), preferred_element_type=F32
-    )
+    (left, left_low), (right, right_low) = split(left), split(right)
+    total = dot(left, right, over)
+    if left_low is not None:
+        total = total + dot(left_low, right, over)
+    if right_low is not None:
+        total = total + dot(left, right_low, over)
+    return total
 
 
 def mm_nt(left, right):
@@ -60,18 +75,20 @@
     return beta, strict, causal, jnp.exp(cumul), jnp.exp(last - cumul), jnp.exp(last)
 
 
-def unit_lower_inverse(lower, rows, cols):
-    def level(width):
+def unit_lower_inverses(lowers, rows, cols):
+    def level(lower, width):
         shift = width.bit_length() - 1
         row_block, col_block = lax.shift_right_logical(rows, shift), lax.shift_right_logical(cols, shift)
         return jnp.where((row_block == col_block + 1) & ((col_block & 1) == 0), lower, 0.0)
 
-    inverse = jnp.where(rows == cols, 1.0, 0.0) - level(1)
+    inverses = [jnp.where(rows == cols, 1.0, 0.0) - level(lower, 1) for lower in lowers]
     width = 2
     while width < CHUNK:
-        inverse = inverse - mm(mm(inverse, level(width)), inverse)
+        steps = [mm(inverse, level(lower, width)) for inverse, lower in zip(inverses, lowers)]
+        steps = [mm(step, inverse) for inverse, step in zip(inverses, steps)]
+        inverses = [inverse - step for inverse, step in zip(inverses, steps)]
         width *= 2
-    return inverse
+    return inverses
 
 
 def convolve(x, edge, taps, held, piece):
@@ -99,31 +116,44 @@
     q_act = q_conv * jax.nn.sigmoid(q_conv)
     k_act = k_conv * jax.nn.sigmoid(k_conv)
     v_act = v_conv * jax.nn.sigmoid(v_conv)
+    chunks = piece // CHUNK
+    parts = [slice(chunk * CHUNK, (chunk + 1) * CHUNK) for chunk in range(chunks)]
+    terms = {}
     for head in range(PAIR):
         queries = units(q_act[:, head * DK : (head + 1) * DK])[0] * DK**-0.5
         keys = units(k_act[:, head * DK : (head + 1) * DK])[0]
-        values = v_act[:, head * DV : (head + 1) * DV]
-        state = jnp.concatenate(
-            [jnp.zeros((DK, DV), F32), jnp.where(rows == cols, 1.0, 0.0)], axis=1
-        )
-        for chunk in range(piece // CHUNK):
-            part = slice(chunk * CHUNK, (chunk + 1) * CHUNK)
-            query, key, value = queries[part], keys[part], values[part]
+        for chunk, part in enumerate(parts):
+            query, key = queries[part], keys[part]
             beta, strict, causal, grow, fade, closing = fades(
                 decay_ref[head, :, part], beta_ref[head, :, part], rows, cols
             )
             both = mm_nt(jnp.concatenate([key, query], axis=0), key)
-            inverse = unit_lower_inverse(beta * both[:CHUNK] * strict, rows, cols)
-            scores = both[CHUNK:] * causal
-            inverse_ref[part, head * CHUNK : (head + 1) * CHUNK] = inverse.astype(BF)
-            seen = mm(jnp.concatenate([key * grow, query * grow], axis=0), state)
-            wide = jnp.concatenate([value, jnp.zeros((CHUNK, DK), F32)], axis=1)
-            fresh = mm(inverse, beta * (wide - seen[:CHUNK]))
+            value = beta * v_act[part, head * DV : (head + 1) * DV]
+            terms[head, chunk] = (
+                beta * both[:CHUNK] * strict,
+                both[CHUNK:] * causal,
+                jnp.concatenate([key * (beta * grow), query * grow], axis=0),
+                key * fade,
+                jnp.concatenate([value, jnp.zeros((CHUNK, DK), F32)], axis=1),
+                closing,
+            )
+    inverses = unit_lower_inverses([term[0] for term in terms.values()], rows, cols)
+    inverses = dict(zip(terms, inverses))
+    opening = jnp.concatenate([jnp.zeros((DK, DV), F32), jnp.where(rows == cols, 1.0, 0.0)], axis=1)
+    held_states = [opening] * PAIR
+    for chunk, part in enumerate(parts):
+        for head in range(PAIR):
+            _, scores, looking, tail, value, closing = terms[head, chunk]
+            inverse, state = inverses[head, chunk], held_states[head]
+            inverse_ref[part, head * CHUNK : (head + 1) * CHUNK] = inverse
+            seen = mm(looking, state)
+            fresh = mm(inverse, value - seen[:CHUNK])
             result = seen[CHUNK:] + mm(scores, fresh)
-            state = closing * state + mm_tn(key * fade, fresh)
+            state = closing * state + mm_tn(tail, fresh)
+            held_states[head] = state
             local_ref[part, head * DV : (head + 1) * DV] = result[:, :DV]
-            reading_ref[part, head * DK : (head + 1) * DK] = result[:, DV:].astype(BF)
-            states_ref[0, head, chunk] = state.astype(BF)
+            reading_ref[part, head * DK : (head + 1) * DK] = result[:, DV:]
+            states_ref[0, head, chunk] = state
 
 
 def finish_kernel(local_ref, reading_ref, incoming_ref, outgate_ref, gain_ref, mixed_ref, gated_ref):
@@ -154,7 +184,7 @@
         grad_outgate_ref[:, wide] = (along * gain * (sigmoid + gate * (1.0 - sigmoid))).astype(BF)
         scaled = grad * gain * gate
         grad_mixed = inverse * (scaled - normed * jnp.mean(scaled * normed, axis=-1, keepdims=True))
-        grad_mixed_ref[:, wide] = grad_mixed.astype(BF)
+        grad_mixed_ref[:, wide] = grad_mixed
         flow_ref[0, head] = mm_tn(reading_ref[:, head * DK : (head + 1) * DK], grad_mixed)
 
 
@@ -190,89 +220,108 @@
     v_conv = convolve(v_ref[...], ve_ref[...], vf_ref[...], held_v, piece)
     q_sig, k_sig, v_sig = jax.nn.sigmoid(q_conv), jax.nn.sigmoid(k_conv), jax.nn.sigmoid(v_conv)
     q_act, k_act, v_act = q_conv * q_sig, k_conv * k_sig, v_conv * v_sig
+    chunks = piece // CHUNK
+    parts = [slice(chunk * CHUNK, (chunk + 1) * CHUNK) for chunk in range(chunks)]
+    narrows = [slice(head * DK, (head + 1) * DK) for head in range(PAIR)]
+    wides = [slice(head * DV, (head + 1) * DV) for head in range(PAIR)]
+    places = [(head, chunk) for chunk in reversed(range(chunks)) for head in range(PAIR)]
+    unit_parts = [units(q_act[:, narrow]) + units(k_act[:, narrow]) for narrow in narrows]
+    terms = {}
+    for head, chunk in places:
+        part = parts[chunk]
+        query, key = unit_parts[head][0][part] * DK**-0.5, unit_parts[head][2][part]
+        beta, strict, causal, grow, fade, closing = fades(
+            decay_ref[head, :, part], beta_ref[head, :, part], rows, cols
+        )
+        both = mm_nt(jnp.concatenate([key, query], axis=0), key)
+        scores = both[CHUNK:] * causal
+        incoming = incoming_ref[0, head]
+        if chunk == 0:
+            state = incoming.astype(F32)
+        else:
+            before = states_ref[0, head, chunk - 1]
+            state = before[:, :DV] + mm(before[:, DV:], incoming)
+        seen = mm(key, state)
+        grad = grad_ref[part, wides[head]]
+        terms[head, chunk] = dict(
+            query=query, key=key, beta=beta, strict=strict, causal=causal, grow=grow, fade=fade, closing=closing,
+            cross=both[:CHUNK] * strict, scores=scores, state=state, seen=seen, grad=grad,
+            plain=v_act[part, wides[head]] - grow * seen,
+            inverse=inverse_ref[part, head * CHUNK : (head + 1) * CHUNK],
+            grad_fresh=mm_tn(scores, grad), grad_state=mm_tn(query * grow, grad),
+        )
+    for place in places:
+        term = terms[place]
+        term["fresh"] = mm(term["inverse"], term["beta"] * term["plain"])
+    grad_states = [leaving_ref[0, head].astype(F32) for head in range(PAIR)]
+    for place in places:
+        term, grad_state = terms[place], grad_states[place[0]]
+        key = term["key"]
+        grad_fresh = term["grad_fresh"] + mm(key * term["fade"], grad_state)
+        grad_right = mm_tn(term["inverse"], grad_fresh)
+        term["grad_right"], term["grad_seen"] = grad_right, -(term["beta"] * term["grow"]) * grad_right
+        term["grad_after"] = grad_state
+        grad_states[place[0]] = term["closing"] * grad_state + term["grad_state"] + mm_tn(key, term["grad_seen"])
+    for head, chunk in places:
+        term, part = terms[head, chunk], parts[chunk]
+        query, key, beta, strict, causal, grow, fade, closing, cross, scores, state, seen, grad = [
+            term[name]
+            for name in (
+                "query", "key", "beta", "strict", "causal", "grow", "fade", "closing", "cross", "scores", "state",
+                "seen", "grad",
+            )
+        ]
+        grad_right, grad_seen, grad_state, fresh = [
+            term[name] for name in ("grad_right", "grad_seen", "grad_after", "fresh")
+        ]
+        pair = mm_nt(jnp.concatenate([grad, grad_right], axis=0), fresh)
+        grad_scores = jnp.where(rows >= cols, pair[:CHUNK], 0.0)
+        grad_lower = jnp.where(rows > cols, -pair[CHUNK:], 0.0)
+        pair = mm_nt(jnp.concatenate([grad, grad_seen], axis=0), state)
+        grad_lifted, grad_key = pair[:CHUNK], pair[CHUNK:]
+        grad_tail = mm_nt(fresh, grad_state)
+        grad_cross = grad_lower * strict * beta
+        grad_both = grad_scores * causal
+        term["grad_query"] = mm(grad_both, key) + grad_lifted * grow
+        term["grad_key"] = (
+            grad_key
+            + mm(grad_cross, key)
+            + mm_tn(jnp.concatenate([grad_cross, grad_both], axis=0), jnp.concatenate([key, query], axis=0))
+            + grad_tail * fade
+        )
+        spread = grad_lower * beta * cross + grad_scores * scores
+        tail_sum = jnp.sum(grad_tail * (key * fade), axis=1, keepdims=True)
+        grad_cumul = (
+            jnp.sum(spread, axis=1, keepdims=True)
+            - to_column(jnp.sum(spread, axis=0, keepdims=True), rows, cols)
+            + jnp.sum(grad_lifted * (query * grow) - grad_tail * (key * fade), axis=1, keepdims=True)
+            + jnp.sum(grad_seen * seen, axis=1, keepdims=True)
+        )
+        grad_last = jnp.sum(tail_sum, axis=0, keepdims=True) + closing * jnp.sum(
+            jnp.sum(state * grad_state, axis=0, keepdims=True), axis=1, keepdims=True
+        )
+        ddecay_ref[head, :, part] = (
+            jnp.sum(jnp.where(rows >= cols, grad_cumul, 0.0), axis=0, keepdims=True) + grad_last
+        )
+        grad_beta = jnp.sum(grad_right * term["plain"], axis=1, keepdims=True) + jnp.sum(
+            grad_lower * cross, axis=1, keepdims=True
+        )
+        dbeta_ref[head, :, part] = to_row(grad_beta, rows, cols)
     dq_all, dk_all, dv_all = [], [], []
-    chunks = piece // CHUNK
     for head in range(PAIR):
-        narrow, wide = slice(head * DK, (head + 1) * DK), slice(head * DV, (head + 1) * DV)
-        query_unit, query_scale = units(q_act[:, narrow])
-        queries = query_unit * DK**-0.5
-        keys, key_scale = units(k_act[:, narrow])
-        values = v_act[:, wide]
-        incoming = incoming_ref[0, head]
-        grad_state = leaving_ref[0, head].astype(F32)
-        grad_queries, grad_keys, grad_values = [None] * chunks, [None] * chunks, [None] * chunks
-        for chunk in reversed(range(chunks)):
-            part = slice(chunk * CHUNK, (chunk + 1) * CHUNK)
-            query, key, value = queries[part], keys[part], values[part]
-            beta, strict, causal, grow, fade, closing = fades(
-                decay_ref[head, :, part], beta_ref[head, :, part], rows, cols
-            )
-            both = mm_nt(jnp.concatenate([key, query], axis=0), key)
-            cross = both[:CHUNK] * strict
-            lower = beta * cross
-            scores = both[CHUNK:] * causal
-            inverse = inverse_ref[part, head * CHUNK : (head + 1) * CHUNK]
-            if chunk == 0:
-                state = incoming.astype(F32)
-            else:
-                before = states_ref[0, head, chunk - 1]
-                state = before[:, :DV].astype(F32) + mm(before[:, DV:], incoming)
-            grad = grad_ref[part, wide]
-            seen = mm(key, state)
-            plain = value - grow * seen
-            fresh = mm(inverse, beta * plain)
-            tail = key * fade
-            lifted = query * grow
-            grad_fresh = mm_tn(scores, grad) + mm(tail, grad_state)
-            grad_right = mm_tn(inverse, grad_fresh)
-            grad_seen = -(beta * grow) * grad_right
-            pair = mm_nt(jnp.concatenate([grad.astype(F32), grad_right], axis=0), fresh)
-            grad_scores = jnp.where(rows >= cols, pair[:CHUNK], 0.0)
-            grad_lower = jnp.where(rows > cols, -pair[CHUNK:], 0.0)
-            pair = mm_nt(jnp.concatenate([grad.astype(F32), grad_seen], axis=0), state)
-            grad_lifted, grad_key = pair[:CHUNK], pair[CHUNK:]
-            grad_tail = mm_nt(fresh, grad_state)
-            grad_cross = grad_lower * strict * beta
-            grad_both = grad_scores * causal
-            grad_query = mm(grad_both, key) + grad_lifted * grow
-            grad_key = (
-                grad_key
-                + mm(grad_cross, key)
-                + mm_tn(jnp.concatenate([grad_cross, grad_both], axis=0), jnp.concatenate([key, query], axis=0))
-                + grad_tail * fade
-            )
-            spread = grad_lower * lower + grad_scores * scores
-            tail_sum = jnp.sum(grad_tail * tail, axis=1, keepdims=True)
-            grad_cumul = (
-                jnp.sum(spread, axis=1, keepdims=True)
-                - to_column(jnp.sum(spread, axis=0, keepdims=True), rows, cols)
-                + jnp.sum(grad_lifted * lifted, axis=1, keepdims=True)
-                - tail_sum
-                + jnp.sum(grad_seen * seen, axis=1, keepdims=True)
-            )
-            grad_last = jnp.sum(tail_sum, axis=0, keepdims=True) + closing * jnp.sum(
-                jnp.sum(state * grad_state, axis=1, keepdims=True), axis=0, keepdims=True
-            )
-            ddecay_ref[head, :, part] = (
-                jnp.sum(jnp.where(rows >= cols, grad_cumul, 0.0), axis=0, keepdims=True) + grad_last
-            )
-            grad_beta = jnp.sum(grad_right * plain, axis=1, keepdims=True) + jnp.sum(
-                grad_lower * cross, axis=1, keepdims=True
-            )
-            dbeta_ref[head, :, part] = to_row(grad_beta, rows, cols)
-            grad_state = (
-                closing * grad_state
-                + mm_tn(jnp.concatenate([lifted, key], axis=0), jnp.concatenate([grad.astype(F32), grad_seen], axis=0))
-            )
-            grad_queries[chunk], grad_keys[chunk], grad_values[chunk] = grad_query, grad_key, beta * grad_right
-        dq, dk, dv = (
-            jnp.concatenate(grad_queries, axis=0) * DK**-0.5,
-            jnp.concatenate(grad_keys, axis=0),
-            jnp.concatenate(grad_values, axis=0),
-        )
+        query_unit, query_scale, keys, key_scale = unit_parts[head]
+        dq, dk = [
+            jnp.concatenate([terms[head, chunk][name] for chunk in range(chunks)], axis=0)
+            for name in ("grad_query", "grad_key")
+        ]
+        dq = dq * DK**-0.5
         dq_all.append(query_scale * (dq - query_unit * jnp.sum(dq * query_unit, axis=-1, keepdims=True)))
         dk_all.append(key_scale * (dk - keys * jnp.sum(dk * keys, axis=-1, keepdims=True)))
-        dv_all.append(dv)
+        dv_all.append(
+            jnp.concatenate(
+                [terms[head, chunk]["beta"] * terms[head, chunk]["grad_right"] for chunk in range(chunks)], axis=0
+            )
+        )
     dq = jnp.concatenate(dq_all, axis=1) * silu_slope(q_conv, q_sig)
     dk = jnp.concatenate(dk_all, axis=1) * silu_slope(k_conv, k_sig)
     dv = jnp.concatenate(dv_all, axis=1) * silu_slope(v_conv, v_sig)
@@ -325,13 +374,13 @@
         out_specs=[rows_spec(piece, DV), rows_spec(piece, DK), head_spec(chunks, DK, WIDE), rows_spec(piece, CHUNK)],
         out_shape=[
             shape_of((rows, HEADS * DV), F32),
-            shape_of((rows, HEADS * DK), BF),
-            shape_of((seqs, HEADS, chunks, DK, WIDE), BF),
-            shape_of((rows, HEADS * CHUNK), BF),
+            shape_of((rows, HEADS * DK), F32),
+            shape_of((seqs, HEADS, chunks, DK, WIDE), F32),
+            shape_of((rows, HEADS * CHUNK), F32),
         ],
         scratch_shapes=held(piece, 8),
         compiler_params=params(),
-        cost_estimate=pl.CostEstimate(flops=8 * 10**9, bytes_accessed=20 * 2**20, transcendentals=0),
+        cost_estimate=pl.CostEstimate(flops=30 * 10**9, bytes_accessed=20 * 2**20, transcendentals=0),
         name="open_rule",
     )(projected, projected, projected, edges, edges, edges, taps, taps, taps, betas, decays)
 
@@ -363,7 +412,7 @@
         ],
         out_specs=[rows_spec(piece, DV), rows_spec(piece, DV), head_spec(8, DV), head_spec(DK, DV)],
         out_shape=[
-            shape_of((rows, HEADS * DV), BF), shape_of((rows, HEADS * DV), BF),
+            shape_of((rows, HEADS * DV), F32), shape_of((rows, HEADS * DV), BF),
             shape_of((seqs, HEADS, 8, DV), F32), shape_of((seqs, HEADS, DK, DV), F32),
         ],
         compiler_params=params(),
@@ -394,7 +443,7 @@
         + [shape_of((HEADS, 1, rows), F32)] * 2,
         scratch_shapes=held(piece, 8) + held(piece, 16),
         compiler_params=params(),
-        cost_estimate=pl.CostEstimate(flops=16 * 10**9, bytes_accessed=30 * 2**20, transcendentals=0),
+        cost_estimate=pl.CostEstimate(flops=45 * 10**9, bytes_accessed=30 * 2**20, transcendentals=0),
         name="close_rule",
     )(projected, projected, projected, edges, edges, edges, taps, taps, taps, betas, decays,
       inverse, states, incoming, grad, leaving)
@@ -437,46 +486,115 @@
     return lax.dynamic_index_in_dim(block, index, dim, keepdims=False)
 
 
-def line_sum(parts, axis, dim):
+def tie(*values):
+    return lax.optimization_barrier(values)
+
+
+def partners(axis):
     size, me = lax.axis_size(axis), lax.axis_index(axis)
-
-    def share(index):
-        index = jnp.clip(index, 0, size - 1)
-        total = take(parts[0], dim, index).astype(F32)
-        for part in parts[1:]:
-            total = total + take(part, dim, index).astype(F32)
-        return total
-
-    from_left = from_right = None
-    for step in range(1, size):
-        right_going = share(me + size - step)
-        left_going = share(me - size + step)
-        if from_left is not None:
-            right_going = right_going + from_left.astype(F32)
-            left_going = left_going + from_right.astype(F32)
-        from_left = lax.ppermute(right_going.astype(BF), axis, [(i, i + 1) for i in range(step) if i + 1 < size])
-        from_right = lax.ppermute(
-            left_going.astype(BF), axis, [(i, i - 1) for i in range(size - step, size) if i > 0]
-        )
-    return [share(me), from_left, from_right]
-
-
-def scatter_sum(grad, order):
-    sizes = [lax.axis_size(axis) for axis in ALL]
-    rows = grad.shape[0] // (sizes[0] * sizes[1] * sizes[2] * sizes[3])
-    parts = [grad.reshape(*sizes, rows, grad.shape[1])]
-    left = list(ALL)
-    for axis in order:
-        dim = left.index(axis)
-        me, size = lax.axis_index(axis), lax.axis_size(axis)
-        if size == 2:
-            total_other = sum_of([take(part, dim, 1 - me) for part in parts])
-            total_mine = sum_of([take(part, dim, me) for part in parts])
-            parts = [total_mine.astype(BF), lax.ppermute(total_other.astype(BF), axis, [(0, 1), (1, 0)])]
-        else:
-            parts = [part for part in line_sum(parts, axis, dim)]
-        left.remove(axis)
-    return sum_of(parts)
+    if size & (size - 1):
+        raise ValueError(f"{axis} has {size}")
+    return [([(i, i ^ away) for i in range(size)], me ^ away) for away in range(1, size)]
+
+
+class Sum:
+    def __init__(self, parts):
+        self.parts, self.left = parts, ["z", SEQ]
+        self.sent_as = parts[0].dtype
+
+    @classmethod
+    def of_rows(cls, grad):
+        shape = (lax.axis_size("z"), 2, lax.axis_size(SEQ), -1, grad.shape[1])
+        whole, me = grad.reshape(shape), lax.axis_index("c")
+        return cls([take(whole, 1, me), lax.ppermute(take(whole, 1, 1 - me), "c", [(0, 1), (1, 0)])])
+
+    @classmethod
+    def of_product(cls, halves, grad, extra=None):
+        mine, other = halves
+        outer, inner = lax.axis_size("z"), lax.axis_size(SEQ)
+
+        def half(chosen, index):
+            found = product_left(chosen, grad).astype(BF)
+            if extra is not None:
+                more = take(extra.reshape(outer, 2, -1, extra.shape[1]), 1, index)
+                found = jnp.concatenate([found, more.reshape(-1, extra.shape[1])], axis=1)
+            return found.reshape(outer, inner, -1, found.shape[1])
+
+        me = lax.axis_index("c")
+        sent = lax.ppermute(half(other, 1 - me), "c", [(0, 1), (1, 0)])
+        return cls([half(mine, me), sent])
+
+    def direct(self, axis):
+        dim = self.left.index(axis)
+        self.left.remove(axis)
+
+        def share(index):
+            return sum_of([take(part, dim, index) for part in self.parts]).astype(self.sent_as)
+
+        came = [lax.ppermute(share(partner), axis, pairs) for pairs, partner in partners(axis)]
+        self.parts = [share(lax.axis_index(axis))] + came
+        return self
+
+    def reduce(self, axis):
+        dim = self.left.index(axis)
+        self.left.remove(axis)
+        total = jnp.moveaxis(sum_of(self.parts).astype(BF), dim, 0)
+        folded = total.reshape(-1, total.shape[-1])
+        folded = lax.psum_scatter(folded, axis, scatter_dimension=0, tiled=True)
+        self.parts = [folded.reshape(total.shape[1:])]
+        return self
+
+    def tied(self, *values):
+        out = tie(*values, *self.parts)
+        self.parts = list(out[len(values) :])
+        return out[0] if len(values) == 1 else out[: len(values)]
+
+    def result(self):
+        return sum_of(self.parts)
+
+
+def core_halves(features):
+    step = features.shape[1] // (2 * lax.axis_size("z"))
+    firsts = jnp.concatenate([features[:, i : i + step] for i in range(0, features.shape[1], 2 * step)], axis=1)
+    seconds = jnp.concatenate([features[:, i : i + step] for i in range(step, features.shape[1], 2 * step)], axis=1)
+    me = lax.axis_index("c")
+    return jnp.where(me == 0, firsts, seconds), jnp.where(me == 0, seconds, firsts)
+
+
+def everywhere(total):
+    for axis in ("c", "x", "y", "z"):
+        size, away = lax.axis_size(axis), 1
+        while away < size:
+            total = total + lax.ppermute(total, axis, [(i, i ^ away) for i in range(size)])
+            away *= 2
+    return total
+
+
+class Gather:
+    def __init__(self, block):
+        self.held, self.have, self.width = block, [], block.shape[-1]
+
+    def along(self, axis):
+        order = ("z", "c", SEQ)
+        size, me, held = lax.axis_size(axis), lax.axis_index(axis), self.held
+        dim = sum(order.index(other) < order.index(axis) for other in self.have)
+        came = [lax.ppermute(held, axis, pairs) for pairs, _ in partners(axis)]
+        entries = []
+        for index in range(size):
+            entry = held
+            for away in range(1, size):
+                entry = jnp.where(me == index ^ away, came[away - 1], entry)
+            entries.append(entry)
+        self.held = jnp.stack(entries, axis=dim)
+        self.have.append(axis)
+        return self
+
+    def tied(self, value):
+        value, self.held = tie(value, self.held)
+        return value
+
+    def result(self):
+        return self.held.reshape(-1, self.width)
 
 
 def sum_of(parts):
@@ -508,15 +626,18 @@
         axis=1,
     )
     extras = jnp.pad(extras, ((0, 0), (0, 128 - extras.shape[1])))
-    group = lax.all_gather(jnp.concatenate([proj_input, proj_outgate, extras], axis=1), ALL, axis=0, tiled=True)
-    output_matrix = lax.all_gather(proj_output, ALL, axis=0, tiled=True)
+    group = lax.all_gather(jnp.concatenate([proj_input, extras], axis=1), ALL, axis=0, tiled=True)
     feed_group = lax.all_gather(jnp.concatenate([feed_gate, feed_up], axis=1), ALL, axis=0, tiled=True)
-    down_matrix = lax.all_gather(feed_down, ALL, axis=0, tiled=True)
+    all_outgate = Gather(proj_outgate).along("z").along(SEQ)
+    all_output = Gather(proj_output).along("z")
+    all_down = Gather(feed_down).along("z")
+    group = all_down.tied(all_output.tied(all_outgate.tied(group)))
+    all_outgate.along("c")
+    all_output.along(SEQ)
     hidden_units = feed_gate.shape[1]
 
     input_matrix = group[:, :channels]
-    outgate_matrix = group[:, channels : channels + HEADS * DV]
-    small = group[:, channels + HEADS * DV :]
+    small = group[:, channels:]
     gates_matrix = small[:, : 2 * HEADS]
     bank = small[:, 2 * HEADS : 2 * HEADS + 16].reshape(channels, CONV).astype(F32)
     gain_first = small[:, 2 * HEADS + 16].astype(F32)
@@ -539,23 +660,39 @@
     edge = shift(projected.reshape(seqs, piece, channels)[:, piece - CONV + 1 :], 1)
     edges = jnp.pad(edge.astype(F32), ((0, 0), (9 - CONV, 0), (0, 0))).reshape(seqs * 8, channels)
     local, reading, states, inverse = open_rule(projected, edges, taps, beta_rows, decay_rows, seqs, piece)
+    states = all_outgate.tied(all_output.tied(states))
+    all_down.along(SEQ)
+    outgate_matrix = all_outgate.result()
     outgate = product(first, outgate_matrix)
+    all_output.along("c")
 
     pieces = lax.axis_size(SEQ)
     carried, transfer = states[:, :, -1, :, :DV], states[:, :, -1, :, DV:]
     incoming = jnp.zeros(carried.shape, BF)
     for hop in range(1, pieces):
         ending = carried.astype(F32) + jnp.einsum(
-            "...dk,...ke->...de", transfer, incoming, preferred_element_type=F32
+            "...dk,...ke->...de", transfer, incoming.astype(F32), precision=lax.Precision.HIGH
         )
         incoming = incoming + lax.ppermute(ending.astype(BF), SEQ, [(hop - 1, hop)])
 
+    after = shift(transfer.astype(BF), -1)
+    chains = [jnp.swapaxes(after, -1, -2)] if pieces > 2 else []
+    for _ in range(pieces - 3):
+        chain = jnp.einsum("...ki,...kj->...ij", after, shift(chains[-1], -1), preferred_element_type=F32)
+        chains.append(chain.astype(BF))
+
+    incoming = all_down.tied(all_output.tied(incoming))
+    all_down.along("c")
+    output_matrix = all_output.result()
+    if chains:
+        outgate, *chains = tie(outgate, *chains)
     mixed, gated = finish(local, reading, incoming, outgate, heads_gain, seqs, piece)
     middle = residual + product(gated, output_matrix)
     inverse_two = inverse_root(middle)
     normed_two = middle * inverse_two
     second = (normed_two * gain_second).astype(BF)
     gate_matrix, upward_matrix = feed_group[:, :hidden_units], feed_group[:, hidden_units:]
+    down_matrix = all_down.result()
     up_gate = product(second, gate_matrix)
     up_linear = product(second, upward_matrix)
     sigmoid_gate = jax.nn.sigmoid(up_gate)
@@ -564,37 +701,45 @@
     layer_out = (middle + product(hidden, down_matrix)).astype(BF)
 
     grad_branch = cotangent.reshape(rows, D)
-    grad_feed_down = product_left(hidden, grad_branch).astype(BF)
+    sum_down = Sum.of_rows(product_left(hidden, grad_branch).astype(BF))
     grad_hidden = product_right(grad_branch, down_matrix)
     grad_gate = (grad_hidden * up_linear * (sigmoid_gate + silu_gate * (1.0 - sigmoid_gate))).astype(BF)
     grad_up = (grad_hidden * silu_gate).astype(BF)
-    grad_feed_gate = product_left(second, grad_gate).astype(BF)
-    grad_feed_up = product_left(second, grad_up).astype(BF)
-    sum_feed_down = scatter_sum(grad_feed_down, ("c", "z", "x", "y"))
-    sum_feed_gate = scatter_sum(grad_feed_gate, ("c", "x", "y", "z"))
-    sum_feed_up = scatter_sum(grad_feed_up, ("c", "y", "x", "z"))
+    sum_feed = Sum.of_product(core_halves(second), jnp.concatenate([grad_gate, grad_up], axis=1))
     grad_second = product_right(grad_gate, gate_matrix) + product_right(grad_up, upward_matrix)
+    grad_second = sum_feed.tied(grad_second)
+    sum_feed.reduce("z")
     grad_gain_feed, grad_norm_two = norm_back(grad_second, normed_two, inverse_two, gain_second)
     grad_middle = grad_branch.astype(F32) + grad_norm_two
     grad_mixer_out = grad_middle.astype(BF)
-    grad_proj_output = product_left(gated, grad_mixer_out).astype(BF)
-    sum_proj_output = scatter_sum(grad_proj_output, ("c", "x", "y", "z"))
+    grad_mixer_out = sum_down.tied(grad_mixer_out)
+    sum_down.direct(SEQ)
     grad_gated = product_right(grad_mixer_out, output_matrix)
     grad_mixed, grad_outgate, gain_parts, flow = unfinish(
         grad_gated, mixed, outgate, heads_gain, reading, seqs, piece
     )
     grad_gain_heads = jnp.sum(gain_parts[:, :, 0], axis=(0, 1))
-    grad_proj_outgate = product_left(first, grad_outgate).astype(BF)
-    sum_proj_outgate = scatter_sum(grad_proj_outgate, ("c", "y", "x", "z"))
-
-    leaving = jnp.zeros(carried.shape, BF)
-    for hop in range(pieces - 1, 0, -1):
-        starting = flow + jnp.einsum("...ki,...ke->...ie", transfer, leaving, preferred_element_type=F32)
-        leaving = leaving + lax.ppermute(starting.astype(BF), SEQ, [(hop, hop - 1)])
+
+    flow = flow.astype(BF)
+    leaving = shift(flow, -1).astype(F32)
+    for ahead, chain in enumerate(chains, 2):
+        leaving = leaving + jnp.einsum(
+            "...ik,...ke->...ie", chain, shift(flow, -ahead), preferred_element_type=F32
+        )
+    first_halves = core_halves(first)
+    sum_outgate = Sum.of_product(first_halves, grad_outgate)
+    sum_output = Sum.of_rows(product_left(gated, grad_mixer_out).astype(BF))
+    leaving = sum_feed.tied(sum_output.tied(sum_outgate.tied(sum_down.tied(leaving.astype(BF)))))
+    sum_down.direct("z")
+    sum_outgate.direct(SEQ)
+    sum_output.direct(SEQ)
+    sum_feed.reduce(SEQ)
 
     outs = close_rule(
         projected, edges, taps, beta_rows, decay_rows, inverse, states, incoming, grad_mixed, leaving, seqs, piece
     )
+    outs = sum_outgate.tied(*sum_down.tied(*outs))
+    sum_outgate.direct("z")
     grad_edges = jnp.concatenate(outs[3:6], axis=1).reshape(seqs, 8, channels)[:, 9 - CONV :]
     returned = shift(grad_edges.astype(BF), -1)
     starts = (0, width, 2 * width, channels)
@@ -611,53 +756,60 @@
     grad_decay_log = jnp.sum(grad_decays * decays, axis=1)
     grad_decay_bias = jnp.sum(grad_decay_pre, axis=1)
     grad_gates = jnp.concatenate([grad_beta_pre, grad_decay_pre], axis=0).astype(BF)
-
-    orders = (("c", "z", "x", "y"), ("c", "x", "y", "z"), ("c", "y", "x", "z"))
-    sums = [
-        scatter_sum(product_left(first, grad).astype(BF), order) for grad, order in zip(grad_parts, orders)
-    ]
-    sum_proj_input = jnp.concatenate(sums, axis=1)
-    grad_first = (
-        product_right(grad_outgate, outgate_matrix)
-        + lax.dot_general(grad_gates, gates_matrix, (((0,), (1,)), ((), ())), preferred_element_type=F32)
+    grad_proj_gates = lax.dot_general(first, grad_gates, (((0,), (1,)), ((), ())), preferred_element_type=F32)
+
+    packed_heads = jnp.pad(
+        grad_gain_heads.reshape(devices, -1), ((0, 0), (0, own - gain_heads.shape[0]))
+    ).reshape(D, 1)
+    grad_extras = jnp.concatenate(
+        [grad_proj_gates, bank_grad.reshape(D, 16), grad_gain_feed[:, None], packed_heads], axis=1
     )
-    for part, grad in enumerate(grad_parts):
-        grad_first = grad_first + product_right(grad, input_matrix[:, starts[part] : starts[part + 1]])
+    grad_extras = jnp.pad(grad_extras, ((0, 0), (0, 128 - grad_extras.shape[1]))).astype(BF)
+    grad_query_key = jnp.concatenate(grad_parts[:2], axis=1)
+    sum_query_key = Sum.of_product(first_halves, grad_query_key)
+    sum_values = Sum.of_product(first_halves, grad_parts[2], grad_extras)
+    grad_first = product_right(grad_outgate, outgate_matrix) + lax.dot_general(
+        grad_gates, gates_matrix, (((0,), (1,)), ((), ())), preferred_element_type=F32
+    )
+    grad_first = sum_query_key.tied(sum_output.tied(grad_first))
+    sum_query_key.direct("z")
+    grad_first = grad_first + product_right(grad_parts[2], input_matrix[:, 2 * width :])
+    grad_first = sum_values.tied(grad_first)
+    sum_values.direct(SEQ)
+    sum_output.direct("z")
+    grad_first = grad_first + product_right(grad_query_key, input_matrix[:, : 2 * width])
     grad_gain_mixer, grad_norm_one = norm_back(grad_first, normed_one, inverse_one, gain_first)
+    sum_gain = Sum.of_rows(grad_gain_mixer.reshape(devices, own))
+    sum_gain.parts = list(sum_values.tied(*sum_gain.parts))
+    sum_values.direct("z")
+    sum_gain.direct(SEQ)
+    sum_gain.parts = list(sum_query_key.tied(*sum_gain.parts))
+    sum_query_key.direct(SEQ)
+    sum_gain.direct("z")
     tokens_grad = (grad_middle + grad_norm_one).reshape(seqs, piece, D)
-    grad_proj_gates = lax.dot_general(first, grad_gates, (((0,), (1,)), ((), ())), preferred_element_type=F32)
-
-    pieces_small = (
-        grad_gain_mixer, grad_gain_feed, grad_gain_heads, grad_decay_log, grad_decay_bias,
-        bank_grad.reshape(-1), grad_proj_gates.reshape(-1),
-    )
-    packed = jnp.concatenate(pieces_small)
-    packed = lax.psum(jnp.pad(packed, (0, -packed.shape[0] % 1024)), ALL)
-    me = lax.axis_index(ALL)
-    found, place = [], 0
-    for block in pieces_small:
-        size = block.shape[0]
-        if size == HEADS:
-            found.append(packed[place : place + size])
-        else:
-            found.append(lax.dynamic_slice(packed, (place + me * (size // devices),), (size // devices,)))
-        place += size
+    sum_value_rows = sum_values.result()
+    sum_proj_input = jnp.concatenate([sum_query_key.result(), sum_value_rows[:, : HEADS * DV]], axis=1)
+    found_extras = sum_value_rows[:, HEADS * DV :]
+
+    decay_sums = jnp.pad(jnp.stack([grad_decay_log, grad_decay_bias]), ((0, 6), (0, 128 - HEADS)))
+    decay_sums = everywhere(decay_sums)
+    feed_rows = sum_feed.result()
     return (
         layer_out.reshape(seqs, piece, D),
         tokens_grad,
-        found[0],
+        sum_gain.result().reshape(own),
         sum_proj_input,
-        found[5].reshape(-1, CONV),
-        found[6].reshape(-1, 2 * HEADS),
-        sum_proj_outgate,
-        found[2],
-        sum_proj_output,
-        found[1],
-        sum_feed_gate,
-        sum_feed_up,
-        sum_feed_down,
-        found[3],
-        found[4],
+        found_extras[:, 2 * HEADS : 2 * HEADS + 16].reshape(-1, CONV),
+        found_extras[:, : 2 * HEADS],
+        sum_outgate.result(),
+        found_extras[: gain_heads.shape[0], 2 * HEADS + 17],
+        sum_output.result(),
+        found_extras[:, 2 * HEADS + 16],
+        feed_rows[:, :hidden_units],
+        feed_rows[:, hidden_units:],
+        sum_down.result(),
+        decay_sums[0, :HEADS],
+        decay_sums[1, :HEADS],
     )
 
 

time: 962 us -> 700 us (0.73)
  waiting for transfers between devices: 430 us -> 153 us
  other arithmetic: 52.5 us -> 86.4 us
  starting transfers between devices: 164 us -> 136 us
  local copies, waits for them, and re-layouts: 44.2 us -> 56 us
    all_gather x3 -> x1, waiting for transfers between devices: 160 us -> 20.3 us  [shards(): lax.all_gather(jnp.concatenate([proj_input, extras], axis=1), ALL, axis=0...]
    psum x1 -> x0, waiting for transfers between devices: 103 us -> none  [shards(): packed = lax.psum(jnp.pad(packed, (0, -packed.shape[0] % 1024)), ALL)]
    ppermute x75 -> x69, starting transfers between devices: 154 us -> 120 us  [the longest x36 72.2 us: direct(): lax.ppermute(share(partner), axis, pairs)]
    all_gather x1, waiting for transfers between devices: 31.4 us -> 0.01 us  [shards(): lax.all_gather(jnp.concatenate([feed_gate, feed_up], axis=1), ALL, axis=0...]
    another operation x3 -> x26, other arithmetic: 2.37 us -> 21 us  [the longest x19 16.8 us: along(): self.held = jnp.stack(entries, axis=dim)]
    pallas_call x1, Pallas kernels: 44.6 us -> 62.2 us  [close_rule(): pl.pallas_call(functools.partial(closing_kernel, piece), grid=(steps, seq...]
    pallas_call x1, Pallas kernels: 61.3 us -> 46.3 us  [open_rule(): pl.pallas_call(functools.partial(opening_kernel, piece), grid=(HEADS // P...]
    ppermute x3, waiting for transfers between devices: 15.2 us -> 2.17 us  [shards(): incoming = incoming + lax.ppermute(ending.astype(BF), SEQ, [(hop - 1, hop)])]
  transfers between devices with their start and end apart: 85 -> 83, of which waited for: 31 -> 25; matrix products, arithmetic and copies ran while one was open for 17% -> 31% of each run, Pallas kernels for 12% -> 18%
where the time goes in v2:
time: 700 us; the launch traced here: 692 us
  waiting for transfers between devices  153 us (22%)
  starting transfers between devices  136 us (19%)
  Pallas kernels  126 us (18%)
  matrix products  119 us (17%)
  other arithmetic  86.4 us (12%)
  local copies, waits for them, and re-layouts  56 us (8%)
  between operations  16 us (2%)
    ppermute x36, starting transfers between devices, direct(): lax.ppermute(share(partner), axis, pairs)  72.2 us
    ppermute x36, waiting for transfers between devices, direct(): lax.ppermute(share(partner), axis, pairs)  65 us
    pallas_call x1, Pallas kernels, close_rule(): pl.pallas_call(functools.partial(closing_kernel, piece), grid=(steps, seq...  62.2 us
    ppermute x21, waiting for transfers between devices, along(): came = [lax.ppermute(held, axis, pairs) for pairs, _ in partners(axis)]  53 us
    pallas_call x1, Pallas kernels, open_rule(): pl.pallas_call(functools.partial(opening_kernel, piece), grid=(HEADS // P...  46.3 us
    ppermute x21, starting transfers between devices, along(): came = [lax.ppermute(held, axis, pairs) for pairs, _ in partners(axis)]  39.5 us
    dot_general x6, matrix products, product(): return jnp.dot(left, right, preferred_element_type=F32)  34.7 us
    dot_general x7, matrix products, product_right(): lax.dot_general(left, right, (((1,), (1,)), ((), ())), preferred_element_...  33.9 us
  transfers between devices with their start and end apart: 83, of which 25 were waited for; matrix products, arithmetic and copies ran while one was open for 31% of the time, Pallas kernels for 18%

profile of v2, /device:TPU:0, one launch (start us, length us, event | category | flops | bytes accessed | tf_op | source)
XLA Modules:
  0.0 692.0 jit_solution(13745628788108658380)
XLA Ops:
  15.0 5.1 collective-permute-start
  20.8 3.7 collective-permute-start.6
  24.9 9.7 %collective-permute-start.8 = (bf16[64,1024]{1,0:T(8,128)(2,1)S(1)}, bf16[64,1024]{1,0:T(8,128)(2,1)S(1)}, u32[]{:S(2)}, u32[]{:S(2)}) collective-permute-start(bf16[64,1024]{1,0:T(8,128)(2,1)S(1)} %copy-done.71), channel_id=1, source_target_pairs={{0,8},{8,0},{16,24},{24,16},{1,9},{9,1},{17,25},{25,17},{2,10},{10... | collective-permute-start | bytes 393224 | tf_op jit(solution)/shard_map/ppermute | solution.py:581
  34.6 9.2 %collective-permute-done.1 = bf16[32,2048]{1,0:T(8,128)(2,1)S(1)} collective-permute-done((bf16[32,2048]{1,0:T(8,128)(2,1)}, bf16[32,2048]{1,0:T(8,128)(2,1)S(1)}, u32[]{:S(2)}, u32[]{:S(2)}) %collective-permute-start.1) | collective-permute-done | bytes 131104 | tf_op jit(solution)/shard_map/ppermute | solution.py:581
  43.8 2.9 collective-permute-start.9
  46.9 5.4 collective-permute-start.11
  52.3 10.8 %collective-permute-done.7 = bf16[64,1024]{1,0:T(8,128)(2,1)} collective-permute-done((bf16[64,1024]{1,0:T(8,128)(2,1)}, bf16[64,1024]{1,0:T(8,128)(2,1)}, u32[]{:S(2)}, u32[]{:S(2)}) %collective-permute-start.7) | collective-permute-done | bytes 131104 | tf_op jit(solution)/shard_map/ppermute | solution.py:581
  63.1 2.5 collective-permute-start.3
  68.5 7.0 %collective-permute-done.10 = bf16[88,1024]{1,0:T(8,128)(2,1)S(1)} collective-permute-done((bf16[88,1024]{1,0:T(8,128)(2,1)S(1)}, bf16[88,1024]{1,0:T(8,128)(2,1)S(1)}, u32[]{:S(2)}, u32[]{:S(2)}) %collective-permute-start.10) | collective-permute-done | bytes 180256 | tf_op jit(solution)/shard_map/ppermute | solution.py:581
  77.4 10.8 %collective-permute-done.4 = bf16[4,32,2048]{2,1,0:T(8,128)(2,1)S(1)} collective-permute-done((bf16[4,32,2048]{2,1,0:T(8,128)(2,1)S(1)}, bf16[4,32,2048]{2,1,0:T(8,128)(2,1)S(1)}, u32[]{:S(2)}, u32[]{:S(2)}) %collective-permute-start.4) | collective-permute-done | bytes 524320 | tf_op jit(solution)/shard_map/ppermute | solution.py:581
  91.3 20.3 %all-gather.3.cloned.1.call-done = bf16[1024,4224]{1,0:T(8,128)(2,1)} async-done(((bf16[32,4224]{1,0:T(8,128)(2,1)}), bf16[1024,4224]{1,0:T(8,128)(2,1)}) %all-gather.3.cloned.1.call-update) | async-done | bytes 8650768 | tf_op jit(solution)/shard_map/all_gather | solution.py:629
  118.0 8.5 %fusion.2.q_ref.k_ref.v_ref = bf16[512,4096]{1,0:T(8,128)(2,1)S(1)} fusion(bf16[512,1024]{1,0:T(8,128)(2,1)S(1)} %fusion.28, bf16[1024,4224]{1,0:T(8,128)(2,1)} %all-gather.3.cloned.1.call-done), kind=kOutput, calls=%fused_computation.5 | convolution fusion | flops 4297064448 | bytes 13631488 | tf_op jit(solution)/shard_map/dot_general | solution.py:457
  128.4 3.2 collective-permute-start.12
  137.2 2.4 collective-permute-done.12
  139.6 3.0 collective-permute-start.21
  143.3 46.3 %open_rule.1 = (f32[512,2048]{1,0:T(8,128)}, f32[512,1024]{1,0:T(8,128)}, f32[1,8,4,128,384]{4,3,2,1,0:T(8,128)}, f32[512,1024]{1,0:T(8,128)}) custom-call(bf16[512,4096]{1,0:T(8,128)(2,1)} %copy-done.89, bf16[512,4096]{1,0:T(8,128)(2,1)} %copy-done.89, bf16[512,4096]{1,0:T(8,128)(2,1)} %copy-done.89, f32[8,4096]{1,0:T(8,128)} %bitcast_convert_fusion.qe_ref.ke_ref.ve_ref, ...), custom_call_target="tpu_custom_call" | custom-call | flops 30000001024 | bytes 20971520 | tf_op jit(solution)/shard_map/open_rule/pallas_call | solution.py:369
  197.1 2.9 fusion.47
  200.0 2.8 collective-permute-start.17
  205.2 12.7 %collective-permute-done.22 = bf16[4,88,1024]{2,1,0:T(8,128)(2,1)S(1)} collective-permute-done((bf16[4,88,1024]{2,1,0:T(8,128)(2,1)S(1)}, bf16[4,88,1024]{2,1,0:T(8,128)(2,1)S(1)}, u32[]{:S(2)}, u32[]{:S(2)}) %collective-permute-start.22) | collective-permute-done | bytes 720928 | tf_op jit(solution)/shard_map/ppermute | solution.py:581
  229.9 4.5 fusion.50.outgate_ref
  241.0 8.1 %finish_heads.1 = (f32[512,2048]{1,0:T(8,128)}, bf16[512,2048]{1,0:T(8,128)(2,1)}) custom-call(f32[512,2048]{1,0:T(8,128)} %get-tuple-element.130.local_ref, f32[512,1024]{1,0:T(8,128)} %get-tuple-element.131.reading_ref, bf16[1,8,128,256]{3,2,1,0:T(8,128)(2,1)} %add.976.incoming_ref, f32[512,2048]{1,0:T(8,128)} %fusion.50.outgate_ref, ...), custom_call_target="tpu_custom_call" | custom-call | tf_op jit(solution)/shard_map/finish_heads/pallas_call | solution.py:390
  249.1 4.0 multiply_reduce_fusion.2
  254.4 5.9 fusion.10
  260.4 4.9 fusion.14
  265.2 3.1 select_bitcast_fusion.1
  269.6 9.9 %fusion.6 = (bf16[512,2816]{1,0:T(8,128)(2,1)S(1)}, bf16[512,2816]{1,0:T(8,128)(2,1)S(1)}, bf16[512,2816]{1,0:T(8,128)(2,1)}) fusion(f32[512,2816]{1,0:T(8,128)S(1)} %fusion.10, f32[512,2816]{1,0:T(8,128)} %fusion.14, bf16[2816,1024]{1,0:T(8,128)(2,1)S(1)} %bitcast.430, bf16[1,512,1024]{2,1,0:T(8,128)(2,1)S(1)} %copy-done.14), kind=kOutput, calls=%fused_computation.11 | convolution fusion | flops 2972975104 | bytes 27000832 | tf_op jit(solution)/shard_map/dot_general | solution.py:465
  282.0 5.6 convolution_convert_fusion
  287.7 8.5 %convolution_convert_fusion.1 = bf16[512,5632]{1,0:T(8,128)(2,1)} fusion(bf16[512,2816]{1,0:T(8,128)(2,1)} %copy-done.97, bf16[512,2816]{1,0:T(8,128)(2,1)} %copy-done.95, pred[]{:T(512)S(6)} %eq.29, bf16[512,128]{1,0:T(8,128)(2,1)S(1)} %copy-done.63, bf16[512,128]{1,0:T(8,128)(2,1)S(1)} %copy-done.64, bf16[512,128]{1,0:T(8,128)(2,1)S(1)} %copy-done.65, ...), kind=kOutput, calls=%fused_computation.2 | convolution fusion | flops 2971664384 | bytes 12582913 | tf_op jit(solution)/shard_map/dot_general | solution.py:461
  296.2 5.1 fusion.8
  301.3 4.5 fusion.38
  305.9 6.8 add_convert_fusion
  312.8 5.5 convolution_convert_fusion.2
  318.2 2.5 constant_dynamic-slice_fusion.30
  323.7 4.1 copy.260
  327.7 6.9 fusion.41
  338.0 4.3 fusion.193.grad_ref
  342.4 9.7 %unfinish_heads.1 = (f32[512,2048]{1,0:T(8,128)}, bf16[512,2048]{1,0:T(8,128)(2,1)}, f32[1,8,8,256]{3,2,1,0:T(8,128)}, f32[1,8,128,256]{3,2,1,0:T(8,128)}) custom-call(f32[512,2048]{1,0:T(8,128)} %fusion.193.grad_ref, f32[512,2048]{1,0:T(8,128)} %get-tuple-element.148.mixed_ref, f32[512,2048]{1,0:T(8,128)} %fusion.50.outgate_ref, ...), custom_call_target="tpu_custom_call" | custom-call | tf_op jit(solution)/shard_map/unfinish_heads/pallas_call | solution.py:406
  358.5 3.0 convolution_convert_fusion.8
  374.2 4.3 fusion.60
  378.9 3.7 fusion.194
  382.5 5.7 collective-permute-done.30
  388.2 13.9 %collective-permute-start.32 = (bf16[4,88,1024]{2,1,0:T(8,128)(2,1)S(1)}, bf16[4,88,1024]{2,1,0:T(8,128)(2,1)S(1)}, u32[]{:S(2)}, u32[]{:S(2)}) collective-permute-start(bf16[4,88,1024]{2,1,0:T(8,128)(2,1)S(1)} %get-tuple-element.327), channel_id=1, source_target_pairs={{0,1},{1,0},{2,3},{3,2},{4,5},{5,4},{6,7},{7,6},{8,9},{9,8},{10,11... | collective-permute-start | bytes 2162696 | tf_op jit(solution)/shard_map/ppermute | solution.py:534
  402.1 5.7 collective-permute-start.33
  412.9 6.1 collective-permute-done.32
  419.0 20.3 %collective-permute-done.33 = bf16[4,88,1024]{2,1,0:T(8,128)(2,1)S(1)} collective-permute-done((bf16[4,88,1024]{2,1,0:T(8,128)(2,1)S(1)}, bf16[4,88,1024]{2,1,0:T(8,128)(2,1)S(1)}, u32[]{:S(2)}, u32[]{:S(2)}) %collective-permute-start.33) | collective-permute-done | bytes 720928 | tf_op jit(solution)/shard_map/ppermute | solution.py:534
  442.3 2.5 collective-permute-start.38
  444.9 3.5 fusion.69
  450.5 3.6 fusion.73
  455.5 62.2 %close_rule.1 = (bf16[512,1024]{1,0:T(8,128)(2,1)}, bf16[512,1024]{1,0:T(8,128)(2,1)}, bf16[512,2048]{1,0:T(8,128)(2,1)}, f32[8,1024]{1,0:T(8,128)}, f32[8,1024]...) custom-call(bf16[512,4096]{1,0:T(8,128)(2,1)} %copy-done.89, ...), custom_call_target="tpu_custom_call" | custom-call | flops 44999999488 | bytes 31457280 | tf_op jit(solution)/shard_map/close_rule/pallas_call | solution.py:431
  528.8 3.5 convolution_add_fusion
  533.6 8.6 %collective-permute-done.44 = bf16[4,64,1024]{2,1,0:T(8,128)(2,1)} collective-permute-done((bf16[4,64,1024]{2,1,0:T(8,128)(2,1)}, bf16[4,64,1024]{2,1,0:T(8,128)(2,1)}, u32[]{:S(2)}, u32[]{:S(2)}) %collective-permute-start.44) | collective-permute-done | bytes 524320 | tf_op jit(solution)/shard_map/ppermute | solution.py:534
  558.2 3.4 collective-permute-start.78
  574.7 3.4 convolution_convert_fusion.6
  595.6 7.9 %collective-permute-done.69 = bf16[32,2048]{1,0:T(8,128)(2,1)S(1)} collective-permute-done((bf16[32,2048]{1,0:T(8,128)(2,1)S(1)}, bf16[32,2048]{1,0:T(8,128)(2,1)S(1)}, u32[]{:S(2)}, u32[]{:S(2)}) %collective-permute-start.69) | collective-permute-done | bytes 131104 | tf_op jit(solution)/shard_map/ppermute | solution.py:534
  608.9 2.6 collective-permute-start.58
  613.8 2.6 collective-permute-start.50
  616.4 4.0 fusion.34
  623.6 5.1 collective-permute-done.50
  628.7 3.1 collective-permute-start.52
  631.9 4.7 fusion.33
  636.6 12.2 %collective-permute-done.51 = bf16[4,32,2176]{2,1,0:T(8,128)(2,1)S(1)} collective-permute-done((bf16[4,32,2176]{2,1,0:T(8,128)(2,1)}, bf16[4,32,2176]{2,1,0:T(8,128)(2,1)S(1)}, u32[]{:S(2)}, u32[]{:S(2)}) %collective-permute-start.51) | collective-permute-done | bytes 557088 | tf_op jit(solution)/shard_map/ppermute | solution.py:534
  654.9 4.1 collective-permute-start.66
  660.0 3.5 collective-permute-start.59
  665.1 5.6 collective-permute-start.64
  (490 shorter events, 194.2 us)
Async XLA Ops:
  7.2 104.3 %all-gather.3.cloned.1.call-start = ((), (), s32[]{:S(2)}) async-start(), calls=%async_computation.2 | async-start | bytes 8921088 | tf_op jit(solution)/shard_map/all_gather | solution.py:629
  13.1 241.3 %all-gather.5.cloned.1.call-start = ((), (), s32[]{:S(2)}) async-start(), calls=%async_computation.3 | async-start | bytes 11894784 | tf_op jit(solution)/shard_map/all_gather | solution.py:630
  15.0 439.1 %reduce-scatter.3.cloned.1.call-start = ((), (), s32[]{:S(2)}) async-start(), calls=%async_computation.4 | async-start | bytes 7208960 | tf_op jit(solution)/shard_map/reduce_scatter | solution.py:543
  20.1 23.7 %collective-permute-start.1 = (bf16[32,2048]{1,0:T(8,128)(2,1)}, bf16[32,2048]{1,0:T(8,128)(2,1)S(1)}, u32[]{:S(2)}, u32[]{:S(2)}) collective-permute-start(bf16[32,2048]{1,0:T(8,128)(2,1)} %param.21), channel_id=1, source_target_pairs={{0,16},{8,24},{16,0},{24,8},{1,17},{9,25},{17,1},{25,9},{2,18},{10... | collective-permute-start | bytes 393224 | tf_op jit(solution)/shard_map/ppermute | solution.py:581
  20.1 26.6 %collective-permute-start.2 = (bf16[32,2048]{1,0:T(8,128)(2,1)}, bf16[32,2048]{1,0:T(8,128)(2,1)S(1)}, u32[]{:S(2)}, u32[]{:S(2)}) collective-permute-start(bf16[32,2048]{1,0:T(8,128)(2,1)} %param.21), channel_id=1, source_target_pairs={{0,8},{8,0},{16,24},{24,16},{1,9},{9,1},{17,25},{25,17},{2,10},{10... | collective-permute-start | bytes 393224 | tf_op jit(solution)/shard_map/ppermute | solution.py:581
  20.8 26.1 %collective-permute-start.6 = (bf16[64,1024]{1,0:T(8,128)(2,1)}, bf16[64,1024]{1,0:T(8,128)(2,1)S(1)}, u32[]{:S(2)}, u32[]{:S(2)}) collective-permute-start(bf16[64,1024]{1,0:T(8,128)(2,1)} %param.23), channel_id=1, source_target_pairs={{0,24},{8,16},{16,8},{24,0},{1,25},{9,17},{17,9},{25,1},{2,26},{10... | collective-permute-start | bytes 393224 | tf_op jit(solution)/shard_map/ppermute | solution.py:581
  24.5 38.6 %collective-permute-start.7 = (bf16[64,1024]{1,0:T(8,128)(2,1)}, bf16[64,1024]{1,0:T(8,128)(2,1)}, u32[]{:S(2)}, u32[]{:S(2)}) collective-permute-start(bf16[64,1024]{1,0:T(8,128)(2,1)} %param.23), channel_id=1, source_target_pairs={{0,16},{8,24},{16,0},{24,8},{1,17},{9,25},{17,1},{25,9},{2,18},{10... | collective-permute-start | bytes 393224 | tf_op jit(solution)/shard_map/ppermute | solution.py:581
  24.9 40.7 %collective-permute-start.8 = (bf16[64,1024]{1,0:T(8,128)(2,1)S(1)}, bf16[64,1024]{1,0:T(8,128)(2,1)S(1)}, u32[]{:S(2)}, u32[]{:S(2)}) collective-permute-start(bf16[64,1024]{1,0:T(8,128)(2,1)S(1)} %copy-done.71), channel_id=1, source_target_pairs={{0,8},{8,0},{16,24},{24,16},{1,9},{9,1},{17,25},{25,17},{2,10},{10... | collective-permute-start | bytes 393224 | tf_op jit(solution)/shard_map/ppermute | solution.py:581
  43.8 22.3 %collective-permute-start.9 = (bf16[88,1024]{1,0:T(8,128)(2,1)S(1)}, bf16[88,1024]{1,0:T(8,128)(2,1)S(1)}, u32[]{:S(2)}, u32[]{:S(2)}) collective-permute-start(bf16[88,1024]{1,0:T(8,128)(2,1)S(1)} %copy-done.33), channel_id=1, source_target_pairs={{0,24},{8,16},{16,8},{24,0},{1,25},{9,17},{17,9},{25,1},{2,26},{10... | collective-permute-start | bytes 540680 | tf_op jit(solution)/shard_map/ppermute | solution.py:581
  46.7 28.7 %collective-permute-start.10 = (bf16[88,1024]{1,0:T(8,128)(2,1)S(1)}, bf16[88,1024]{1,0:T(8,128)(2,1)S(1)}, u32[]{:S(2)}, u32[]{:S(2)}) collective-permute-start(bf16[88,1024]{1,0:T(8,128)(2,1)S(1)} %copy-done.33), channel_id=1, source_target_pairs={{0,16},{8,24},{16,0},{24,8},{1,17},{9,25},{17,1},{25,9},{2,18},{10... | collective-permute-start | bytes 540680 | tf_op jit(solution)/shard_map/ppermute | solution.py:581
  46.9 28.6 %collective-permute-start.11 = (bf16[88,1024]{1,0:T(8,128)(2,1)S(1)}, bf16[88,1024]{1,0:T(8,128)(2,1)S(1)}, u32[]{:S(2)}, u32[]{:S(2)}) collective-permute-start(bf16[88,1024]{1,0:T(8,128)(2,1)S(1)} %copy-done.33), channel_id=1, source_target_pairs={{0,8},{8,0},{16,24},{24,16},{1,9},{9,1},{17,25},{25,17},{2,10},{10... | collective-permute-start | bytes 540680 | tf_op jit(solution)/shard_map/ppermute | solution.py:581
  63.1 14.3 %collective-permute-start.3 = (bf16[4,32,2048]{2,1,0:T(8,128)(2,1)S(1)}, bf16[4,32,2048]{2,1,0:T(8,128)(2,1)S(1)}, u32[]{:S(2)}, u32[]{:S(2)}) collective-permute-start(bf16[4,32,2048]{2,1,0:T(8,128)(2,1)S(1)} %pad_maximum_fusion.16), channel_id=1, source_target_pairs={{0,3},{1,2},{2,1},{3,0},{4,7},{5,6},{6,5},{7,4},{8,11},{9,10},{10,... | collective-permute-start | bytes 1572872 | tf_op jit(solution)/shard_map/ppermute | solution.py:581
  65.6 22.6 %collective-permute-start.4 = (bf16[4,32,2048]{2,1,0:T(8,128)(2,1)S(1)}, bf16[4,32,2048]{2,1,0:T(8,128)(2,1)S(1)}, u32[]{:S(2)}, u32[]{:S(2)}) collective-permute-start(bf16[4,32,2048]{2,1,0:T(8,128)(2,1)S(1)} %pad_maximum_fusion.16), channel_id=1, source_target_pairs={{0,2},{1,3},{2,0},{3,1},{4,6},{5,7},{6,4},{7,5},{8,10},{9,11},{10,... | collective-permute-start | bytes 1572872 | tf_op jit(solution)/shard_map/ppermute | solution.py:581
  66.1 23.2 %collective-permute-start.5 = (bf16[4,32,2048]{2,1,0:T(8,128)(2,1)S(1)}, bf16[4,32,2048]{2,1,0:T(8,128)(2,1)S(1)}, u32[]{:S(2)}, u32[]{:S(2)}) collective-permute-start(bf16[4,32,2048]{2,1,0:T(8,128)(2,1)S(1)} %pad_maximum_fusion.16), channel_id=1, source_target_pairs={{0,1},{1,0},{2,3},{3,2},{4,5},{5,4},{6,7},{7,6},{8,9},{9,8},{10,11... | collective-permute-start | bytes 1572872 | tf_op jit(solution)/shard_map/ppermute | solution.py:581
  111.5 78.1 %collective-permute-start.13 = (bf16[4,64,1024]{2,1,0:T(8,128)(2,1)}, bf16[4,64,1024]{2,1,0:T(8,128)(2,1)}, u32[]{:S(2)}, u32[]{:S(2)}) collective-permute-start(bf16[4,64,1024]{2,1,0:T(8,128)(2,1)} %pad_maximum_fusion.17), channel_id=1, source_target_pairs={{0,3},{1,2},{2,1},{3,0},{4,7},{5,6},{6,5},{7,4},{8,11},{9,10},{10,... | collective-permute-start | bytes 1572872 | tf_op jit(solution)/shard_map/ppermute | solution.py:581
  113.2 77.1 %collective-permute-start.14 = (bf16[4,64,1024]{2,1,0:T(8,128)(2,1)}, bf16[4,64,1024]{2,1,0:T(8,128)(2,1)}, u32[]{:S(2)}, u32[]{:S(2)}) collective-permute-start(bf16[4,64,1024]{2,1,0:T(8,128)(2,1)} %pad_maximum_fusion.17), channel_id=1, source_target_pairs={{0,2},{1,3},{2,0},{3,1},{4,6},{5,7},{6,4},{7,5},{8,10},{9,11},{10,... | collective-permute-start | bytes 1572872 | tf_op jit(solution)/shard_map/ppermute | solution.py:581
  114.3 77.1 %collective-permute-start.15 = (bf16[4,64,1024]{2,1,0:T(8,128)(2,1)}, bf16[4,64,1024]{2,1,0:T(8,128)(2,1)}, u32[]{:S(2)}, u32[]{:S(2)}) collective-permute-start(bf16[4,64,1024]{2,1,0:T(8,128)(2,1)} %pad_maximum_fusion.17), channel_id=1, source_target_pairs={{0,1},{1,0},{2,3},{3,2},{4,5},{5,4},{6,7},{7,6},{8,9},{9,8},{10,11... | collective-permute-start | bytes 1572872 | tf_op jit(solution)/shard_map/ppermute | solution.py:581
  128.4 11.1 %collective-permute-start.12 = (bf16[1,3,4096]{2,1,0:T(4,128)(2,1)S(1)}, bf16[1,3,4096]{2,1,0:T(4,128)(2,1)S(1)}, u32[]{:S(2)}, u32[]{:S(2)}) collective-permute-start(bf16[1,3,4096]{2,1,0:T(4,128)(2,1)S(1)} %slice.219), channel_id=1, source_target_pairs={{0,1},{1,2},{2,3},{4,5},{5,6},{6,7},{8,9},{9,10},{10,11},{12,13},{... | collective-permute-start | bytes 73736 | tf_op jit(solution)/shard_map/ppermute | solution.py:482
  135.1 58.4 %collective-permute-start.16 = (bf16[4,4,32,2048]{3,2,1,0:T(8,128)(2,1)}, bf16[4,4,32,2048]{3,2,1,0:T(8,128)(2,1)}, u32[]{:S(2)}, u32[]{:S(2)}) collective-permute-start(bf16[4,4,32,2048]{3,2,1,0:T(8,128)(2,1)} %pad_maximum_fusion.9), channel_id=1, source_target_pairs={{0,4},{4,0},{1,5},{5,1},{2,6},{6,2},{3,7},{7,3},{8,12},{12,8},{9,1... | collective-permute-start | bytes 6291464 | tf_op jit(solution)/shard_map/ppermute | solution.py:581
  139.6 64.4 %collective-permute-start.21 = (bf16[4,88,1024]{2,1,0:T(8,128)(2,1)}, bf16[4,88,1024]{2,1,0:T(8,128)(2,1)}, u32[]{:S(2)}, u32[]{:S(2)}) collective-permute-start(bf16[4,88,1024]{2,1,0:T(8,128)(2,1)} %pad_maximum_fusion.12), channel_id=1, source_target_pairs={{0,3},{1,2},{2,1},{3,0},{4,7},{5,6},{6,5},{7,4},{8,11},{9,10},{10,... | collective-permute-start | bytes 2162696 | tf_op jit(solution)/shard_map/ppermute | solution.py:581
  189.6 28.3 %collective-permute-start.22 = (bf16[4,88,1024]{2,1,0:T(8,128)(2,1)S(1)}, bf16[4,88,1024]{2,1,0:T(8,128)(2,1)S(1)}, u32[]{:S(2)}, u32[]{:S(2)}) collective-permute-start(bf16[4,88,1024]{2,1,0:T(8,128)(2,1)S(1)} %copy-done.16), channel_id=1, source_target_pairs={{0,2},{1,3},{2,0},{3,1},{4,6},{5,7},{6,4},{7,5},{8,10},{9,11},{10,... | collective-permute-start | bytes 2162696 | tf_op jit(solution)/shard_map/ppermute | solution.py:581
  190.3 28.2 %collective-permute-start.23 = (bf16[4,88,1024]{2,1,0:T(8,128)(2,1)S(1)}, bf16[4,88,1024]{2,1,0:T(8,128)(2,1)S(1)}, u32[]{:S(2)}, u32[]{:S(2)}) collective-permute-start(bf16[4,88,1024]{2,1,0:T(8,128)(2,1)S(1)} %copy-done.16), channel_id=1, source_target_pairs={{0,1},{1,0},{2,3},{3,2},{4,5},{5,4},{6,7},{7,6},{8,9},{9,8},{10,11... | collective-permute-start | bytes 2162696 | tf_op jit(solution)/shard_map/ppermute | solution.py:581
  193.4 44.7 %collective-permute-start.20 = (bf16[4,4,64,1024]{3,2,1,0:T(8,128)(2,1)S(1)}, bf16[4,4,64,1024]{3,2,1,0:T(8,128)(2,1)S(1)}, u32[]{:S(2)}, u32[]{:S(2)}) collective-permute-start(bf16[4,4,64,1024]{3,2,1,0:T(8,128)(2,1)S(1)} %pad_maximum_fusion.10), channel_id=1, source_target_pairs={{0,4},{4,0},{1,5},{5,1},{2,6},{6,2},{3,7},{7,3},{8,12},{12,8},{9,1... | collective-permute-start | bytes 6291464 | tf_op jit(solution)/shard_map/ppermute | solution.py:581
  200.0 26.9 %collective-permute-start.17 = (bf16[1,8,128,256]{3,2,1,0:T(8,128)(2,1)S(1)}, bf16[1,8,128,256]{3,2,1,0:T(8,128)(2,1)S(1)}, u32[]{:S(2)}, u32[]{:S(2)}) collective-permute-start(bf16[1,8,128,256]{3,2,1,0:T(8,128)(2,1)S(1)} %fusion.47), channel_id=1, source_target_pairs={{0,1},{4,5},{8,9},{12,13},{16,17},{20,21},{24,25},{28,29}} | collective-permute-start | bytes 1572872 | tf_op jit(solution)/shard_map/ppermute | solution.py:676
  203.9 19.5 %collective-permute-start.24 = (bf16[1,8,128,128]{3,2,1,0:T(8,128)(2,1)S(1)}, bf16[1,8,128,128]{3,2,1,0:T(8,128)(2,1)S(1)}, u32[]{:S(2)}, u32[]{:S(2)}) collective-permute-start(bf16[1,8,128,128]{3,2,1,0:T(8,128)(2,1)S(1)} %fusion.101), channel_id=1, source_target_pairs={{1,0},{2,1},{3,2},{5,4},{6,5},{7,6},{9,8},{10,9},{11,10},{13,12},{... | collective-permute-start | bytes 786440 | tf_op jit(solution)/shard_map/ppermute | solution.py:482
  239.9 25.3 %collective-permute-start.26 = (bf16[4,4,88,1024]{3,2,1,0:T(8,128)(2,1)}, bf16[4,4,88,1024]{3,2,1,0:T(8,128)(2,1)}, u32[]{:S(2)}, u32[]{:S(2)}) collective-permute-start(bf16[4,4,88,1024]{3,2,1,0:T(8,128)(2,1)} %pad_maximum_fusion.6), channel_id=1, source_target_pairs={{0,4},{4,0},{1,5},{5,1},{2,6},{6,2},{3,7},{7,3},{8,12},{12,8},{9,1... | collective-permute-start | bytes 8650760 | tf_op jit(solution)/shard_map/ppermute | solution.py:581
  287.6 18.3 %collective-permute-start.27 = (bf16[4,4,32,5632]{3,2,1,0:T(8,128)(2,1)}, bf16[4,4,32,5632]{3,2,1,0:T(8,128)(2,1)S(1)}, u32[]{:S(2)}, u32[]{:S(2)}) collective-permute-start(bf16[4,4,32,5632]{3,2,1,0:T(8,128)(2,1)} %bitcast.470), channel_id=1, source_target_pairs={{0,4},{4,0},{1,5},{5,1},{2,6},{6,2},{3,7},{7,3},{8,12},{12,8},{9,1... | collective-permute-start | bytes 17301512 | tf_op jit(solution)/shard_map/ppermute | solution.py:524
  312.7 360.4 %reduce-scatter.5.cloned.1.call-start = ((), (), s32[]{:S(2)}) async-start(), calls=%async_computation.5 | async-start | bytes 1802240 | tf_op jit(solution)/shard_map/reduce_scatter | solution.py:543
  322.8 13.7 %collective-permute-start.28 = (bf16[4,4,88,1024]{3,2,0,1:T(8,128)(2,1)}, bf16[4,4,88,1024]{3,2,0,1:T(8,128)(2,1)}, u32[]{:S(2)}, u32[]{:S(2)}) collective-permute-start(bf16[4,4,88,1024]{3,2,0,1:T(8,128)(2,1)} %bitcast.423), channel_id=1, source_target_pairs={{0,4},{4,0},{1,5},{5,1},{2,6},{6,2},{3,7},{7,3},{8,12},{12,8},{9,1... | collective-permute-start | bytes 8650760 | tf_op jit(solution)/shard_map/ppermute | solution.py:509
  354.2 34.0 %collective-permute-start.30 = (bf16[1,8,128,256]{3,2,1,0:T(8,128)(2,1)}, bf16[1,8,128,256]{3,2,1,0:T(8,128)(2,1)}, u32[]{:S(2)}, u32[]{:S(2)}) collective-permute-start(bf16[1,8,128,256]{3,2,1,0:T(8,128)(2,1)} %convert_element_type.920), channel_id=1, source_target_pairs={{2,0},{3,1},{6,4},{7,5},{10,8},{11,9},{14,12},{15,13},{18,16},{19,... | collective-permute-start | bytes 1572872 | tf_op jit(solution)/shard_map/ppermute | solution.py:482
  355.4 46.6 %collective-permute-start.29 = (bf16[1,8,128,256]{3,2,1,0:T(8,128)(2,1)}, bf16[1,8,128,256]{3,2,1,0:T(8,128)(2,1)}, u32[]{:S(2)}, u32[]{:S(2)}) collective-permute-start(bf16[1,8,128,256]{3,2,1,0:T(8,128)(2,1)} %convert_element_type.920), channel_id=1, source_target_pairs={{1,0},{2,1},{3,2},{5,4},{6,5},{7,6},{9,8},{10,9},{11,10},{13,12},{... | collective-permute-start | bytes 1572872 | tf_op jit(solution)/shard_map/ppermute | solution.py:482
  356.7 51.1 %collective-permute-start.31 = (bf16[1,8,128,256]{3,2,1,0:T(8,128)(2,1)}, bf16[1,8,128,256]{3,2,1,0:T(8,128)(2,1)}, u32[]{:S(2)}, u32[]{:S(2)}) collective-permute-start(bf16[1,8,128,256]{3,2,1,0:T(8,128)(2,1)} %convert_element_type.920), channel_id=1, source_target_pairs={{3,0},{7,4},{11,8},{15,12},{19,16},{23,20},{27,24},{31,28}} | collective-permute-start | bytes 1572872 | tf_op jit(solution)/shard_map/ppermute | solution.py:482
  363.0 81.9 %collective-permute-start.35 = (bf16[4,4,32,2048]{3,2,0,1:T(8,128)(2,1)}, bf16[4,4,32,2048]{3,2,0,1:T(8,128)(2,1)}, u32[]{:S(2)}, u32[]{:S(2)}) collective-permute-start(bf16[4,4,32,2048]{3,2,0,1:T(8,128)(2,1)} %copy.221), channel_id=1, source_target_pairs={{0,4},{4,0},{1,5},{5,1},{2,6},{6,2},{3,7},{7,3},{8,12},{12,8},{9,1... | collective-permute-start | bytes 6291464 | tf_op jit(solution)/shard_map/ppermute | solution.py:524
  370.0 78.4 %collective-permute-start.36 = (bf16[4,4,64,1024]{3,2,0,1:T(8,128)(2,1)}, bf16[4,4,64,1024]{3,2,0,1:T(8,128)(2,1)}, u32[]{:S(2)}, u32[]{:S(2)}) collective-permute-start(bf16[4,4,64,1024]{3,2,0,1:T(8,128)(2,1)} %bitcast.425), channel_id=1, source_target_pairs={{0,4},{4,0},{1,5},{5,1},{2,6},{6,2},{3,7},{7,3},{8,12},{12,8},{9,1... | collective-permute-start | bytes 6291464 | tf_op jit(solution)/shard_map/ppermute | solution.py:509
  388.2 30.8 %collective-permute-start.32 = (bf16[4,88,1024]{2,1,0:T(8,128)(2,1)S(1)}, bf16[4,88,1024]{2,1,0:T(8,128)(2,1)S(1)}, u32[]{:S(2)}, u32[]{:S(2)}) collective-permute-start(bf16[4,88,1024]{2,1,0:T(8,128)(2,1)S(1)} %get-tuple-element.327), channel_id=1, source_target_pairs={{0,1},{1,0},{2,3},{3,2},{4,5},{5,4},{6,7},{7,6},{8,9},{9,8},{10,11... | collective-permute-start | bytes 2162696 | tf_op jit(solution)/shard_map/ppermute | solution.py:534
  402.1 37.2 %collective-permute-start.33 = (bf16[4,88,1024]{2,1,0:T(8,128)(2,1)S(1)}, bf16[4,88,1024]{2,1,0:T(8,128)(2,1)S(1)}, u32[]{:S(2)}, u32[]{:S(2)}) collective-permute-start(bf16[4,88,1024]{2,1,0:T(8,128)(2,1)S(1)} %get-tuple-element.326), channel_id=1, source_target_pairs={{0,2},{1,3},{2,0},{3,1},{4,6},{5,7},{6,4},{7,5},{8,10},{9,11},{10,... | collective-permute-start | bytes 2162696 | tf_op jit(solution)/shard_map/ppermute | solution.py:534
  407.8 31.5 %collective-permute-start.34 = (bf16[4,88,1024]{2,1,0:T(8,128)(2,1)S(1)}, bf16[4,88,1024]{2,1,0:T(8,128)(2,1)S(1)}, u32[]{:S(2)}, u32[]{:S(2)}) collective-permute-start(bf16[4,88,1024]{2,1,0:T(8,128)(2,1)S(1)} %get-tuple-element.325), channel_id=1, source_target_pairs={{0,3},{1,2},{2,1},{3,0},{4,7},{5,6},{6,5},{7,4},{8,11},{9,10},{10,... | collective-permute-start | bytes 2162696 | tf_op jit(solution)/shard_map/ppermute | solution.py:534
  440.5 13.6 %collective-permute-start.37 = (bf16[88,1024]{1,0:T(8,128)(2,1)S(1)}, bf16[88,1024]{1,0:T(8,128)(2,1)S(1)}, u32[]{:S(2)}, u32[]{:S(2)}) collective-permute-start(bf16[88,1024]{1,0:T(8,128)(2,1)S(1)} %get-tuple-element.357), channel_id=1, source_target_pairs={{0,8},{8,0},{16,24},{24,16},{1,9},{9,1},{17,25},{25,17},{2,10},{10... | collective-permute-start | bytes 540680 | tf_op jit(solution)/shard_map/ppermute | solution.py:534
  442.3 75.5 %collective-permute-start.38 = (bf16[88,1024]{1,0:T(8,128)(2,1)}, bf16[88,1024]{1,0:T(8,128)(2,1)}, u32[]{:S(2)}, u32[]{:S(2)}) collective-permute-start(bf16[88,1024]{1,0:T(8,128)(2,1)} %get-tuple-element.356), channel_id=1, source_target_pairs={{0,16},{8,24},{16,0},{24,8},{1,17},{9,25},{17,1},{25,9},{2,18},{10... | collective-permute-start | bytes 540680 | tf_op jit(solution)/shard_map/ppermute | solution.py:534
  444.8 74.5 %collective-permute-start.39 = (bf16[88,1024]{1,0:T(8,128)(2,1)}, bf16[88,1024]{1,0:T(8,128)(2,1)}, u32[]{:S(2)}, u32[]{:S(2)}) collective-permute-start(bf16[88,1024]{1,0:T(8,128)(2,1)} %get-tuple-element.355), channel_id=1, source_target_pairs={{0,24},{8,16},{16,8},{24,0},{1,25},{9,17},{17,9},{25,1},{2,26},{10... | collective-permute-start | bytes 540680 | tf_op jit(solution)/shard_map/ppermute | solution.py:534
  448.4 71.6 %collective-permute-start.40 = (bf16[4,32,2048]{2,1,0:T(8,128)(2,1)}, bf16[4,32,2048]{2,1,0:T(8,128)(2,1)}, u32[]{:S(2)}, u32[]{:S(2)}) collective-permute-start(bf16[4,32,2048]{2,1,0:T(8,128)(2,1)} %get-tuple-element.347), channel_id=1, source_target_pairs={{0,1},{1,0},{2,3},{3,2},{4,5},{5,4},{6,7},{7,6},{8,9},{9,8},{10,11... | collective-permute-start | bytes 1572872 | tf_op jit(solution)/shard_map/ppermute | solution.py:534
  449.9 71.6 %collective-permute-start.41 = (bf16[4,32,2048]{2,1,0:T(8,128)(2,1)}, bf16[4,32,2048]{2,1,0:T(8,128)(2,1)}, u32[]{:S(2)}, u32[]{:S(2)}) collective-permute-start(bf16[4,32,2048]{2,1,0:T(8,128)(2,1)} %get-tuple-element.346), channel_id=1, source_target_pairs={{0,2},{1,3},{2,0},{3,1},{4,6},{5,7},{6,4},{7,5},{8,10},{9,11},{10,... | collective-permute-start | bytes 1572872 | tf_op jit(solution)/shard_map/ppermute | solution.py:534
  454.1 67.3 %collective-permute-start.42 = (bf16[4,32,2048]{2,1,0:T(8,128)(2,1)}, bf16[4,32,2048]{2,1,0:T(8,128)(2,1)}, u32[]{:S(2)}, u32[]{:S(2)}) collective-permute-start(bf16[4,32,2048]{2,1,0:T(8,128)(2,1)} %get-tuple-element.345), channel_id=1, source_target_pairs={{0,3},{1,2},{2,1},{3,0},{4,7},{5,6},{6,5},{7,4},{8,11},{9,10},{10,... | collective-permute-start | bytes 1572872 | tf_op jit(solution)/shard_map/ppermute | solution.py:534
  517.8 15.7 %collective-permute-start.43 = (bf16[4,64,1024]{2,1,0:T(8,128)(2,1)}, bf16[4,64,1024]{2,1,0:T(8,128)(2,1)}, u32[]{:S(2)}, u32[]{:S(2)}) collective-permute-start(bf16[4,64,1024]{2,1,0:T(8,128)(2,1)} %get-tuple-element.343), channel_id=1, source_target_pairs={{0,1},{1,0},{2,3},{3,2},{4,5},{5,4},{6,7},{7,6},{8,9},{9,8},{10,11... | collective-permute-start | bytes 1572872 | tf_op jit(solution)/shard_map/ppermute | solution.py:534
  519.4 22.8 %collective-permute-start.44 = (bf16[4,64,1024]{2,1,0:T(8,128)(2,1)}, bf16[4,64,1024]{2,1,0:T(8,128)(2,1)}, u32[]{:S(2)}, u32[]{:S(2)}) collective-permute-start(bf16[4,64,1024]{2,1,0:T(8,128)(2,1)} %get-tuple-element.342), channel_id=1, source_target_pairs={{0,2},{1,3},{2,0},{3,1},{4,6},{5,7},{6,4},{7,5},{8,10},{9,11},{10,... | collective-permute-start | bytes 1572872 | tf_op jit(solution)/shard_map/ppermute | solution.py:534
  520.0 22.2 %collective-permute-start.45 = (bf16[4,64,1024]{2,1,0:T(8,128)(2,1)}, bf16[4,64,1024]{2,1,0:T(8,128)(2,1)}, u32[]{:S(2)}, u32[]{:S(2)}) collective-permute-start(bf16[4,64,1024]{2,1,0:T(8,128)(2,1)} %get-tuple-element.341), channel_id=1, source_target_pairs={{0,3},{1,2},{2,1},{3,0},{4,7},{5,6},{6,5},{7,4},{8,11},{9,10},{10,... | collective-permute-start | bytes 1572872 | tf_op jit(solution)/shard_map/ppermute | solution.py:534
  528.7 13.5 %collective-permute-start.74 = (f32[8,128]{1,0:T(8,128)S(1)}, f32[8,128]{1,0:T(8,128)S(1)}, u32[]{:S(2)}, u32[]{:S(2)}) collective-permute-start(f32[8,128]{1,0:T(8,128)S(1)} %select_maximum_fusion), channel_id=1, source_target_pairs={{0,4},{4,0},{1,5},{5,1},{2,6},{6,2},{3,7},{7,3},{8,12},{12,8},{9,1... | collective-permute-start | bytes 12296 | tf_op jit(solution)/shard_map/ppermute | solution.py:568
  549.3 41.9 %collective-permute-start.71 = (bf16[64,1024]{1,0:T(8,128)(2,1)}, bf16[64,1024]{1,0:T(8,128)(2,1)}, u32[]{:S(2)}, u32[]{:S(2)}) collective-permute-start(bf16[64,1024]{1,0:T(8,128)(2,1)} %get-tuple-element.366), channel_id=1, source_target_pairs={{0,8},{8,0},{16,24},{24,16},{1,9},{9,1},{17,25},{25,17},{2,10},{10... | collective-permute-start | bytes 393224 | tf_op jit(solution)/shard_map/ppermute | solution.py:534
  558.2 13.8 %collective-permute-start.78 = (f32[8,128]{1,0:T(8,128)S(1)}, f32[8,128]{1,0:T(8,128)S(1)}, u32[]{:S(2)}, u32[]{:S(2)}) collective-permute-start(f32[8,128]{1,0:T(8,128)S(1)} %add.1150), channel_id=1, source_target_pairs={{0,16},{8,24},{16,0},{24,8},{1,17},{9,25},{17,1},{25,9},{2,18},{10... | collective-permute-start | bytes 12296 | tf_op jit(solution)/shard_map/ppermute | solution.py:568
  569.9 17.3 %collective-permute-start.73 = (bf16[64,1024]{1,0:T(8,128)(2,1)}, bf16[64,1024]{1,0:T(8,128)(2,1)S(1)}, u32[]{:S(2)}, u32[]{:S(2)}) collective-permute-start(bf16[64,1024]{1,0:T(8,128)(2,1)} %get-tuple-element.367), channel_id=1, source_target_pairs={{0,24},{8,16},{16,8},{24,0},{1,25},{9,17},{17,9},{25,1},{2,26},{10... | collective-permute-start | bytes 393224 | tf_op jit(solution)/shard_map/ppermute | solution.py:534
  570.2 19.3 %collective-permute-start.72 = (bf16[64,1024]{1,0:T(8,128)(2,1)}, bf16[64,1024]{1,0:T(8,128)(2,1)S(1)}, u32[]{:S(2)}, u32[]{:S(2)}) collective-permute-start(bf16[64,1024]{1,0:T(8,128)(2,1)} %get-tuple-element.368), channel_id=1, source_target_pairs={{0,16},{8,24},{16,0},{24,8},{1,17},{9,25},{17,1},{25,9},{2,18},{10... | collective-permute-start | bytes 393224 | tf_op jit(solution)/shard_map/ppermute | solution.py:534
  578.1 27.3 %collective-permute-start.47 = (bf16[4,4,32,2048]{3,2,1,0:T(8,128)(2,1)S(1)}, bf16[4,4,32,2048]{3,2,1,0:T(8,128)(2,1)S(1)}, u32[]{:S(2)}, u32[]{:S(2)}) collective-permute-start(bf16[4,4,32,2048]{3,2,1,0:T(8,128)(2,1)S(1)} %bitcast.471), channel_id=1, source_target_pairs={{0,4},{4,0},{1,5},{5,1},{2,6},{6,2},{3,7},{7,3},{8,12},{12,8},{9,1... | collective-permute-start | bytes 6291464 | tf_op jit(solution)/shard_map/ppermute | solution.py:524
  582.6 29.4 %collective-permute-start.48 = (bf16[4,4,32,2176]{3,2,1,0:T(8,128)(2,1)S(1)}, bf16[4,4,32,2176]{3,2,1,0:T(8,128)(2,1)S(1)}, u32[]{:S(2)}, u32[]{:S(2)}) collective-permute-start(bf16[4,4,32,2176]{3,2,1,0:T(8,128)(2,1)S(1)} %pad_maximum_fusion.8), channel_id=1, source_target_pairs={{0,4},{4,0},{1,5},{5,1},{2,6},{6,2},{3,7},{7,3},{8,12},{12,8},{9,1... | collective-permute-start | bytes 6684680 | tf_op jit(solution)/shard_map/ppermute | solution.py:524
  589.4 14.1 %collective-permute-start.69 = (bf16[32,2048]{1,0:T(8,128)(2,1)S(1)}, bf16[32,2048]{1,0:T(8,128)(2,1)S(1)}, u32[]{:S(2)}, u32[]{:S(2)}) collective-permute-start(bf16[32,2048]{1,0:T(8,128)(2,1)S(1)} %copy-done.61), channel_id=1, source_target_pairs={{0,16},{8,24},{16,0},{24,8},{1,17},{9,25},{17,1},{25,9},{2,18},{10... | collective-permute-start | bytes 393224 | tf_op jit(solution)/shard_map/ppermute | solution.py:534
  591.2 12.3 %collective-permute-start.68 = (bf16[32,2048]{1,0:T(8,128)(2,1)S(1)}, bf16[32,2048]{1,0:T(8,128)(2,1)S(1)}, u32[]{:S(2)}, u32[]{:S(2)}) collective-permute-start(bf16[32,2048]{1,0:T(8,128)(2,1)S(1)} %copy-done.60), channel_id=1, source_target_pairs={{0,8},{8,0},{16,24},{24,16},{1,9},{9,1},{17,25},{25,17},{2,10},{10... | collective-permute-start | bytes 393224 | tf_op jit(solution)/shard_map/ppermute | solution.py:534
  607.2 44.3 %collective-permute-start.56 = (bf16[4,32,2048]{2,1,0:T(8,128)(2,1)}, bf16[4,32,2048]{2,1,0:T(8,128)(2,1)}, u32[]{:S(2)}, u32[]{:S(2)}) collective-permute-start(bf16[4,32,2048]{2,1,0:T(8,128)(2,1)} %get-tuple-element.339), channel_id=1, source_target_pairs={{0,8},{8,0},{16,24},{24,16},{1,9},{9,1},{17,25},{25,17},{2,10},{10... | collective-permute-start | bytes 1572872 | tf_op jit(solution)/shard_map/ppermute | solution.py:534
  607.2 46.4 %collective-permute-start.57 = (bf16[4,32,2048]{2,1,0:T(8,128)(2,1)}, bf16[4,32,2048]{2,1,0:T(8,128)(2,1)}, u32[]{:S(2)}, u32[]{:S(2)}) collective-permute-start(bf16[4,32,2048]{2,1,0:T(8,128)(2,1)} %get-tuple-element.338), channel_id=1, source_target_pairs={{0,16},{8,24},{16,0},{24,8},{1,17},{9,25},{17,1},{25,9},{2,18},{10... | collective-permute-start | bytes 1572872 | tf_op jit(solution)/shard_map/ppermute | solution.py:534
  608.9 46.0 %collective-permute-start.58 = (bf16[4,32,2048]{2,1,0:T(8,128)(2,1)}, bf16[4,32,2048]{2,1,0:T(8,128)(2,1)}, u32[]{:S(2)}, u32[]{:S(2)}) collective-permute-start(bf16[4,32,2048]{2,1,0:T(8,128)(2,1)} %get-tuple-element.337), channel_id=1, source_target_pairs={{0,24},{8,16},{16,8},{24,0},{1,25},{9,17},{17,9},{25,1},{2,26},{10... | collective-permute-start | bytes 1572872 | tf_op jit(solution)/shard_map/ppermute | solution.py:534
  613.8 15.0 %collective-permute-start.50 = (bf16[4,32,2176]{2,1,0:T(8,128)(2,1)}, bf16[4,32,2176]{2,1,0:T(8,128)(2,1)}, u32[]{:S(2)}, u32[]{:S(2)}) collective-permute-start(bf16[4,32,2176]{2,1,0:T(8,128)(2,1)} %get-tuple-element.335), channel_id=1, source_target_pairs={{0,1},{1,0},{2,3},{3,2},{4,5},{5,4},{6,7},{7,6},{8,9},{9,8},{10,11... | collective-permute-start | bytes 1671176 | tf_op jit(solution)/shard_map/ppermute | solution.py:534
  621.7 27.0 %collective-permute-start.51 = (bf16[4,32,2176]{2,1,0:T(8,128)(2,1)}, bf16[4,32,2176]{2,1,0:T(8,128)(2,1)S(1)}, u32[]{:S(2)}, u32[]{:S(2)}) collective-permute-start(bf16[4,32,2176]{2,1,0:T(8,128)(2,1)} %get-tuple-element.334), channel_id=1, source_target_pairs={{0,2},{1,3},{2,0},{3,1},{4,6},{5,7},{6,4},{7,5},{8,10},{9,11},{10,... | collective-permute-start | bytes 1671176 | tf_op jit(solution)/shard_map/ppermute | solution.py:534
  628.7 20.0 %collective-permute-start.52 = (bf16[4,32,2176]{2,1,0:T(8,128)(2,1)}, bf16[4,32,2176]{2,1,0:T(8,128)(2,1)S(1)}, u32[]{:S(2)}, u32[]{:S(2)}) collective-permute-start(bf16[4,32,2176]{2,1,0:T(8,128)(2,1)} %get-tuple-element.333), channel_id=1, source_target_pairs={{0,3},{1,2},{2,1},{3,0},{4,7},{5,6},{6,5},{7,4},{8,11},{9,10},{10,... | collective-permute-start | bytes 1671176 | tf_op jit(solution)/shard_map/ppermute | solution.py:534
  653.6 24.6 %collective-permute-start.67 = (bf16[32,2176]{1,0:T(8,128)(2,1)S(1)}, bf16[32,2176]{1,0:T(8,128)(2,1)S(1)}, u32[]{:S(2)}, u32[]{:S(2)}) collective-permute-start(bf16[32,2176]{1,0:T(8,128)(2,1)S(1)} %get-tuple-element.364), channel_id=1, source_target_pairs={{0,24},{8,16},{16,8},{24,0},{1,25},{9,17},{17,9},{25,1},{2,26},{10... | collective-permute-start | bytes 417800 | tf_op jit(solution)/shard_map/ppermute | solution.py:534
  654.9 23.4 %collective-permute-start.66 = (bf16[32,2176]{1,0:T(8,128)(2,1)S(1)}, bf16[32,2176]{1,0:T(8,128)(2,1)S(1)}, u32[]{:S(2)}, u32[]{:S(2)}) collective-permute-start(bf16[32,2176]{1,0:T(8,128)(2,1)S(1)} %get-tuple-element.365), channel_id=1, source_target_pairs={{0,16},{8,24},{16,0},{24,8},{1,17},{9,25},{17,1},{25,9},{2,18},{10... | collective-permute-start | bytes 417800 | tf_op jit(solution)/shard_map/ppermute | solution.py:534
  660.0 11.6 %collective-permute-start.59 = (f32[1,32]{1,0:T(1,128)S(1)}, f32[1,32]{1,0:T(1,128)S(1)}, u32[]{:S(2)}, u32[]{:S(2)}) collective-permute-start(f32[1,32]{1,0:T(1,128)S(1)} %get-tuple-element.428), channel_id=1, source_target_pairs={{0,8},{8,0},{16,24},{24,16},{1,9},{9,1},{17,25},{25,17},{2,10},{10... | collective-permute-start | bytes 392 | tf_op jit(solution)/shard_map/ppermute | solution.py:534
  (123 other events, 2012.9 us)
Sparse Core Ops, SparseCore 0:
  13.2 98.2 all-gather.2
  114.9 116.6 all-gather.4
  312.8 123.3 reduce-scatter.2
  550.2 30.5 reduce-scatter.4

commit v3 on v2

--- a/solution.py
+++ b/solution.py
@@ -712,8 +712,6 @@
     grad_gain_feed, grad_norm_two = norm_back(grad_second, normed_two, inverse_two, gain_second)
     grad_middle = grad_branch.astype(F32) + grad_norm_two
     grad_mixer_out = grad_middle.astype(BF)
-    grad_mixer_out = sum_down.tied(grad_mixer_out)
-    sum_down.direct(SEQ)
     grad_gated = product_right(grad_mixer_out, output_matrix)
     grad_mixed, grad_outgate, gain_parts, flow = unfinish(
         grad_gated, mixed, outgate, heads_gain, reading, seqs, piece
@@ -730,7 +728,7 @@
     sum_outgate = Sum.of_product(first_halves, grad_outgate)
     sum_output = Sum.of_rows(product_left(gated, grad_mixer_out).astype(BF))
     leaving = sum_feed.tied(sum_output.tied(sum_outgate.tied(sum_down.tied(leaving.astype(BF)))))
-    sum_down.direct("z")
+    sum_down.direct(SEQ)
     sum_outgate.direct(SEQ)
     sum_output.direct(SEQ)
     sum_feed.reduce(SEQ)
@@ -739,6 +737,7 @@
         projected, edges, taps, beta_rows, decay_rows, inverse, states, incoming, grad_mixed, leaving, seqs, piece
     )
     outs = sum_outgate.tied(*sum_down.tied(*outs))
+    sum_down.direct("z")
     sum_outgate.direct("z")
     grad_edges = jnp.concatenate(outs[3:6], axis=1).reshape(seqs, 8, channels)[:, 9 - CONV :]
     returned = shift(grad_edges.astype(BF), -1)

time: 700 us -> 697 us (level)
  waiting for transfers between devices: 153 us -> 190 us
  starting transfers between devices: 136 us -> 120 us
  local copies, waits for them, and re-layouts: 56 us -> 43 us
  other arithmetic: 86.4 us -> 76.6 us
    ppermute x7, waiting for transfers between devices: 9.76 us -> 49.2 us  [shift(): lax.ppermute(block, SEQ, [(i - distance, i) for i in devices if i - dista...]
    ppermute x36, starting transfers between devices: 72.2 us -> 55 us  [direct(): lax.ppermute(share(partner), axis, pairs)]
    ppermute x36, waiting for transfers between devices: 65 us -> 55.9 us  [direct(): lax.ppermute(share(partner), axis, pairs)]
    ppermute x5, waiting for transfers between devices: 1.57 us -> 8.58 us  [everywhere(): lax.ppermute(total, axis, [(i, i ^ away) for i in range(size)])]
  transfers between devices with their start and end apart: 83 -> 83, of which waited for: 25 -> 27; matrix products, arithmetic and copies ran while one was open for 31% -> 27% of each run, Pallas kernels for 18% -> 18%
where the time goes in v3:
time: 697 us; the launch traced here: 690 us
  waiting for transfers between devices  190 us (27%)
  Pallas kernels  127 us (18%)
  starting transfers between devices  120 us (17%)
  matrix products  117 us (17%)
  other arithmetic  76.6 us (11%)
  local copies, waits for them, and re-layouts  43 us (6%)
  between operations  16.2 us (2%)
    pallas_call x1, Pallas kernels, close_rule(): pl.pallas_call(functools.partial(closing_kernel, piece), grid=(steps, seq...  62.5 us
    ppermute x36, waiting for transfers between devices, direct(): lax.ppermute(share(partner), axis, pairs)  55.9 us
    ppermute x36, starting transfers between devices, direct(): lax.ppermute(share(partner), axis, pairs)  55 us
    ppermute x21, waiting for transfers between devices, along(): came = [lax.ppermute(held, axis, pairs) for pairs, _ in partners(axis)]  54 us
    ppermute x7, waiting for transfers between devices, shift(): lax.ppermute(block, SEQ, [(i - distance, i) for i in devices if i - dista...  49.2 us
    pallas_call x1, Pallas kernels, open_rule(): pl.pallas_call(functools.partial(opening_kernel, piece), grid=(HEADS // P...  46.3 us
    ppermute x21, starting transfers between devices, along(): came = [lax.ppermute(held, axis, pairs) for pairs, _ in partners(axis)]  39.5 us
    dot_general x7, matrix products, product_right(): lax.dot_general(left, right, (((1,), (1,)), ((), ())), preferred_element_...  36.8 us
  transfers between devices with their start and end apart: 83, of which 27 were waited for; matrix products, arithmetic and copies ran while one was open for 27% of the time, Pallas kernels for 18%

profile of v3, /device:TPU:0, one launch (start us, length us, event | category | flops | bytes accessed | tf_op | source)
XLA Modules:
  0.0 690.0 jit_solution(4811201071846479782)
XLA Ops:
  15.0 5.1 collective-permute-start
  20.8 3.7 collective-permute-start.6
  24.9 9.7 %collective-permute-start.8 = (bf16[64,1024]{1,0:T(8,128)(2,1)S(1)}, bf16[64,1024]{1,0:T(8,128)(2,1)S(1)}, u32[]{:S(2)}, u32[]{:S(2)}) collective-permute-start(bf16[64,1024]{1,0:T(8,128)(2,1)S(1)} %copy-done.71), channel_id=1, source_target_pairs={{0,8},{8,0},{16,24},{24,16},{1,9},{9,1},{17,25},{25,17},{2,10},{10... | collective-permute-start | bytes 393224 | tf_op jit(solution)/shard_map/ppermute | solution.py:581
  34.6 9.2 %collective-permute-done.1 = bf16[32,2048]{1,0:T(8,128)(2,1)S(1)} collective-permute-done((bf16[32,2048]{1,0:T(8,128)(2,1)}, bf16[32,2048]{1,0:T(8,128)(2,1)S(1)}, u32[]{:S(2)}, u32[]{:S(2)}) %collective-permute-start.1) | collective-permute-done | bytes 131104 | tf_op jit(solution)/shard_map/ppermute | solution.py:581
  43.8 2.9 collective-permute-start.9
  46.9 5.4 collective-permute-start.11
  52.3 10.7 %collective-permute-done.7 = bf16[64,1024]{1,0:T(8,128)(2,1)S(1)} collective-permute-done((bf16[64,1024]{1,0:T(8,128)(2,1)}, bf16[64,1024]{1,0:T(8,128)(2,1)S(1)}, u32[]{:S(2)}, u32[]{:S(2)}) %collective-permute-start.7) | collective-permute-done | bytes 131104 | tf_op jit(solution)/shard_map/ppermute | solution.py:581
  63.0 2.5 collective-permute-start.3
  67.5 8.0 %collective-permute-done.10 = bf16[88,1024]{1,0:T(8,128)(2,1)S(1)} collective-permute-done((bf16[88,1024]{1,0:T(8,128)(2,1)S(1)}, bf16[88,1024]{1,0:T(8,128)(2,1)S(1)}, u32[]{:S(2)}, u32[]{:S(2)}) %collective-permute-start.10) | collective-permute-done | bytes 180256 | tf_op jit(solution)/shard_map/ppermute | solution.py:581
  77.4 10.7 %collective-permute-done.4 = bf16[4,32,2048]{2,1,0:T(8,128)(2,1)S(1)} collective-permute-done((bf16[4,32,2048]{2,1,0:T(8,128)(2,1)S(1)}, bf16[4,32,2048]{2,1,0:T(8,128)(2,1)S(1)}, u32[]{:S(2)}, u32[]{:S(2)}) %collective-permute-start.4) | collective-permute-done | bytes 524320 | tf_op jit(solution)/shard_map/ppermute | solution.py:581
  91.2 20.3 %all-gather.3.cloned.1.call-done = bf16[1024,4224]{1,0:T(8,128)(2,1)} async-done(((bf16[32,4224]{1,0:T(8,128)(2,1)}), bf16[1024,4224]{1,0:T(8,128)(2,1)}) %all-gather.3.cloned.1.call-update) | async-done | bytes 8650768 | tf_op jit(solution)/shard_map/all_gather | solution.py:629
  117.9 8.1 %fusion.2.q_ref.k_ref.v_ref = bf16[512,4096]{1,0:T(8,128)(2,1)S(1)} fusion(bf16[512,1024]{1,0:T(8,128)(2,1)S(1)} %fusion.28, bf16[1024,4224]{1,0:T(8,128)(2,1)} %all-gather.3.cloned.1.call-done), kind=kOutput, calls=%fused_computation.5 | convolution fusion | flops 4297064448 | bytes 13631488 | tf_op jit(solution)/shard_map/dot_general | solution.py:457
  127.9 3.2 collective-permute-start.12
  139.6 3.0 collective-permute-start.21
  143.3 46.3 %open_rule.1 = (f32[512,2048]{1,0:T(8,128)}, f32[512,1024]{1,0:T(8,128)}, f32[1,8,4,128,384]{4,3,2,1,0:T(8,128)}, f32[512,1024]{1,0:T(8,128)}) custom-call(bf16[512,4096]{1,0:T(8,128)(2,1)} %copy-done.87, bf16[512,4096]{1,0:T(8,128)(2,1)} %copy-done.87, bf16[512,4096]{1,0:T(8,128)(2,1)} %copy-done.87, f32[8,4096]{1,0:T(8,128)} %bitcast_convert_fusion.qe_ref.ke_ref.ve_ref, ...), custom_call_target="tpu_custom_call" | custom-call | flops 30000001024 | bytes 20971520 | tf_op jit(solution)/shard_map/open_rule/pallas_call | solution.py:369
  197.0 2.9 fusion.47
  200.0 2.8 collective-permute-start.17
  205.2 12.7 %collective-permute-done.22 = bf16[4,88,1024]{2,1,0:T(8,128)(2,1)S(1)} collective-permute-done((bf16[4,88,1024]{2,1,0:T(8,128)(2,1)S(1)}, bf16[4,88,1024]{2,1,0:T(8,128)(2,1)S(1)}, u32[]{:S(2)}, u32[]{:S(2)}) %collective-permute-start.22) | collective-permute-done | bytes 720928 | tf_op jit(solution)/shard_map/ppermute | solution.py:581
  220.7 2.8 collective-permute-done.24
  229.9 4.5 fusion.50.outgate_ref
  238.5 2.3 pad_maximum_fusion.3
  242.4 8.1 %finish_heads.1 = (f32[512,2048]{1,0:T(8,128)}, bf16[512,2048]{1,0:T(8,128)(2,1)}) custom-call(f32[512,2048]{1,0:T(8,128)} %get-tuple-element.125.local_ref, f32[512,1024]{1,0:T(8,128)} %get-tuple-element.126.reading_ref, bf16[1,8,128,256]{3,2,1,0:T(8,128)(2,1)} %add.976.incoming_ref, f32[512,2048]{1,0:T(8,128)} %fusion.50.outgate_ref, ...), custom_call_target="tpu_custom_call" | custom-call | tf_op jit(solution)/shard_map/finish_heads/pallas_call | solution.py:390
  250.5 5.3 multiply_reduce_fusion.2
  258.0 6.2 fusion.10
  264.5 4.9 fusion.14
  269.4 3.1 select_bitcast_fusion.1
  273.8 9.8 %fusion.6 = (bf16[512,2816]{1,0:T(8,128)(2,1)S(1)}, bf16[512,2816]{1,0:T(8,128)(2,1)S(1)}, bf16[512,2816]{1,0:T(8,128)(2,1)}) fusion(f32[512,2816]{1,0:T(8,128)S(1)} %fusion.10, f32[512,2816]{1,0:T(8,128)} %fusion.14, bf16[2816,1024]{1,0:T(8,128)(2,1)S(1)} %bitcast.427, bf16[1,512,1024]{2,1,0:T(8,128)(2,1)S(1)} %copy-done.23), kind=kOutput, calls=%fused_computation.11 | convolution fusion | flops 2972975104 | bytes 27000832 | tf_op jit(solution)/shard_map/dot_general | solution.py:465
  283.6 5.6 convolution_convert_fusion
  289.9 8.6 %convolution_convert_fusion.1 = bf16[512,5632]{1,0:T(8,128)(2,1)} fusion(bf16[512,2816]{1,0:T(8,128)(2,1)} %copy-done.95, bf16[512,2816]{1,0:T(8,128)(2,1)} %copy-done.93, pred[]{:T(512)S(6)} %eq.29, bf16[512,128]{1,0:T(8,128)(2,1)S(1)} %copy-done.63, bf16[512,128]{1,0:T(8,128)(2,1)S(1)} %copy-done.64, bf16[512,128]{1,0:T(8,128)(2,1)S(1)} %copy-done.65, ...), kind=kOutput, calls=%fused_computation.2 | convolution fusion | flops 2971664384 | bytes 12582913 | tf_op jit(solution)/shard_map/dot_general | solution.py:461
  298.5 5.1 fusion.8
  303.7 4.6 fusion.38
  308.2 6.8 add_convert_fusion
  315.7 5.6 convolution_convert_fusion.2
  327.6 4.3 fusion.92.grad_ref
  332.0 10.2 %unfinish_heads.1 = (f32[512,2048]{1,0:T(8,128)}, bf16[512,2048]{1,0:T(8,128)(2,1)}, f32[1,8,8,256]{3,2,1,0:T(8,128)}, f32[1,8,128,256]{3,2,1,0:T(8,128)}) custom-call(f32[512,2048]{1,0:T(8,128)} %fusion.92.grad_ref, f32[512,2048]{1,0:T(8,128)} %get-tuple-element.142.mixed_ref, f32[512,2048]{1,0:T(8,128)} %fusion.50.outgate_ref, ...), custom_call_target="tpu_custom_call" | custom-call | tf_op jit(solution)/shard_map/unfinish_heads/pallas_call | solution.py:406
  342.1 4.8 convolution_convert_fusion.3
  353.7 4.2 fusion.41
  364.6 6.7 fusion.197
  371.3 22.0 %collective-permute-done.29 = bf16[1,8,128,256]{3,2,1,0:T(8,128)(2,1)} collective-permute-done((bf16[1,8,128,256]{3,2,1,0:T(8,128)(2,1)}, bf16[1,8,128,256]{3,2,1,0:T(8,128)(2,1)}, u32[]{:S(2)}, u32[]{:S(2)}) %collective-permute-start.29) | collective-permute-done | bytes 524320 | tf_op jit(solution)/shard_map/ppermute | solution.py:482
  397.6 22.1 %collective-permute-done.30 = bf16[1,8,128,256]{3,2,1,0:T(8,128)(2,1)S(1)} collective-permute-done((bf16[1,8,128,256]{3,2,1,0:T(8,128)(2,1)}, bf16[1,8,128,256]{3,2,1,0:T(8,128)(2,1)S(1)}, u32[]{:S(2)}, u32[]{:S(2)}) %collective-permute-start.30) | collective-permute-done | bytes 524320 | tf_op jit(solution)/shard_map/ppermute | solution.py:482
  421.9 4.3 fusion.60
  426.5 3.3 collective-permute-start.36
  429.8 3.5 fusion.69
  433.8 3.5 fusion.73
  437.4 8.2 %collective-permute-done.34 = bf16[4,88,1024]{2,1,0:T(8,128)(2,1)} collective-permute-done((bf16[4,88,1024]{2,1,0:T(8,128)(2,1)}, bf16[4,88,1024]{2,1,0:T(8,128)(2,1)}, u32[]{:S(2)}, u32[]{:S(2)}) %collective-permute-start.34) | collective-permute-done | bytes 720928 | tf_op jit(solution)/shard_map/ppermute | solution.py:534
  445.6 62.5 %close_rule.1 = (bf16[512,1024]{1,0:T(8,128)(2,1)}, bf16[512,1024]{1,0:T(8,128)(2,1)}, bf16[512,2048]{1,0:T(8,128)(2,1)}, f32[8,1024]{1,0:T(8,128)}, f32[8,1024]...) custom-call(bf16[512,4096]{1,0:T(8,128)(2,1)} %copy-done.87, ...), custom_call_target="tpu_custom_call" | custom-call | flops 44999999488 | bytes 31457280 | tf_op jit(solution)/shard_map/close_rule/pallas_call | solution.py:431
  508.2 3.5 collective-permute-start.41
  519.1 2.6 collective-permute-start.75
  523.2 7.4 %collective-permute-done.75 = f32[8,128]{1,0:T(8,128)S(1)} collective-permute-done((f32[8,128]{1,0:T(8,128)}, f32[8,128]{1,0:T(8,128)S(1)}, u32[]{:S(2)}, u32[]{:S(2)}) %collective-permute-start.75) | collective-permute-done | bytes 4128 | tf_op jit(solution)/shard_map/ppermute | solution.py:568
  532.4 2.3 fusion.137
  536.5 2.6 fusion.125
  540.9 2.4 collective-permute-start.67
  558.9 2.4 fusion.19
  562.6 2.6 collective-permute-start.70
  570.9 2.6 collective-permute-start.73
  573.5 10.2 %collective-permute-done.69 = bf16[64,1024]{1,0:T(8,128)(2,1)S(1)} collective-permute-done((bf16[64,1024]{1,0:T(8,128)(2,1)S(1)}, bf16[64,1024]{1,0:T(8,128)(2,1)S(1)}, u32[]{:S(2)}, u32[]{:S(2)}) %collective-permute-start.69) | collective-permute-done | bytes 131104 | tf_op jit(solution)/shard_map/ppermute | solution.py:534
  585.7 6.5 collective-permute-done.72
  600.5 4.0 fusion.34
  608.8 6.2 collective-permute-done.47
  616.4 4.2 fusion.33
  620.6 11.2 %collective-permute-done.48 = bf16[4,32,2176]{2,1,0:T(8,128)(2,1)S(1)} collective-permute-done((bf16[4,32,2176]{2,1,0:T(8,128)(2,1)}, bf16[4,32,2176]{2,1,0:T(8,128)(2,1)S(1)}, u32[]{:S(2)}, u32[]{:S(2)}) %collective-permute-start.48) | collective-permute-done | bytes 557088 | tf_op jit(solution)/shard_map/ppermute | solution.py:534
  636.7 8.4 %collective-permute-done.54 = bf16[4,32,2048]{2,1,0:T(8,128)(2,1)S(1)} collective-permute-done((bf16[4,32,2048]{2,1,0:T(8,128)(2,1)}, bf16[4,32,2048]{2,1,0:T(8,128)(2,1)S(1)}, u32[]{:S(2)}, u32[]{:S(2)}) %collective-permute-start.54) | collective-permute-done | bytes 524320 | tf_op jit(solution)/shard_map/ppermute | solution.py:534
  646.6 13.3 %collective-permute-start.63 = (bf16[32,2176]{1,0:T(8,128)(2,1)S(1)}, bf16[32,2176]{1,0:T(8,128)(2,1)S(1)}, u32[]{:S(2)}, u32[]{:S(2)}) collective-permute-start(bf16[32,2176]{1,0:T(8,128)(2,1)S(1)} %get-tuple-element.354), channel_id=1, source_target_pairs={{0,16},{8,24},{16,0},{24,8},{1,17},{9,25},{17,1},{25,9},{2,18},{10... | collective-permute-start | bytes 417800 | tf_op jit(solution)/shard_map/ppermute | solution.py:534
  659.9 2.5 collective-permute-start.58
  (491 shorter events, 168.5 us)
Async XLA Ops:
  7.2 104.3 %all-gather.3.cloned.1.call-start = ((), (), s32[]{:S(2)}) async-start(), calls=%async_computation.2 | async-start | bytes 8921088 | tf_op jit(solution)/shard_map/all_gather | solution.py:629
  13.1 244.8 %all-gather.5.cloned.1.call-start = ((), (), s32[]{:S(2)}) async-start(), calls=%async_computation.3 | async-start | bytes 11894784 | tf_op jit(solution)/shard_map/all_gather | solution.py:630
  15.0 422.4 %reduce-scatter.3.cloned.1.call-start = ((), (), s32[]{:S(2)}) async-start(), calls=%async_computation.4 | async-start | bytes 7208960 | tf_op jit(solution)/shard_map/reduce_scatter | solution.py:543
  20.1 23.7 %collective-permute-start.1 = (bf16[32,2048]{1,0:T(8,128)(2,1)}, bf16[32,2048]{1,0:T(8,128)(2,1)S(1)}, u32[]{:S(2)}, u32[]{:S(2)}) collective-permute-start(bf16[32,2048]{1,0:T(8,128)(2,1)} %param.21), channel_id=1, source_target_pairs={{0,16},{8,24},{16,0},{24,8},{1,17},{9,25},{17,1},{25,9},{2,18},{10... | collective-permute-start | bytes 393224 | tf_op jit(solution)/shard_map/ppermute | solution.py:581
  20.1 26.6 %collective-permute-start.2 = (bf16[32,2048]{1,0:T(8,128)(2,1)}, bf16[32,2048]{1,0:T(8,128)(2,1)S(1)}, u32[]{:S(2)}, u32[]{:S(2)}) collective-permute-start(bf16[32,2048]{1,0:T(8,128)(2,1)} %param.21), channel_id=1, source_target_pairs={{0,8},{8,0},{16,24},{24,16},{1,9},{9,1},{17,25},{25,17},{2,10},{10... | collective-permute-start | bytes 393224 | tf_op jit(solution)/shard_map/ppermute | solution.py:581
  20.8 26.1 %collective-permute-start.6 = (bf16[64,1024]{1,0:T(8,128)(2,1)}, bf16[64,1024]{1,0:T(8,128)(2,1)S(1)}, u32[]{:S(2)}, u32[]{:S(2)}) collective-permute-start(bf16[64,1024]{1,0:T(8,128)(2,1)} %param.23), channel_id=1, source_target_pairs={{0,24},{8,16},{16,8},{24,0},{1,25},{9,17},{17,9},{25,1},{2,26},{10... | collective-permute-start | bytes 393224 | tf_op jit(solution)/shard_map/ppermute | solution.py:581
  24.5 38.5 %collective-permute-start.7 = (bf16[64,1024]{1,0:T(8,128)(2,1)}, bf16[64,1024]{1,0:T(8,128)(2,1)S(1)}, u32[]{:S(2)}, u32[]{:S(2)}) collective-permute-start(bf16[64,1024]{1,0:T(8,128)(2,1)} %param.23), channel_id=1, source_target_pairs={{0,16},{8,24},{16,0},{24,8},{1,17},{9,25},{17,1},{25,9},{2,18},{10... | collective-permute-start | bytes 393224 | tf_op jit(solution)/shard_map/ppermute | solution.py:581
  24.9 40.6 %collective-permute-start.8 = (bf16[64,1024]{1,0:T(8,128)(2,1)S(1)}, bf16[64,1024]{1,0:T(8,128)(2,1)S(1)}, u32[]{:S(2)}, u32[]{:S(2)}) collective-permute-start(bf16[64,1024]{1,0:T(8,128)(2,1)S(1)} %copy-done.71), channel_id=1, source_target_pairs={{0,8},{8,0},{16,24},{24,16},{1,9},{9,1},{17,25},{25,17},{2,10},{10... | collective-permute-start | bytes 393224 | tf_op jit(solution)/shard_map/ppermute | solution.py:581
  43.8 22.2 %collective-permute-start.9 = (bf16[88,1024]{1,0:T(8,128)(2,1)S(1)}, bf16[88,1024]{1,0:T(8,128)(2,1)S(1)}, u32[]{:S(2)}, u32[]{:S(2)}) collective-permute-start(bf16[88,1024]{1,0:T(8,128)(2,1)S(1)} %copy-done.34), channel_id=1, source_target_pairs={{0,24},{8,16},{16,8},{24,0},{1,25},{9,17},{17,9},{25,1},{2,26},{10... | collective-permute-start | bytes 540680 | tf_op jit(solution)/shard_map/ppermute | solution.py:581
  46.7 28.7 %collective-permute-start.10 = (bf16[88,1024]{1,0:T(8,128)(2,1)S(1)}, bf16[88,1024]{1,0:T(8,128)(2,1)S(1)}, u32[]{:S(2)}, u32[]{:S(2)}) collective-permute-start(bf16[88,1024]{1,0:T(8,128)(2,1)S(1)} %copy-done.34), channel_id=1, source_target_pairs={{0,16},{8,24},{16,0},{24,8},{1,17},{9,25},{17,1},{25,9},{2,18},{10... | collective-permute-start | bytes 540680 | tf_op jit(solution)/shard_map/ppermute | solution.py:581
  46.9 28.6 %collective-permute-start.11 = (bf16[88,1024]{1,0:T(8,128)(2,1)S(1)}, bf16[88,1024]{1,0:T(8,128)(2,1)S(1)}, u32[]{:S(2)}, u32[]{:S(2)}) collective-permute-start(bf16[88,1024]{1,0:T(8,128)(2,1)S(1)} %copy-done.34), channel_id=1, source_target_pairs={{0,8},{8,0},{16,24},{24,16},{1,9},{9,1},{17,25},{25,17},{2,10},{10... | collective-permute-start | bytes 540680 | tf_op jit(solution)/shard_map/ppermute | solution.py:581
  63.0 14.4 %collective-permute-start.3 = (bf16[4,32,2048]{2,1,0:T(8,128)(2,1)S(1)}, bf16[4,32,2048]{2,1,0:T(8,128)(2,1)S(1)}, u32[]{:S(2)}, u32[]{:S(2)}) collective-permute-start(bf16[4,32,2048]{2,1,0:T(8,128)(2,1)S(1)} %pad_maximum_fusion.16), channel_id=1, source_target_pairs={{0,3},{1,2},{2,1},{3,0},{4,7},{5,6},{6,5},{7,4},{8,11},{9,10},{10,... | collective-permute-start | bytes 1572872 | tf_op jit(solution)/shard_map/ppermute | solution.py:581
  65.5 22.6 %collective-permute-start.4 = (bf16[4,32,2048]{2,1,0:T(8,128)(2,1)S(1)}, bf16[4,32,2048]{2,1,0:T(8,128)(2,1)S(1)}, u32[]{:S(2)}, u32[]{:S(2)}) collective-permute-start(bf16[4,32,2048]{2,1,0:T(8,128)(2,1)S(1)} %pad_maximum_fusion.16), channel_id=1, source_target_pairs={{0,2},{1,3},{2,0},{3,1},{4,6},{5,7},{6,4},{7,5},{8,10},{9,11},{10,... | collective-permute-start | bytes 1572872 | tf_op jit(solution)/shard_map/ppermute | solution.py:581
  66.0 23.3 %collective-permute-start.5 = (bf16[4,32,2048]{2,1,0:T(8,128)(2,1)S(1)}, bf16[4,32,2048]{2,1,0:T(8,128)(2,1)S(1)}, u32[]{:S(2)}, u32[]{:S(2)}) collective-permute-start(bf16[4,32,2048]{2,1,0:T(8,128)(2,1)S(1)} %pad_maximum_fusion.16), channel_id=1, source_target_pairs={{0,1},{1,0},{2,3},{3,2},{4,5},{5,4},{6,7},{7,6},{8,9},{9,8},{10,11... | collective-permute-start | bytes 1572872 | tf_op jit(solution)/shard_map/ppermute | solution.py:581
  111.5 78.0 %collective-permute-start.13 = (bf16[4,64,1024]{2,1,0:T(8,128)(2,1)}, bf16[4,64,1024]{2,1,0:T(8,128)(2,1)}, u32[]{:S(2)}, u32[]{:S(2)}) collective-permute-start(bf16[4,64,1024]{2,1,0:T(8,128)(2,1)} %pad_maximum_fusion.17), channel_id=1, source_target_pairs={{0,3},{1,2},{2,1},{3,0},{4,7},{5,6},{6,5},{7,4},{8,11},{9,10},{10,... | collective-permute-start | bytes 1572872 | tf_op jit(solution)/shard_map/ppermute | solution.py:581
  113.2 77.1 %collective-permute-start.14 = (bf16[4,64,1024]{2,1,0:T(8,128)(2,1)}, bf16[4,64,1024]{2,1,0:T(8,128)(2,1)}, u32[]{:S(2)}, u32[]{:S(2)}) collective-permute-start(bf16[4,64,1024]{2,1,0:T(8,128)(2,1)} %pad_maximum_fusion.17), channel_id=1, source_target_pairs={{0,2},{1,3},{2,0},{3,1},{4,6},{5,7},{6,4},{7,5},{8,10},{9,11},{10,... | collective-permute-start | bytes 1572872 | tf_op jit(solution)/shard_map/ppermute | solution.py:581
  114.3 77.1 %collective-permute-start.15 = (bf16[4,64,1024]{2,1,0:T(8,128)(2,1)}, bf16[4,64,1024]{2,1,0:T(8,128)(2,1)}, u32[]{:S(2)}, u32[]{:S(2)}) collective-permute-start(bf16[4,64,1024]{2,1,0:T(8,128)(2,1)} %pad_maximum_fusion.17), channel_id=1, source_target_pairs={{0,1},{1,0},{2,3},{3,2},{4,5},{5,4},{6,7},{7,6},{8,9},{9,8},{10,11... | collective-permute-start | bytes 1572872 | tf_op jit(solution)/shard_map/ppermute | solution.py:581
  127.9 11.6 %collective-permute-start.12 = (bf16[1,3,4096]{2,1,0:T(4,128)(2,1)S(1)}, bf16[1,3,4096]{2,1,0:T(4,128)(2,1)S(1)}, u32[]{:S(2)}, u32[]{:S(2)}) collective-permute-start(bf16[1,3,4096]{2,1,0:T(4,128)(2,1)S(1)} %slice.219), channel_id=1, source_target_pairs={{0,1},{1,2},{2,3},{4,5},{5,6},{6,7},{8,9},{9,10},{10,11},{12,13},{... | collective-permute-start | bytes 73736 | tf_op jit(solution)/shard_map/ppermute | solution.py:482
  135.3 58.2 %collective-permute-start.16 = (bf16[4,4,32,2048]{3,2,1,0:T(8,128)(2,1)}, bf16[4,4,32,2048]{3,2,1,0:T(8,128)(2,1)}, u32[]{:S(2)}, u32[]{:S(2)}) collective-permute-start(bf16[4,4,32,2048]{3,2,1,0:T(8,128)(2,1)} %pad_maximum_fusion.9), channel_id=1, source_target_pairs={{0,4},{4,0},{1,5},{5,1},{2,6},{6,2},{3,7},{7,3},{8,12},{12,8},{9,1... | collective-permute-start | bytes 6291464 | tf_op jit(solution)/shard_map/ppermute | solution.py:581
  139.6 64.4 %collective-permute-start.21 = (bf16[4,88,1024]{2,1,0:T(8,128)(2,1)}, bf16[4,88,1024]{2,1,0:T(8,128)(2,1)S(1)}, u32[]{:S(2)}, u32[]{:S(2)}) collective-permute-start(bf16[4,88,1024]{2,1,0:T(8,128)(2,1)} %pad_maximum_fusion.12), channel_id=1, source_target_pairs={{0,3},{1,2},{2,1},{3,0},{4,7},{5,6},{6,5},{7,4},{8,11},{9,10},{10,... | collective-permute-start | bytes 2162696 | tf_op jit(solution)/shard_map/ppermute | solution.py:581
  189.6 28.3 %collective-permute-start.22 = (bf16[4,88,1024]{2,1,0:T(8,128)(2,1)S(1)}, bf16[4,88,1024]{2,1,0:T(8,128)(2,1)S(1)}, u32[]{:S(2)}, u32[]{:S(2)}) collective-permute-start(bf16[4,88,1024]{2,1,0:T(8,128)(2,1)S(1)} %copy-done.15), channel_id=1, source_target_pairs={{0,2},{1,3},{2,0},{3,1},{4,6},{5,7},{6,4},{7,5},{8,10},{9,11},{10,... | collective-permute-start | bytes 2162696 | tf_op jit(solution)/shard_map/ppermute | solution.py:581
  190.3 28.3 %collective-permute-start.23 = (bf16[4,88,1024]{2,1,0:T(8,128)(2,1)S(1)}, bf16[4,88,1024]{2,1,0:T(8,128)(2,1)S(1)}, u32[]{:S(2)}, u32[]{:S(2)}) collective-permute-start(bf16[4,88,1024]{2,1,0:T(8,128)(2,1)S(1)} %copy-done.15), channel_id=1, source_target_pairs={{0,1},{1,0},{2,3},{3,2},{4,5},{5,4},{6,7},{7,6},{8,9},{9,8},{10,11... | collective-permute-start | bytes 2162696 | tf_op jit(solution)/shard_map/ppermute | solution.py:581
  193.4 44.8 %collective-permute-start.20 = (bf16[4,4,64,1024]{3,2,1,0:T(8,128)(2,1)S(1)}, bf16[4,4,64,1024]{3,2,1,0:T(8,128)(2,1)S(1)}, u32[]{:S(2)}, u32[]{:S(2)}) collective-permute-start(bf16[4,4,64,1024]{3,2,1,0:T(8,128)(2,1)S(1)} %pad_maximum_fusion.10), channel_id=1, source_target_pairs={{0,4},{4,0},{1,5},{5,1},{2,6},{6,2},{3,7},{7,3},{8,12},{12,8},{9,1... | collective-permute-start | bytes 6291464 | tf_op jit(solution)/shard_map/ppermute | solution.py:581
  200.0 27.0 %collective-permute-start.17 = (bf16[1,8,128,256]{3,2,1,0:T(8,128)(2,1)S(1)}, bf16[1,8,128,256]{3,2,1,0:T(8,128)(2,1)S(1)}, u32[]{:S(2)}, u32[]{:S(2)}) collective-permute-start(bf16[1,8,128,256]{3,2,1,0:T(8,128)(2,1)S(1)} %fusion.47), channel_id=1, source_target_pairs={{0,1},{4,5},{8,9},{12,13},{16,17},{20,21},{24,25},{28,29}} | collective-permute-start | bytes 1572872 | tf_op jit(solution)/shard_map/ppermute | solution.py:676
  203.9 19.6 %collective-permute-start.24 = (bf16[1,8,128,128]{3,2,1,0:T(8,128)(2,1)S(1)}, bf16[1,8,128,128]{3,2,1,0:T(8,128)(2,1)S(1)}, u32[]{:S(2)}, u32[]{:S(2)}) collective-permute-start(bf16[1,8,128,128]{3,2,1,0:T(8,128)(2,1)S(1)} %fusion.106), channel_id=1, source_target_pairs={{1,0},{2,1},{3,2},{5,4},{6,5},{7,6},{9,8},{10,9},{11,10},{13,12},{... | collective-permute-start | bytes 786440 | tf_op jit(solution)/shard_map/ppermute | solution.py:482
  241.8 27.7 %collective-permute-start.26 = (bf16[4,4,88,1024]{3,2,1,0:T(8,128)(2,1)}, bf16[4,4,88,1024]{3,2,1,0:T(8,128)(2,1)}, u32[]{:S(2)}, u32[]{:S(2)}) collective-permute-start(bf16[4,4,88,1024]{3,2,1,0:T(8,128)(2,1)} %pad_maximum_fusion.6), channel_id=1, source_target_pairs={{0,4},{4,0},{1,5},{5,1},{2,6},{6,2},{3,7},{7,3},{8,12},{12,8},{9,1... | collective-permute-start | bytes 8650760 | tf_op jit(solution)/shard_map/ppermute | solution.py:581
  289.3 19.0 %collective-permute-start.27 = (bf16[4,4,32,5632]{3,2,1,0:T(8,128)(2,1)}, bf16[4,4,32,5632]{3,2,1,0:T(8,128)(2,1)S(1)}, u32[]{:S(2)}, u32[]{:S(2)}) collective-permute-start(bf16[4,4,32,5632]{3,2,1,0:T(8,128)(2,1)} %bitcast.469), channel_id=1, source_target_pairs={{0,4},{4,0},{1,5},{5,1},{2,6},{6,2},{3,7},{7,3},{8,12},{12,8},{9,1... | collective-permute-start | bytes 17301512 | tf_op jit(solution)/shard_map/ppermute | solution.py:524
  315.1 355.3 %reduce-scatter.5.cloned.1.call-start = ((), (), s32[]{:S(2)}) async-start(), calls=%async_computation.5 | async-start | bytes 1802240 | tf_op jit(solution)/shard_map/reduce_scatter | solution.py:543
  324.1 97.7 %collective-permute-start.31 = (bf16[4,4,88,1024]{3,2,0,1:T(8,128)(2,1)}, bf16[4,4,88,1024]{3,2,0,1:T(8,128)(2,1)}, u32[]{:S(2)}, u32[]{:S(2)}) collective-permute-start(bf16[4,4,88,1024]{3,2,0,1:T(8,128)(2,1)} %bitcast.420), channel_id=1, source_target_pairs={{0,4},{4,0},{1,5},{5,1},{2,6},{6,2},{3,7},{7,3},{8,12},{12,8},{9,1... | collective-permute-start | bytes 8650760 | tf_op jit(solution)/shard_map/ppermute | solution.py:509
  349.8 79.9 %collective-permute-start.32 = (bf16[4,4,32,2048]{3,2,0,1:T(8,128)(2,1)}, bf16[4,4,32,2048]{3,2,0,1:T(8,128)(2,1)}, u32[]{:S(2)}, u32[]{:S(2)}) collective-permute-start(bf16[4,4,32,2048]{3,2,0,1:T(8,128)(2,1)} %copy.221), channel_id=1, source_target_pairs={{0,4},{4,0},{1,5},{5,1},{2,6},{6,2},{3,7},{7,3},{8,12},{12,8},{9,1... | collective-permute-start | bytes 6291464 | tf_op jit(solution)/shard_map/ppermute | solution.py:524
  352.5 77.3 %collective-permute-start.33 = (bf16[4,4,64,1024]{3,2,0,1:T(8,128)(2,1)}, bf16[4,4,64,1024]{3,2,0,1:T(8,128)(2,1)}, u32[]{:S(2)}, u32[]{:S(2)}) collective-permute-start(bf16[4,4,64,1024]{3,2,0,1:T(8,128)(2,1)} %bitcast.422), channel_id=1, source_target_pairs={{0,4},{4,0},{1,5},{5,1},{2,6},{6,2},{3,7},{7,3},{8,12},{12,8},{9,1... | collective-permute-start | bytes 6291464 | tf_op jit(solution)/shard_map/ppermute | solution.py:509
  360.7 32.7 %collective-permute-start.29 = (bf16[1,8,128,256]{3,2,1,0:T(8,128)(2,1)}, bf16[1,8,128,256]{3,2,1,0:T(8,128)(2,1)}, u32[]{:S(2)}, u32[]{:S(2)}) collective-permute-start(bf16[1,8,128,256]{3,2,1,0:T(8,128)(2,1)} %convert_element_type.919), channel_id=1, source_target_pairs={{2,0},{3,1},{6,4},{7,5},{10,8},{11,9},{14,12},{15,13},{18,16},{19,... | collective-permute-start | bytes 1572872 | tf_op jit(solution)/shard_map/ppermute | solution.py:482
  362.0 35.6 %collective-permute-start.28 = (bf16[1,8,128,256]{3,2,1,0:T(8,128)(2,1)}, bf16[1,8,128,256]{3,2,1,0:T(8,128)(2,1)}, u32[]{:S(2)}, u32[]{:S(2)}) collective-permute-start(bf16[1,8,128,256]{3,2,1,0:T(8,128)(2,1)} %convert_element_type.919), channel_id=1, source_target_pairs={{1,0},{2,1},{3,2},{5,4},{6,5},{7,6},{9,8},{10,9},{11,10},{13,12},{... | collective-permute-start | bytes 1572872 | tf_op jit(solution)/shard_map/ppermute | solution.py:482
  393.3 26.3 %collective-permute-start.30 = (bf16[1,8,128,256]{3,2,1,0:T(8,128)(2,1)}, bf16[1,8,128,256]{3,2,1,0:T(8,128)(2,1)S(1)}, u32[]{:S(2)}, u32[]{:S(2)}) collective-permute-start(bf16[1,8,128,256]{3,2,1,0:T(8,128)(2,1)} %convert_element_type.919), channel_id=1, source_target_pairs={{3,0},{7,4},{11,8},{15,12},{19,16},{23,20},{27,24},{31,28}} | collective-permute-start | bytes 1572872 | tf_op jit(solution)/shard_map/ppermute | solution.py:482
  426.2 19.4 %collective-permute-start.34 = (bf16[4,88,1024]{2,1,0:T(8,128)(2,1)}, bf16[4,88,1024]{2,1,0:T(8,128)(2,1)}, u32[]{:S(2)}, u32[]{:S(2)}) collective-permute-start(bf16[4,88,1024]{2,1,0:T(8,128)(2,1)} %get-tuple-element.317), channel_id=1, source_target_pairs={{0,1},{1,0},{2,3},{3,2},{4,5},{5,4},{6,7},{7,6},{8,9},{9,8},{10,11... | collective-permute-start | bytes 2162696 | tf_op jit(solution)/shard_map/ppermute | solution.py:534
  426.2 81.9 %collective-permute-start.35 = (bf16[4,88,1024]{2,1,0:T(8,128)(2,1)}, bf16[4,88,1024]{2,1,0:T(8,128)(2,1)}, u32[]{:S(2)}, u32[]{:S(2)}) collective-permute-start(bf16[4,88,1024]{2,1,0:T(8,128)(2,1)} %get-tuple-element.316), channel_id=1, source_target_pairs={{0,2},{1,3},{2,0},{3,1},{4,6},{5,7},{6,4},{7,5},{8,10},{9,11},{10,... | collective-permute-start | bytes 2162696 | tf_op jit(solution)/shard_map/ppermute | solution.py:534
  426.5 81.7 %collective-permute-start.36 = (bf16[4,88,1024]{2,1,0:T(8,128)(2,1)}, bf16[4,88,1024]{2,1,0:T(8,128)(2,1)}, u32[]{:S(2)}, u32[]{:S(2)}) collective-permute-start(bf16[4,88,1024]{2,1,0:T(8,128)(2,1)} %get-tuple-element.315), channel_id=1, source_target_pairs={{0,3},{1,2},{2,1},{3,0},{4,7},{5,6},{6,5},{7,4},{8,11},{9,10},{10,... | collective-permute-start | bytes 2162696 | tf_op jit(solution)/shard_map/ppermute | solution.py:534
  433.3 78.4 %collective-permute-start.37 = (bf16[4,32,2048]{2,1,0:T(8,128)(2,1)}, bf16[4,32,2048]{2,1,0:T(8,128)(2,1)}, u32[]{:S(2)}, u32[]{:S(2)}) collective-permute-start(bf16[4,32,2048]{2,1,0:T(8,128)(2,1)} %get-tuple-element.337), channel_id=1, source_target_pairs={{0,1},{1,0},{2,3},{3,2},{4,5},{5,4},{6,7},{7,6},{8,9},{9,8},{10,11... | collective-permute-start | bytes 1572872 | tf_op jit(solution)/shard_map/ppermute | solution.py:534
  433.4 78.3 %collective-permute-start.38 = (bf16[4,32,2048]{2,1,0:T(8,128)(2,1)}, bf16[4,32,2048]{2,1,0:T(8,128)(2,1)}, u32[]{:S(2)}, u32[]{:S(2)}) collective-permute-start(bf16[4,32,2048]{2,1,0:T(8,128)(2,1)} %get-tuple-element.336), channel_id=1, source_target_pairs={{0,2},{1,3},{2,0},{3,1},{4,6},{5,7},{6,4},{7,5},{8,10},{9,11},{10,... | collective-permute-start | bytes 1572872 | tf_op jit(solution)/shard_map/ppermute | solution.py:534
  445.6 66.1 %collective-permute-start.39 = (bf16[4,32,2048]{2,1,0:T(8,128)(2,1)}, bf16[4,32,2048]{2,1,0:T(8,128)(2,1)S(1)}, u32[]{:S(2)}, u32[]{:S(2)}) collective-permute-start(bf16[4,32,2048]{2,1,0:T(8,128)(2,1)} %get-tuple-element.335), channel_id=1, source_target_pairs={{0,3},{1,2},{2,1},{3,0},{4,7},{5,6},{6,5},{7,4},{8,11},{9,10},{10,... | collective-permute-start | bytes 1572872 | tf_op jit(solution)/shard_map/ppermute | solution.py:534
  508.1 32.8 %collective-permute-start.40 = (bf16[4,64,1024]{2,1,0:T(8,128)(2,1)}, bf16[4,64,1024]{2,1,0:T(8,128)(2,1)}, u32[]{:S(2)}, u32[]{:S(2)}) collective-permute-start(bf16[4,64,1024]{2,1,0:T(8,128)(2,1)} %get-tuple-element.333), channel_id=1, source_target_pairs={{0,1},{1,0},{2,3},{3,2},{4,5},{5,4},{6,7},{7,6},{8,9},{9,8},{10,11... | collective-permute-start | bytes 1572872 | tf_op jit(solution)/shard_map/ppermute | solution.py:534
  508.2 35.1 %collective-permute-start.41 = (bf16[4,64,1024]{2,1,0:T(8,128)(2,1)}, bf16[4,64,1024]{2,1,0:T(8,128)(2,1)}, u32[]{:S(2)}, u32[]{:S(2)}) collective-permute-start(bf16[4,64,1024]{2,1,0:T(8,128)(2,1)} %get-tuple-element.332), channel_id=1, source_target_pairs={{0,2},{1,3},{2,0},{3,1},{4,6},{5,7},{6,4},{7,5},{8,10},{9,11},{10,... | collective-permute-start | bytes 1572872 | tf_op jit(solution)/shard_map/ppermute | solution.py:534
  511.7 31.8 %collective-permute-start.42 = (bf16[4,64,1024]{2,1,0:T(8,128)(2,1)}, bf16[4,64,1024]{2,1,0:T(8,128)(2,1)}, u32[]{:S(2)}, u32[]{:S(2)}) collective-permute-start(bf16[4,64,1024]{2,1,0:T(8,128)(2,1)} %get-tuple-element.331), channel_id=1, source_target_pairs={{0,3},{1,2},{2,1},{3,0},{4,7},{5,6},{6,5},{7,4},{8,11},{9,10},{10,... | collective-permute-start | bytes 1572872 | tf_op jit(solution)/shard_map/ppermute | solution.py:534
  514.7 36.9 %collective-permute-start.43 = (bf16[1,3,4096]{2,1,0:T(4,128)(2,1)S(1)}, bf16[1,3,4096]{2,1,0:T(4,128)(2,1)S(1)}, u32[]{:S(2)}, u32[]{:S(2)}) collective-permute-start(bf16[1,3,4096]{2,1,0:T(4,128)(2,1)S(1)} %slice.243), channel_id=1, source_target_pairs={{1,0},{2,1},{3,2},{5,4},{6,5},{7,6},{9,8},{10,9},{11,10},{13,12},{... | collective-permute-start | bytes 73736 | tf_op jit(solution)/shard_map/ppermute | solution.py:482
  519.1 11.5 %collective-permute-start.75 = (f32[8,128]{1,0:T(8,128)}, f32[8,128]{1,0:T(8,128)S(1)}, u32[]{:S(2)}, u32[]{:S(2)}) collective-permute-start(f32[8,128]{1,0:T(8,128)} %fusion.189), channel_id=1, source_target_pairs={{0,1},{1,0},{2,3},{3,2},{4,5},{5,4},{6,7},{7,6},{8,9},{9,8},{10,11... | collective-permute-start | bytes 12296 | tf_op jit(solution)/shard_map/ppermute | solution.py:568
  540.9 21.8 %collective-permute-start.67 = (bf16[32,2048]{1,0:T(8,128)(2,1)}, bf16[32,2048]{1,0:T(8,128)(2,1)S(1)}, u32[]{:S(2)}, u32[]{:S(2)}) collective-permute-start(bf16[32,2048]{1,0:T(8,128)(2,1)} %get-tuple-element.359), channel_id=1, source_target_pairs={{0,24},{8,16},{16,8},{24,0},{1,25},{9,17},{17,9},{25,1},{2,26},{10... | collective-permute-start | bytes 393224 | tf_op jit(solution)/shard_map/ppermute | solution.py:534
  543.3 22.0 %collective-permute-start.66 = (bf16[32,2048]{1,0:T(8,128)(2,1)}, bf16[32,2048]{1,0:T(8,128)(2,1)S(1)}, u32[]{:S(2)}, u32[]{:S(2)}) collective-permute-start(bf16[32,2048]{1,0:T(8,128)(2,1)} %get-tuple-element.360), channel_id=1, source_target_pairs={{0,16},{8,24},{16,0},{24,8},{1,17},{9,25},{17,1},{25,9},{2,18},{10... | collective-permute-start | bytes 393224 | tf_op jit(solution)/shard_map/ppermute | solution.py:534
  543.5 22.0 %collective-permute-start.65 = (bf16[32,2048]{1,0:T(8,128)(2,1)}, bf16[32,2048]{1,0:T(8,128)(2,1)S(1)}, u32[]{:S(2)}, u32[]{:S(2)}) collective-permute-start(bf16[32,2048]{1,0:T(8,128)(2,1)} %get-tuple-element.358), channel_id=1, source_target_pairs={{0,8},{8,0},{16,24},{24,16},{1,9},{9,1},{17,25},{25,17},{2,10},{10... | collective-permute-start | bytes 393224 | tf_op jit(solution)/shard_map/ppermute | solution.py:534
  556.6 38.1 %collective-permute-start.44 = (bf16[4,4,32,2048]{3,2,1,0:T(8,128)(2,1)S(1)}, bf16[4,4,32,2048]{3,2,1,0:T(8,128)(2,1)S(1)}, u32[]{:S(2)}, u32[]{:S(2)}) collective-permute-start(bf16[4,4,32,2048]{3,2,1,0:T(8,128)(2,1)S(1)} %bitcast.470), channel_id=1, source_target_pairs={{0,4},{4,0},{1,5},{5,1},{2,6},{6,2},{3,7},{7,3},{8,12},{12,8},{9,1... | collective-permute-start | bytes 6291464 | tf_op jit(solution)/shard_map/ppermute | solution.py:524
  556.9 40.4 %collective-permute-start.45 = (bf16[4,4,32,2176]{3,2,1,0:T(8,128)(2,1)S(1)}, bf16[4,4,32,2176]{3,2,1,0:T(8,128)(2,1)S(1)}, u32[]{:S(2)}, u32[]{:S(2)}) collective-permute-start(bf16[4,4,32,2176]{3,2,1,0:T(8,128)(2,1)S(1)} %pad_maximum_fusion.8), channel_id=1, source_target_pairs={{0,4},{4,0},{1,5},{5,1},{2,6},{6,2},{3,7},{7,3},{8,12},{12,8},{9,1... | collective-permute-start | bytes 6684680 | tf_op jit(solution)/shard_map/ppermute | solution.py:524
  565.3 18.4 %collective-permute-start.69 = (bf16[64,1024]{1,0:T(8,128)(2,1)S(1)}, bf16[64,1024]{1,0:T(8,128)(2,1)S(1)}, u32[]{:S(2)}, u32[]{:S(2)}) collective-permute-start(bf16[64,1024]{1,0:T(8,128)(2,1)S(1)} %get-tuple-element.357), channel_id=1, source_target_pairs={{0,16},{8,24},{16,0},{24,8},{1,17},{9,25},{17,1},{25,9},{2,18},{10... | collective-permute-start | bytes 393224 | tf_op jit(solution)/shard_map/ppermute | solution.py:534
  565.4 18.2 %collective-permute-start.68 = (bf16[64,1024]{1,0:T(8,128)(2,1)S(1)}, bf16[64,1024]{1,0:T(8,128)(2,1)S(1)}, u32[]{:S(2)}, u32[]{:S(2)}) collective-permute-start(bf16[64,1024]{1,0:T(8,128)(2,1)S(1)} %get-tuple-element.355), channel_id=1, source_target_pairs={{0,8},{8,0},{16,24},{24,16},{1,9},{9,1},{17,25},{25,17},{2,10},{10... | collective-permute-start | bytes 393224 | tf_op jit(solution)/shard_map/ppermute | solution.py:534
  570.9 14.7 %collective-permute-start.73 = (bf16[88,1024]{1,0:T(8,128)(2,1)S(1)}, bf16[88,1024]{1,0:T(8,128)(2,1)S(1)}, u32[]{:S(2)}, u32[]{:S(2)}) collective-permute-start(bf16[88,1024]{1,0:T(8,128)(2,1)S(1)} %copy-done.37), channel_id=1, source_target_pairs={{0,24},{8,16},{16,8},{24,0},{1,25},{9,17},{17,9},{25,1},{2,26},{10... | collective-permute-start | bytes 540680 | tf_op jit(solution)/shard_map/ppermute | solution.py:534
  596.9 37.0 %collective-permute-start.53 = (bf16[4,32,2048]{2,1,0:T(8,128)(2,1)}, bf16[4,32,2048]{2,1,0:T(8,128)(2,1)}, u32[]{:S(2)}, u32[]{:S(2)}) collective-permute-start(bf16[4,32,2048]{2,1,0:T(8,128)(2,1)} %get-tuple-element.329), channel_id=1, source_target_pairs={{0,8},{8,0},{16,24},{24,16},{1,9},{9,1},{17,25},{25,17},{2,10},{10... | collective-permute-start | bytes 1572872 | tf_op jit(solution)/shard_map/ppermute | solution.py:534
  599.1 15.9 %collective-permute-start.47 = (bf16[4,32,2176]{2,1,0:T(8,128)(2,1)}, bf16[4,32,2176]{2,1,0:T(8,128)(2,1)}, u32[]{:S(2)}, u32[]{:S(2)}) collective-permute-start(bf16[4,32,2176]{2,1,0:T(8,128)(2,1)} %get-tuple-element.325), channel_id=1, source_target_pairs={{0,1},{1,0},{2,3},{3,2},{4,5},{5,4},{6,7},{7,6},{8,9},{9,8},{10,11... | collective-permute-start | bytes 1671176 | tf_op jit(solution)/shard_map/ppermute | solution.py:534
  604.6 27.2 %collective-permute-start.48 = (bf16[4,32,2176]{2,1,0:T(8,128)(2,1)}, bf16[4,32,2176]{2,1,0:T(8,128)(2,1)S(1)}, u32[]{:S(2)}, u32[]{:S(2)}) collective-permute-start(bf16[4,32,2176]{2,1,0:T(8,128)(2,1)} %get-tuple-element.324), channel_id=1, source_target_pairs={{0,2},{1,3},{2,0},{3,1},{4,6},{5,7},{6,4},{7,5},{8,10},{9,11},{10,... | collective-permute-start | bytes 1671176 | tf_op jit(solution)/shard_map/ppermute | solution.py:534
  605.8 26.1 %collective-permute-start.49 = (bf16[4,32,2176]{2,1,0:T(8,128)(2,1)}, bf16[4,32,2176]{2,1,0:T(8,128)(2,1)S(1)}, u32[]{:S(2)}, u32[]{:S(2)}) collective-permute-start(bf16[4,32,2176]{2,1,0:T(8,128)(2,1)} %get-tuple-element.323), channel_id=1, source_target_pairs={{0,3},{1,2},{2,1},{3,0},{4,7},{5,6},{6,5},{7,4},{8,11},{9,10},{10,... | collective-permute-start | bytes 1671176 | tf_op jit(solution)/shard_map/ppermute | solution.py:534
  606.8 38.4 %collective-permute-start.54 = (bf16[4,32,2048]{2,1,0:T(8,128)(2,1)}, bf16[4,32,2048]{2,1,0:T(8,128)(2,1)S(1)}, u32[]{:S(2)}, u32[]{:S(2)}) collective-permute-start(bf16[4,32,2048]{2,1,0:T(8,128)(2,1)} %get-tuple-element.328), channel_id=1, source_target_pairs={{0,16},{8,24},{16,0},{24,8},{1,17},{9,25},{17,1},{25,9},{2,18},{10... | collective-permute-start | bytes 1572872 | tf_op jit(solution)/shard_map/ppermute | solution.py:534
  614.9 31.6 %collective-permute-start.55 = (bf16[4,32,2048]{2,1,0:T(8,128)(2,1)}, bf16[4,32,2048]{2,1,0:T(8,128)(2,1)S(1)}, u32[]{:S(2)}, u32[]{:S(2)}) collective-permute-start(bf16[4,32,2048]{2,1,0:T(8,128)(2,1)} %get-tuple-element.327), channel_id=1, source_target_pairs={{0,24},{8,16},{16,8},{24,0},{1,25},{9,17},{17,9},{25,1},{2,26},{10... | collective-permute-start | bytes 1572872 | tf_op jit(solution)/shard_map/ppermute | solution.py:534
  631.9 28.0 %collective-permute-start.50 = (f32[4,1,32]{2,0,1:T(4,128)S(1)}, f32[4,1,32]{2,0,1:T(4,128)S(1)}, u32[]{:S(2)}, u32[]{:S(2)}) collective-permute-start(f32[4,1,32]{2,0,1:T(4,128)S(1)} %bitcast.463), channel_id=1, source_target_pairs={{0,1},{1,0},{2,3},{3,2},{4,5},{5,4},{6,7},{7,6},{8,9},{9,8},{10,11... | collective-permute-start | bytes 1544 | tf_op jit(solution)/shard_map/ppermute | solution.py:534
  632.5 27.4 %collective-permute-start.51 = (f32[4,1,32]{2,0,1:T(4,128)S(1)}, f32[4,1,32]{2,0,1:T(4,128)S(1)}, u32[]{:S(2)}, u32[]{:S(2)}) collective-permute-start(f32[4,1,32]{2,0,1:T(4,128)S(1)} %bitcast.462), channel_id=1, source_target_pairs={{0,2},{1,3},{2,0},{3,1},{4,6},{5,7},{6,4},{7,5},{8,10},{9,11},{10,... | collective-permute-start | bytes 1544 | tf_op jit(solution)/shard_map/ppermute | solution.py:534
  633.9 26.0 %collective-permute-start.52 = (f32[4,1,32]{2,0,1:T(4,128)S(1)}, f32[4,1,32]{2,0,1:T(4,128)S(1)}, u32[]{:S(2)}, u32[]{:S(2)}) collective-permute-start(f32[4,1,32]{2,0,1:T(4,128)S(1)} %bitcast.461), channel_id=1, source_target_pairs={{0,3},{1,2},{2,1},{3,0},{4,7},{5,6},{6,5},{7,4},{8,11},{9,10},{10,... | collective-permute-start | bytes 1544 | tf_op jit(solution)/shard_map/ppermute | solution.py:534
  645.2 30.9 %collective-permute-start.64 = (bf16[32,2176]{1,0:T(8,128)(2,1)S(1)}, bf16[32,2176]{1,0:T(8,128)(2,1)S(1)}, u32[]{:S(2)}, u32[]{:S(2)}) collective-permute-start(bf16[32,2176]{1,0:T(8,128)(2,1)S(1)} %get-tuple-element.353), channel_id=1, source_target_pairs={{0,24},{8,16},{16,8},{24,0},{1,25},{9,17},{17,9},{25,1},{2,26},{10... | collective-permute-start | bytes 417800 | tf_op jit(solution)/shard_map/ppermute | solution.py:534
  646.6 29.5 %collective-permute-start.63 = (bf16[32,2176]{1,0:T(8,128)(2,1)S(1)}, bf16[32,2176]{1,0:T(8,128)(2,1)S(1)}, u32[]{:S(2)}, u32[]{:S(2)}) collective-permute-start(bf16[32,2176]{1,0:T(8,128)(2,1)S(1)} %get-tuple-element.354), channel_id=1, source_target_pairs={{0,16},{8,24},{16,0},{24,8},{1,17},{9,25},{17,1},{25,9},{2,18},{10... | collective-permute-start | bytes 417800 | tf_op jit(solution)/shard_map/ppermute | solution.py:534
  (123 other events, 2178.1 us)
Sparse Core Ops, SparseCore 0:
  13.2 98.2 all-gather.2
  114.9 116.6 all-gather.4
  315.2 121.4 reduce-scatter.2
  523.3 31.3 reduce-scatter.4
